TPU v7x, 32 devices: a whole 2x2x4 slice. The times are simulated.
32 devices in a mesh: groups: 2 (over x), ex: 16 (over z, y, core).
Axes of the slice: x: 2, y: 2, z: 4, core: 2. Of those that a mesh axis runs over, the one named last changes fastest.
Arguments:
- acts: bfloat16 [24576, 5120], P(('groups', 'ex')), parts along dimension 0, may hold values from -6 to 6
- grads: bfloat16 [24576, 1024], P(('groups', 'ex')), parts along dimension 0, may hold values from -6 to 6
- domain: int32 [3072], P(('groups', 'ex')), parts along dimension 0, may hold values from 0 to 47
- listed: int32 [32, 2], P(('groups', 'ex')), parts along dimension 0, may hold values 0 or 1
Outputs:
- influence: float32 [3072, 48], P(('groups', 'ex')), parts along dimension 0
There are 2 independent parts, one for each index of `groups`. A program takes and returns all parts, laid end to end along the dimension named above; each array names one. Nothing has to cross between parts.
All inputs are finite; a program needn't handle non-finite values. No bound on the sum of `listed` on one device may be relied on, other than what follows from the above.
Results may differ from a plain program's by a relative error of at most 0.0003.
Values may be sent and summed in bfloat16 or wider, within the bound.
No kernel may reach another device: no remote copies, remote signals or barrier semaphores. Data moves between devices by JAX's collectives and lax.ppermute only.
A program may use at most 192 MiB of HBM per device.

v0:
```python
import functools
import math

import jax
import jax.numpy as jnp
from jax import lax
from jax.experimental import pallas as pl
from jax.experimental.pallas import tpu as pltpu
from jax.sharding import PartitionSpec as P

TOK = 8
TOK_BITS = 3
DOMAINS = 48
LANES = 128
VMEM_BYTES = 63 * 1024 * 1024
PAIRS_VMEM_BYTES = 44 * 1024 * 1024

INFO = 16

XS, XC, YS, YC, ZS, ZC = range(6)
PAIRS = (
    (YS, XS, 1), (YS, ZS, 1), (YS, XC, 0), (XC, XS, 0),
    (YC, XC, 1), (YC, ZC, 1), (YC, ZS, 0), (YS, ZC, 0), (YC, XS, 0),
)
ONLY = {2: 0, 6: 0, 7: 1, 8: 1}
SLOT = (0, 1, 2, 3, 4, 5, 6, 6, 2)
SLOTS = 7
FIRST = (0, 1, 2, 3)
SMALL = pl.CostEstimate(flops=1, bytes_accessed=1, transcendentals=0)
NT = (((1,), (1,)), ((), ()))
NN = (((1,), (0,)), ((), ()))


def across(chip):
    return chip ^ 1


def along(chip):
    return chip + 2 if chip & 1 else chip - 2


def against(chip):
    return chip - 2 if chip & 1 else chip + 2


def stay(chip):
    return chip


def send(value, move, flip):
    chips = lax.axis_size("ex") // 2
    pairs = [
        (2 * chip + core, 2 * (move(chip) % chips) + (core ^ flip))
        for chip in range(chips)
        for core in range(2)
    ]
    return lax.ppermute(value, "ex", pairs)


def token_major(rows):
    to = lax.broadcasted_iota(jnp.int32, (rows, rows), 0)
    source = lax.broadcasted_iota(jnp.int32, (rows, rows), 1)
    examples = rows // TOK
    place = (source & (TOK - 1)) * examples + lax.shift_right_logical(source, TOK_BITS)
    return (place == to).astype(jnp.bfloat16)


def reorder(order, block):
    return jnp.dot(order, block, preferred_element_type=jnp.float32).astype(jnp.bfloat16)


def put(target, value, info):
    rows = value.shape[0]
    target[:rows, :] = value
    target[rows:, :] = jnp.concatenate([info[...]] * (target.shape[1] // LANES), axis=1)


def chunks(quarter):
    second = quarter // LANES // 5 * LANES
    return quarter - second, second


def cut_kernel(places, info, y_acts, z_acts, y_one, z_one, y_two, z_two, order):
    rows, split = order.shape[0], y_one.shape[1]
    order[...] = token_major(rows)
    put(y_one, reorder(order[...], y_acts[:, :split]), info)
    put(z_one, z_acts[:, :split], info)
    y_two[...] = reorder(order[...], y_acts[:, split:])
    z_two[...] = z_acts[:, split:]


def cut(acts, info, places):
    rows, width = acts.shape
    quarter = width // 4
    one, two = chunks(quarter)
    shapes = [(rows + INFO, one)] * 2 + [(rows, two)] * 2
    return pl.pallas_call(
        cut_kernel,
        grid_spec=pltpu.PrefetchScalarGridSpec(
            num_scalar_prefetch=1,
            grid=(1,),
            in_specs=[
                pl.BlockSpec((INFO, LANES), lambda i, p: (0, 0)),
                pl.BlockSpec((rows, quarter), lambda i, p: (0, p[0])),
                pl.BlockSpec((rows, quarter), lambda i, p: (0, p[1])),
            ],
            out_specs=[pl.BlockSpec(shape, lambda i, p: (0, 0)) for shape in shapes],
            scratch_shapes=[pltpu.VMEM((rows, rows), jnp.bfloat16)],
        ),
        out_shape=[jax.ShapeDtypeStruct(shape, acts.dtype) for shape in shapes],
        compiler_params=pltpu.CompilerParams(vmem_limit_bytes=VMEM_BYTES),
        cost_estimate=SMALL,
        name="cut",
    )(places, info, acts, acts)


def half_kernel(steps, place, info, acts, grads, out):
    @pl.when(pl.program_id(0) < steps)
    def _():
        put(out, acts[...], info)

    @pl.when(pl.program_id(0) >= steps)
    def _():
        put(out, grads[...], info)


def cut_half(acts, grads, info, place):
    rows, width = acts.shape
    half, depth = width // 2, grads.shape[1]
    step = math.gcd(math.gcd(half, depth), 512)
    steps = half // step
    return pl.pallas_call(
        functools.partial(half_kernel, steps),
        grid_spec=pltpu.PrefetchScalarGridSpec(
            num_scalar_prefetch=1,
            grid=(steps + depth // step,),
            in_specs=[
                pl.BlockSpec((INFO, LANES), lambda i, p: (0, 0)),
                pl.BlockSpec((rows, step), lambda i, p: (0, p[0] * steps + jnp.minimum(i, steps - 1))),
                pl.BlockSpec((rows, step), lambda i, p: (0, jnp.maximum(i - steps, 0))),
            ],
            out_specs=pl.BlockSpec((rows + INFO, step), lambda i, p: (0, i)),
        ),
        out_shape=jax.ShapeDtypeStruct((rows + INFO, half + depth), acts.dtype),
        compiler_params=pltpu.CompilerParams(vmem_limit_bytes=VMEM_BYTES),
        cost_estimate=SMALL,
        name="half",
    )(place, info, acts, grads)


def grams_kernel(table, xs, xc, ys, yc, zs, zc, out, held, result, in_sems, out_sems):
    rows, depth = xs.shape
    order = token_major(rows)
    sources = (xs, xc.at[:rows, xc.shape[1] - depth:], ys, yc, zs, zc)
    loads = [
        pltpu.make_async_copy(source, held.at[at], in_sems.at[at])
        for at, source in enumerate(sources)
    ]
    for load in loads:
        load.start()
    for load in loads:
        load.wait()
    for block in (YS, YC):
        held[block] = reorder(order, held[block])

    def leave(slot):
        return pltpu.make_async_copy(result.at[slot], out.at[slot], out_sems.at[slot])

    @pl.loop(0, SLOTS)
    def _(slot):
        result[slot] = lax.dot_general(
            held[table[slot]], held[table[SLOTS + slot]], NT, preferred_element_type=jnp.float32
        )
        leave(slot).start()

    for slot in range(SLOTS):
        leave(slot).wait()


def grams(table, grads, *messages):
    rows, width = grads.shape
    return pl.pallas_call(
        grams_kernel,
        in_specs=[pl.BlockSpec(memory_space=pltpu.SMEM)] + [pl.BlockSpec(memory_space=pl.ANY)] * 6,
        out_specs=pl.BlockSpec(memory_space=pl.ANY),
        out_shape=jax.ShapeDtypeStruct((SLOTS, rows, rows), jnp.float32),
        scratch_shapes=[
            pltpu.VMEM((6, rows, width), grads.dtype),
            pltpu.VMEM((SLOTS, rows, rows), jnp.float32),
            pltpu.SemaphoreType.DMA((6,)),
            pltpu.SemaphoreType.DMA((SLOTS,)),
        ],
        compiler_params=pltpu.CompilerParams(vmem_limit_bytes=VMEM_BYTES),
        cost_estimate=SMALL,
        name="grams",
    )(table, grads, *messages)


def product(one, two, inner):
    rows = inner.shape[0]
    inner[...] = lax.dot_general(
        one[:rows, :], two[:rows, :], NT, preferred_element_type=jnp.float32
    )


def token_sums(inner, gram, sums, ordered=True):
    examples, rows = sums.shape
    if ordered:
        sums[...] = sum(
            inner[at:at + examples, :] * gram[at:at + examples, :]
            for at in range(0, rows, examples)
        )
    else:
        weighted = inner[...] * gram[...]
        sums[...] = weighted.reshape(examples, TOK, rows).sum(axis=1)


def two_parts(value):
    high = value.astype(jnp.bfloat16)
    return high, (value - high.astype(jnp.float32)).astype(jnp.bfloat16)


def dot_parts(value, table):
    high, low = two_parts(value)
    return lax.dot_general(low, table, NT, preferred_element_type=jnp.float32) + lax.dot_general(
        high, table, NT, preferred_element_type=jnp.float32
    )


def side_by_side(values):
    return jnp.concatenate(values, axis=1)


def domain_sums(pairs, factor, place, info, sums):
    count, examples, rows = sums.shape
    example = lax.broadcasted_iota(jnp.int32, (LANES, rows), 0)
    column = lax.broadcasted_iota(jnp.int32, (LANES, rows), 1)
    gather = (lax.shift_right_logical(column, TOK_BITS) == example).astype(jnp.bfloat16)
    tiles = dot_parts(sums[...].reshape(count * examples, rows), gather)
    tiles = tiles.reshape(count, examples, LANES)
    mirrored, core, side = place
    lane = lax.broadcasted_iota(jnp.int32, (1, LANES), 1)
    row = lax.broadcasted_iota(jnp.int32, (DOMAINS, LANES), 0)
    hot = {
        block: ((value.astype(jnp.int32) == row) & (lane < examples)).astype(jnp.bfloat16)
        for block, value in info.items()
    }

    def listed_flag(block, apart):
        return jnp.sum(jnp.where(lane == examples + apart, info[block], 0.0), axis=1, keepdims=True)

    pad = jnp.zeros((LANES - examples, LANES), jnp.float32)
    groups = {}
    for at, pair in pairs:
        one, two, apart = PAIRS[pair]
        if one == XC:
            two_leads = core == 0
        elif two in (XS, XC):
            two_leads = side == 0
        else:
            two_leads = side == 1
        flag = jnp.where(two_leads, listed_flag(two, apart), listed_flag(one, apart))
        if pair in ONLY:
            flag = jnp.where(mirrored == ONLY[pair], flag, 0.0)
        tile = jnp.concatenate([tiles[at], pad], axis=0) * (flag * factor)
        groups.setdefault(one, []).append((two, *two_parts(tile)))
    total = {}

    def add(block, term):
        total[block] = total[block] + term if block in total else term

    for one, group in groups.items():
        others = side_by_side([hot[two] for two, _, _ in group])
        highs = side_by_side([high for _, high, _ in group])
        lows = side_by_side([low for _, _, low in group])
        add(one, lax.dot_general(
            side_by_side([others, others]), side_by_side([highs, lows]), NT,
            preferred_element_type=jnp.float32,
        ))
        columns_of = lax.dot_general(
            side_by_side([hot[one], hot[one]]), jnp.concatenate([highs, lows], axis=0), NN,
            preferred_element_type=jnp.float32,
        )
        for at, (two, _, _) in enumerate(group):
            add(two, columns_of[:, at * LANES:(at + 1) * LANES])
    return total


def copies_of(loads, sems):
    return {
        key: pltpu.make_async_copy(source, target, sems.at[at])
        for at, (key, (source, target)) in enumerate(loads.items())
    }


def start(copies, *keys):
    for key in keys:
        copies[key].start()


def wait(copies, *keys):
    for key in keys:
        copies[key].wait()


def info_row(notes, block):
    return notes[block].astype(jnp.float32)[:1]


def columns(ref, at, width):
    return ref.at[:, pl.ds(pl.multiple_of(at, LANES), width)]


def same_one_kernel(factor, own_info, acts, x_half, ys, zs, gram, out, notes,
                    held, own_v, half_v, gram_v, inner, sums, sems):
    rows, width = inner.shape[1], held.shape[2]
    quarter = acts.shape[1] // 4
    core, side = position()
    mirrored = core ^ side
    in_half = (1 - side) * quarter
    half_at = core * 2 * quarter
    copies = copies_of({
        XS: (columns(acts, half_at + in_half, width), held.at[XS, :rows]),
        XC: (columns(x_half, in_half, width), held.at[XC]),
        YS: (ys, held.at[YS]),
        ZS: (zs, held.at[ZS]),
        "g0": (gram.at[0], gram_v.at[0]),
        "g1": (gram.at[1], gram_v.at[1]),
        "g2": (gram.at[2], gram_v.at[2]),
        "own": (columns(acts, half_at, 2 * quarter), own_v),
        "half": (x_half.at[:, :2 * quarter], half_v),
        "g3": (gram.at[3], gram_v.at[3]),
        "info": (own_info, held.at[XS, rows:, :LANES]),
    }, sems)
    start(copies, YS, XS, "info", ZS, "g0", XC, "g1", "g2", "own", "half", "g3")
    wait(copies, YS, XS, "info")
    product(held.at[YS], held.at[XS], inner.at[0])
    wait(copies, "g0", ZS)
    product(held.at[YS], held.at[ZS], inner.at[1])
    token_sums(inner.at[0], gram_v.at[0], sums.at[0])
    wait(copies, "g1", XC, "g2")
    product(held.at[YS], held.at[XC], inner.at[0])
    token_sums(inner.at[1], gram_v.at[1], sums.at[1])
    wait(copies, "own", "half")
    product(half_v, own_v, inner.at[1])
    token_sums(inner.at[0], gram_v.at[2], sums.at[2])
    wait(copies, "g3")
    token_sums(inner.at[1], gram_v.at[3], sums.at[3], ordered=False)
    notes[...] = jnp.zeros_like(notes)
    for block in (XS, XC, YS, ZS):
        notes[block] = held[block, rows:, :LANES]
    info = {block: info_row(notes, block) for block in (XS, XC, YS, ZS)}
    total = domain_sums(tuple(enumerate(FIRST)), factor, (mirrored, core, side), info, sums)
    out[...] = jnp.zeros_like(out)
    for block, value in total.items():
        out[block] = value


def same_two_kernel(factor, at, notes, earlier, acts, x_half, ys, zs, gram, out,
                    held, notes_v, earlier_v, gram_v, inner, sums, sems):
    rows, width = inner.shape[1], held.shape[2]
    quarter = acts.shape[1] // 4
    core, side = position()
    mirrored = core ^ side
    in_half = (1 - side) * quarter
    copies = copies_of({
        XS: (columns(acts, core * 2 * quarter + in_half + at, width), held.at[XS, :rows]),
        XC: (columns(x_half, in_half + at, width), held.at[XC]),
        YS: (ys, held.at[YS, :rows]),
        ZS: (zs, held.at[ZS, :rows]),
        "g0": (gram.at[0], gram_v.at[0]),
        "g1": (gram.at[1], gram_v.at[1]),
        "g2": (gram.at[2], gram_v.at[2]),
        "notes": (notes, notes_v),
        "earlier": (earlier, earlier_v),
    }, sems)
    start(copies, YS, XS, ZS, "g0", "g1", XC, "g2", "notes", "earlier")
    wait(copies, YS, XS)
    product(held.at[YS], held.at[XS], inner.at[0])
    wait(copies, ZS, "g0")
    product(held.at[YS], held.at[ZS], inner.at[1])
    token_sums(inner.at[0], gram_v.at[0], sums.at[0])
    wait(copies, "g1", XC, "g2", "notes", "earlier")
    product(held.at[YS], held.at[XC], inner.at[0])
    token_sums(inner.at[1], gram_v.at[1], sums.at[1])
    token_sums(inner.at[0], gram_v.at[2], sums.at[2])
    info = {block: info_row(notes_v, block) for block in (XS, XC, YS, ZS)}
    pairs = ((0, 0), (1, 1), (2, 2))
    total = domain_sums(pairs, factor, (mirrored, core, side), info, sums)
    out[...] = earlier_v[...]
    for block, value in total.items():
        out[block] = earlier_v[block] + value


def position():
    me = lax.axis_index("ex")
    return me & 1, lax.shift_right_logical(me, 1) & 1


def cross_kernel(factor, at, notes, earlier, *refs):
    (acts, x_half, ys, yc, zs, zc, gram), refs = refs[:7], refs[7:]
    outs, (held, notes_v, earlier_v, gram_v, inner, sums, sems) = refs[:-7], refs[-7:]
    rows, width = inner.shape[1], held.shape[2]
    quarter = acts.shape[1] // 4
    core, side = position()
    mirrored = core ^ side
    in_half = (1 - side) * quarter
    work_at = core * 2 * quarter + in_half
    copies = copies_of({
        XS: (columns(acts, work_at + at, width), held.at[XS, :rows, :]),
        XC: (columns(x_half, in_half + at, width), held.at[XC]),
        YS: (ys, held.at[YS, :ys.shape[0]]),
        YC: (yc, held.at[YC, :yc.shape[0]]),
        ZS: (zs, held.at[ZS, :zs.shape[0]]),
        ZC: (zc, held.at[ZC, :zc.shape[0]]),
        "g4": (gram.at[4], gram_v.at[0]),
        "g5": (gram.at[5], gram_v.at[1]),
        "g6": (gram.at[6], gram_v.at[2]),
        "g2": (gram.at[2], gram_v.at[3]),
        "notes": (notes, notes_v),
        "earlier": (earlier, earlier_v),
    }, sems)
    start(copies, YC, XC, ZC, "g4", YS, ZS, "g5", XS, "g6", "g2", "notes", "earlier")
    wait(copies, YC, XC)
    product(held.at[YC], held.at[XC], inner.at[0])
    wait(copies, ZC)
    product(held.at[YC], held.at[ZC], inner.at[1])
    wait(copies, "g4", YS, ZS)
    token_sums(inner.at[0], gram_v.at[0], sums.at[0])
    product(held.at[jnp.where(mirrored == 0, YC, YS)], held.at[jnp.where(mirrored == 0, ZS, ZC)], inner.at[0])
    wait(copies, "g5", XS)
    token_sums(inner.at[1], gram_v.at[1], sums.at[1])
    wait(copies, "g6", "g2", "notes", "earlier")

    @pl.when(mirrored == 1)
    def _():
        product(held.at[YC], held.at[XS], inner.at[1])
        token_sums(inner.at[0], gram_v.at[2], sums.at[2])
        token_sums(inner.at[1], gram_v.at[3], sums.at[3])

    @pl.when(mirrored == 0)
    def _():
        token_sums(inner.at[0], gram_v.at[2], sums.at[2])
        sums[3] = jnp.zeros(sums.shape[1:], jnp.float32)

    if at == 0:
        total_out, notes_out = outs
        for block in (YC, ZC):
            notes_v[block] = held[block, rows:, :LANES]
        notes_out[...] = notes_v[...]
    info = {block: info_row(notes_v, block) for block in range(6)}
    pairs = ((0, 4), (1, 5), (2, 6), (2, 7), (3, 8))
    total = domain_sums(pairs, factor, (mirrored, core, side), info, sums)
    examples = sums.shape[1]
    for block, value in total.items():
        value = value + earlier_v[block]
        if at == 0:
            total_out[block] = value
        else:
            outs[block][...] = value[:, :examples]


def per_device(acts, grads, domain, listed):
    rows, width = acts.shape
    examples = rows // TOK
    quarter = width // 4
    me = lax.axis_index("ex")
    core = me % 2
    side = (me // 2) % 2
    mirrored = core ^ side

    pair_of = [
        [pair for pair in range(len(PAIRS)) if SLOT[pair] == slot] for slot in range(SLOTS)
    ]

    def listing(end):
        return [
            PAIRS[pairs[0]][end] if len(pairs) == 1 else jnp.where(
                mirrored == ONLY[pairs[0]], PAIRS[pairs[0]][end], PAIRS[pairs[1]][end])
            for pairs in pair_of
        ]

    table = jnp.stack([jnp.asarray(block, jnp.int32) for block in listing(0) + listing(1)])
    places = jnp.stack([core * 2 + side, core * 2 + (1 - side)]).astype(jnp.int32)
    cross_places = jnp.stack([(1 - core) * 2 + side, (1 - core) * 2 + (1 - side)]).astype(jnp.int32)
    half_place = jnp.stack([1 - core]).astype(jnp.int32)

    own_info = jnp.concatenate(
        [domain, listed[0], jnp.zeros((LANES - examples - 2,), jnp.int32)]
    )
    own_info = jnp.broadcast_to(own_info.astype(acts.dtype)[None, :], (INFO, LANES))

    grads_ys = send(grads, across, 0)
    grads_zs = send(grads, along, 0)
    cut_ys, cut_zs, cut_ys_two, cut_zs_two = cut(acts, own_info, places)
    own_info, _ = lax.optimization_barrier((own_info, cut_ys))
    cut_yc, cut_zc, cut_yc_two, cut_zc_two = cut(acts, own_info, cross_places)
    own_info, _ = lax.optimization_barrier((own_info, cut_yc))
    ys_one = send(cut_ys, across, 0)
    zs_one = send(cut_zs, along, 0)
    ys_two = send(cut_ys_two, across, 0)
    yc_one = send(cut_yc, across, 1)
    zc_one = send(cut_zc, along, 1)

    def exchange(*values):
        return lax.cond(
            listed[0, 0] < 2,
            lambda *sent: tuple(send(value, stay, 1) for value in sent),
            lambda *sent: tuple(jnp.zeros_like(value) for value in sent),
            *values,
        )

    x_half, = exchange(cut_half(acts, grads, own_info, half_place))
    grads_ys, grads_zs, x_half = lax.optimization_barrier((grads_ys, grads_zs, x_half))
    grads_yc, grads_zc = exchange(grads_ys, grads_zs)
    factor = 1.0 / (TOK * math.sqrt(width * grads.shape[1]))

    gram = grams(table, grads, x_half, grads_ys, grads_yc, grads_zs, grads_zc)
    cut_zs_two, cut_yc_two, gram = lax.optimization_barrier((cut_zs_two, cut_yc_two, gram))
    zs_two = send(cut_zs_two, along, 0)
    yc_two = send(cut_yc_two, across, 1)

    vmem = pl.BlockSpec(memory_space=pltpu.VMEM)
    hbm = pl.BlockSpec(memory_space=pl.ANY)
    all_sums = jax.ShapeDtypeStruct((6, DOMAINS, LANES), jnp.float32)
    all_notes = jax.ShapeDtypeStruct((6, INFO, LANES), acts.dtype)
    notes_v = pltpu.VMEM(all_notes.shape, acts.dtype)
    sums_v = pltpu.VMEM(all_sums.shape, jnp.float32)

    def call(kernel, name, vmem_bytes, width, extra, operands, out_shape):
        return pl.pallas_call(
            kernel,
            in_specs=[hbm] * len(operands),
            out_specs=[vmem] * len(out_shape),
            out_shape=out_shape,
            scratch_shapes=[pltpu.VMEM((6, rows + INFO, width), acts.dtype)] + extra + [
                pltpu.VMEM((4, rows, rows), jnp.float32),
                pltpu.VMEM((2, rows, rows), jnp.float32),
                pltpu.VMEM((4, examples, rows), jnp.float32),
                pltpu.SemaphoreType.DMA((12,)),
            ],
            compiler_params=pltpu.CompilerParams(vmem_limit_bytes=vmem_bytes),
            cost_estimate=SMALL,
            name=name,
        )(*operands)

    one, two = chunks(quarter)
    extra = [
        pltpu.VMEM((rows, 2 * quarter), acts.dtype),
        pltpu.VMEM((rows + INFO, 2 * quarter), acts.dtype),
    ]
    partial = functools.partial
    sums, notes = call(
        partial(same_one_kernel, factor), "same_one", VMEM_BYTES, one, extra,
        (own_info, acts, x_half, ys_one, zs_one, gram), [all_sums, all_notes],
    )
    cut_zc_two, sums = lax.optimization_barrier((cut_zc_two, sums))
    zc_two = send(cut_zc_two, along, 1)
    extra = [notes_v, sums_v]
    sums, notes = call(
        partial(cross_kernel, factor, 0), "cross_one", PAIRS_VMEM_BYTES, one, extra,
        (notes, sums, acts, x_half, ys_one, yc_one, zs_one, zc_one, gram), [all_sums, all_notes],
    )
    sums, = call(
        partial(same_two_kernel, factor, one), "same_two", PAIRS_VMEM_BYTES, two, extra,
        (notes, sums, acts, x_half, ys_two, zs_two, gram), [all_sums],
    )
    sums = call(
        partial(cross_kernel, factor, one), "cross_two", PAIRS_VMEM_BYTES, two, extra,
        (notes, sums, acts, x_half, ys_two, yc_two, zs_two, zc_two, gram),
        [jax.ShapeDtypeStruct((DOMAINS, examples), jnp.float32)] * 6,
    )

    total = sums[XS]
    total = total + send(sums[ZS], against, 0)
    total = total + send(sums[ZC], against, 1)
    total = total + send(sums[YS], across, 0)
    total = total + send(sums[YC], across, 1)
    total = total + send(sums[XC], stay, 1)
    return total.T


def solution(mesh):
    in_specs = (
        P(("groups", "ex"), None),
        P(("groups", "ex"), None),
        P(("groups", "ex")),
        P(("groups", "ex"), None),
    )
    out_specs = P(("groups", "ex"), None)
    return jax.shard_map(
        per_device, mesh=mesh, in_specs=in_specs, out_specs=out_specs, check_vma=False
    )
```

profile of v0, /device:TPU:0, one launch (start us, length us, event | category | flops | bytes accessed | tf_op | source)
XLA Modules:
  0.0 142.2 jit_solution(4586177264014503687)
XLA Ops:
  0.0 5.0 %collective-permute-start.4 = (bf16[768,1024]{1,0:T(8,128)(2,1)}, bf16[768,1024]{1,0:T(8,128)(2,1)}, u32[]{:S(2)}, u32[]{:S(2)}) collective-permute-start(bf16[768,1024]{1,0:T(8,128)(2,1)} %xs.1), channel_id=1, source_target_pairs={{0,12},{1,13},{2,6},{3,7},{4,0},{5,1},{6,10},{7,11},{8,4},{9,5},{1... | collective-permute-start | bytes 4718600 | tf_op jit(solution)/shard_map/ppermute | solution.py:57
  7.7 6.5 %cut.2 = (bf16[784,1024]{1,0:T(8,128)(2,1)}, bf16[784,1024]{1,0:T(8,128)(2,1)}, bf16[768,256]{1,0:T(8,128)(2,1)}, bf16[768,256]{1,0:T(8,128)(2,1)}) custom-call(s32[2]{0:T(128)} %pad_add_fusion.places, bf16[16,128]{1,0:T(8,128)(2,1)} %broadcast_in_dim.2.info.own_info, bf16[768,5120]{1,0:T(8,128)(2,1)} %refs_0_.3, bf16[768,5120]{1,0:T(8,128)(2,1)} %refs_0_.3), custom_call_target="tpu_custom_call" | custom-call | flops 1 | bytes 1 | tf_op jit(solution)/shard_map/cut/pallas_call | solution.py:97
  14.2 1.7 %collective-permute-start.6 = (bf16[784,1024]{1,0:T(8,128)(2,1)}, bf16[784,1024]{1,0:T(8,128)(2,1)}, u32[]{:S(2)}, u32[]{:S(2)}) collective-permute-start(bf16[784,1024]{1,0:T(8,128)(2,1)} %get-tuple-element.50), channel_id=1, source_target_pairs={{0,12},{1,13},{2,6},{3,7},{4,0},{5,1},{6,10},{7,11},{8,4},{9,5},{1... | collective-permute-start | bytes 4816904 | tf_op jit(solution)/shard_map/ppermute | solution.py:57
  16.7 6.5 %cut.3 = (bf16[784,1024]{1,0:T(8,128)(2,1)}, bf16[784,1024]{1,0:T(8,128)(2,1)}, bf16[768,256]{1,0:T(8,128)(2,1)}, bf16[768,256]{1,0:T(8,128)(2,1)}) custom-call(s32[2]{0:T(128)} %pad_add_fusion.1.places, bf16[16,128]{1,0:T(8,128)(2,1)} %broadcast_in_dim.2.info.own_info, bf16[768,5120]{1,0:T(8,128)(2,1)} %refs_0_.3, bf16[768,5120]{1,0:T(8,128)(2,1)} %refs_0_.3), custom_call_target="tpu_custom_call" | custom-call | flops 1 | bytes 1 | tf_op jit(solution)/shard_map/cut/pallas_call | solution.py:97
  23.2 7.8 %half.1 = bf16[784,3584]{1,0:T(8,128)(2,1)} custom-call(s32[1]{0:T(128)} %bitcast.6.place, bf16[16,128]{1,0:T(8,128)(2,1)} %broadcast_in_dim.2.info.own_info, bf16[768,5120]{1,0:T(8,128)(2,1)} %refs_0_.3, bf16[768,1024]{1,0:T(8,128)(2,1)} %xs.1), custom_call_target="tpu_custom_call" | custom-call | flops 1 | bytes 1 | tf_op jit(solution)/shard_map/half/pallas_call | solution.py:132
  31.1 9.6 %conditional.2 = (bf16[784,3584]{1,0:T(8,128)(2,1)}) conditional(s32[]{:T(128)} %bitcast.5, () %tuple.26, bf16[784,3584]{1,0:T(8,128)(2,1)} %half.1), branch_computations={%region_0.1_spmd, %region_1.2_spmd} | conditional | bytes 22478896 | solution.py:506
  31.2 9.5 %collective-permute-done = bf16[784,3584]{1,0:T(8,128)(2,1)} collective-permute-done((bf16[784,3584]{1,0:T(8,128)(2,1)}, bf16[784,3584]{1,0:T(8,128)(2,1)}, u32[]{:S(2)}, u32[]{:S(2)}) %collective-permute-start) | collective-permute-done | bytes 5619744 | tf_op jit(solution)/shard_map/cond/branch_1_fun/ppermute | solution.py:57
  40.8 3.6 %collective-permute-start.8 = (bf16[784,1024]{1,0:T(8,128)(2,1)}, bf16[784,1024]{1,0:T(8,128)(2,1)}, u32[]{:S(2)}, u32[]{:S(2)}) collective-permute-start(bf16[784,1024]{1,0:T(8,128)(2,1)} %get-tuple-element.62), channel_id=1, source_target_pairs={{0,13},{1,12},{2,7},{3,6},{4,1},{5,0},{6,11},{7,10},{8,5},{9,4},{1... | collective-permute-start | bytes 4816904 | tf_op jit(solution)/shard_map/ppermute | solution.py:57
  44.3 6.0 %conditional.3 = (bf16[768,1024]{1,0:T(8,128)(2,1)}, bf16[768,1024]{1,0:T(8,128)(2,1)}) conditional(s32[]{:T(128)} %bitcast.5, () %tuple.28, (bf16[768,1024]{1,0:T(8,128)(2,1)}, bf16[768,1024]{1,0:T(8,128)(2,1)}) %tuple.29), branch_computations={%region_2.3_spmd, %region_3.4_spmd} | conditional | bytes 12583008 | solution.py:506
  44.8 3.2 %collective-permute-done.1 = bf16[768,1024]{1,0:T(8,128)(2,1)} collective-permute-done((bf16[768,1024]{1,0:T(8,128)(2,1)}, bf16[768,1024]{1,0:T(8,128)(2,1)}, u32[]{:S(2)}, u32[]{:S(2)}) %collective-permute-start.1) | collective-permute-done | bytes 1572896 | tf_op jit(solution)/shard_map/cond/branch_1_fun/ppermute | solution.py:57
  48.1 2.2 %collective-permute-done.2 = bf16[768,1024]{1,0:T(8,128)(2,1)} collective-permute-done((bf16[768,1024]{1,0:T(8,128)(2,1)}, bf16[768,1024]{1,0:T(8,128)(2,1)}, u32[]{:S(2)}, u32[]{:S(2)}) %collective-permute-start.2) | collective-permute-done | bytes 1572896 | tf_op jit(solution)/shard_map/cond/branch_1_fun/ppermute | solution.py:57
  50.3 2.0 %collective-permute-start.9 = (bf16[768,256]{1,0:T(8,128)(2,1)}, bf16[768,256]{1,0:T(8,128)(2,1)S(1)}, u32[]{:S(2)}, u32[]{:S(2)}) collective-permute-start(bf16[768,256]{1,0:T(8,128)(2,1)} %get-tuple-element.65), channel_id=1, source_target_pairs={{0,2},{1,3},{2,0},{3,1},{4,6},{5,7},{6,4},{7,5},{8,10},{9,11},{10,... | collective-permute-start | bytes 1179656 | tf_op jit(solution)/shard_map/ppermute | solution.py:57
  53.0 18.5 %grams.1.gram.refs_6_ = f32[7,768,768]{2,1,0:T(8,128)} custom-call(s32[14]{0:T(128)} %stack.47.table, bf16[768,1024]{1,0:T(8,128)(2,1)} %xs.1, bf16[784,3584]{1,0:T(8,128)(2,1)} %get-tuple-element.79.xc.x_half.refs_1_, bf16[768,1024]{1,0:T(8,128)(2,1)} %collective-permute-done.3.ys, bf16[768,1024]{1,0:T(8,128)(2,1)} %get-tuple-element.55.yc, ...), custom_call_target="tpu_custom_call" | custom-call | flops 1 | bytes 1 | tf_op jit(solution)/shard_map/grams/pallas_call | solution.py:182
  71.4 3.1 %collective-permute-done.6.zs.refs_4_ = bf16[784,1024]{1,0:T(8,128)(2,1)} collective-permute-done((bf16[784,1024]{1,0:T(8,128)(2,1)}, bf16[784,1024]{1,0:T(8,128)(2,1)}, u32[]{:S(2)}, u32[]{:S(2)}) %collective-permute-start.6) | collective-permute-done | bytes 1605664 | tf_op jit(solution)/shard_map/ppermute | solution.py:57
  74.6 4.3 %collective-permute-start.10 = (bf16[768,256]{1,0:T(8,128)(2,1)}, bf16[768,256]{1,0:T(8,128)(2,1)S(1)}, u32[]{:S(2)}, u32[]{:S(2)}) collective-permute-start(bf16[768,256]{1,0:T(8,128)(2,1)} %get-tuple-element.66), channel_id=1, source_target_pairs={{0,12},{1,13},{2,6},{3,7},{4,0},{5,1},{6,10},{7,11},{8,4},{9,5},{1... | collective-permute-start | bytes 1179656 | tf_op jit(solution)/shard_map/ppermute | solution.py:57
  78.9 14.9 %same_one.1 = (f32[6,48,128]{2,1,0:T(8,128)}, bf16[6,16,128]{2,1,0:T(8,128)(2,1)}) custom-call(bf16[16,128]{1,0:T(8,128)(2,1)} %broadcast_in_dim.2.info.own_info, bf16[768,5120]{1,0:T(8,128)(2,1)} %refs_0_.3, bf16[784,3584]{1,0:T(8,128)(2,1)} %get-tuple-element.79.xc.x_half.refs_1_, bf16[784,1024]{1,0:T(8,128)(2,1)} %collective-permute-done.5.ys.refs_2_, ...), custom_call_target="tpu_custom_call" | custom-call | flops 1 | bytes 1 | tf_op jit(solution)/shard_map/same_one/pallas_call | solution.py:531
  93.8 15.2 %collective-permute-done.8.refs_5_ = bf16[784,1024]{1,0:T(8,128)(2,1)} collective-permute-done((bf16[784,1024]{1,0:T(8,128)(2,1)}, bf16[784,1024]{1,0:T(8,128)(2,1)}, u32[]{:S(2)}, u32[]{:S(2)}) %collective-permute-start.8) | collective-permute-done | bytes 1605664 | tf_op jit(solution)/shard_map/ppermute | solution.py:57
  109.0 3.7 %collective-permute-start.12 = (bf16[768,256]{1,0:T(8,128)(2,1)}, bf16[768,256]{1,0:T(8,128)(2,1)S(1)}, u32[]{:S(2)}, u32[]{:S(2)}) collective-permute-start(bf16[768,256]{1,0:T(8,128)(2,1)} %get-tuple-element.68), channel_id=1, source_target_pairs={{0,13},{1,12},{2,7},{3,6},{4,1},{5,0},{6,11},{7,10},{8,5},{9,4},{1... | collective-permute-start | bytes 1179656 | tf_op jit(solution)/shard_map/ppermute | solution.py:57
  114.8 8.8 %cross_one.1 = (f32[6,48,128]{2,1,0:T(8,128)S(1)}, bf16[6,16,128]{2,1,0:T(8,128)(2,1)S(1)}) custom-call(bf16[6,16,128]{2,1,0:T(8,128)(2,1)S(1)} %copy-done.1, f32[6,48,128]{2,1,0:T(8,128)S(1)} %copy-done, bf16[768,5120]{1,0:T(8,128)(2,1)} %refs_0_.3, bf16[784,3584]{1,0:T(8,128)(2,1)} %get-tuple-element.79.xc.x_half.refs_1_, ...), custom_call_target="tpu_custom_call" | custom-call | flops 1 | bytes 1 | tf_op jit(solution)/shard_map/cross_one/pallas_call | solution.py:531
  123.6 5.1 %same_two.1.earlier = f32[6,48,128]{2,1,0:T(8,128)S(1)} custom-call(bf16[6,16,128]{2,1,0:T(8,128)(2,1)S(1)} %get-tuple-element.63.notes, f32[6,48,128]{2,1,0:T(8,128)S(1)} %get-tuple-element.64.earlier, bf16[768,5120]{1,0:T(8,128)(2,1)S(1)} %bitcast.16, bf16[784,3584]{1,0:T(8,128)(2,1)} %get-tuple-element.79.xc.x_half.refs_1_, ...), custom_call_target="tpu_custom_call" | custom-call | flops 1 | bytes 1 | tf_op jit(solution)/shard_map/same_two/pallas_call | solution.py:531
  128.8 5.4 %cross_two.1 = (f32[48,96]{1,0:T(8,128)S(1)}, f32[48,96]{1,0:T(8,128)S(1)}, f32[48,96]{1,0:T(8,128)S(1)}, f32[48,96]{1,0:T(8,128)S(1)}, f32[48,96]{1,0:T(8,128)S(1)}, /*index=5*/f32[48,96]{1,0:T(8,128)S(1)}) custom-call(bf16[6,16,128]{2,1,0:T(8,128)(2,1)S(1)} %get-tuple-element.63.notes, f32[6,48,128]{2,1,0:T(8,128)S(1)} %same_two.1.earlier, ...), custom_call_target="tpu_custom_call" | custom-call | flops 1 | bytes 1 | tf_op jit(solution)/shard_map/cross_two/pallas_call | solution.py:531
  135.2 3.0 %collective-permute-start.15 = (f32[48,96]{1,0:T(8,128)S(1)}, f32[48,96]{1,0:T(8,128)S(1)}, u32[]{:S(2)}, u32[]{:S(2)}) collective-permute-start(f32[48,96]{1,0:T(8,128)S(1)} %get-tuple-element.72), channel_id=1, source_target_pairs={{0,2},{1,3},{2,0},{3,1},{4,6},{5,7},{6,4},{7,5},{8,10},{9,11},{10,... | collective-permute-start | bytes 55304 | tf_op jit(solution)/shard_map/ppermute | solution.py:57
  138.3 1.7 %collective-permute-done.13 = f32[48,96]{1,0:T(8,128)S(1)} collective-permute-done((f32[48,96]{1,0:T(8,128)S(1)}, f32[48,96]{1,0:T(8,128)S(1)}, u32[]{:S(2)}, u32[]{:S(2)}) %collective-permute-start.13) | collective-permute-done | bytes 18464 | tf_op jit(solution)/shard_map/ppermute | solution.py:57
  140.5 1.1 collective-permute-done.16
  (44 shorter events, 9.1 us)
Async XLA Ops:
  0.0 44.3 %collective-permute-start.4 = (bf16[768,1024]{1,0:T(8,128)(2,1)}, bf16[768,1024]{1,0:T(8,128)(2,1)}, u32[]{:S(2)}, u32[]{:S(2)}) collective-permute-start(bf16[768,1024]{1,0:T(8,128)(2,1)} %xs.1), channel_id=1, source_target_pairs={{0,12},{1,13},{2,6},{3,7},{4,0},{5,1},{6,10},{7,11},{8,4},{9,5},{1... | collective-permute-start | bytes 4718600 | tf_op jit(solution)/shard_map/ppermute | solution.py:57
  5.0 39.3 %collective-permute-start.3 = (bf16[768,1024]{1,0:T(8,128)(2,1)}, bf16[768,1024]{1,0:T(8,128)(2,1)}, u32[]{:S(2)}, u32[]{:S(2)}) collective-permute-start(bf16[768,1024]{1,0:T(8,128)(2,1)} %xs.1), channel_id=1, source_target_pairs={{0,2},{1,3},{2,0},{3,1},{4,6},{5,7},{6,4},{7,5},{8,10},{9,11},{10,... | collective-permute-start | bytes 4718600 | tf_op jit(solution)/shard_map/ppermute | solution.py:57
  14.2 60.4 %collective-permute-start.6 = (bf16[784,1024]{1,0:T(8,128)(2,1)}, bf16[784,1024]{1,0:T(8,128)(2,1)}, u32[]{:S(2)}, u32[]{:S(2)}) collective-permute-start(bf16[784,1024]{1,0:T(8,128)(2,1)} %get-tuple-element.50), channel_id=1, source_target_pairs={{0,12},{1,13},{2,6},{3,7},{4,0},{5,1},{6,10},{7,11},{8,4},{9,5},{1... | collective-permute-start | bytes 4816904 | tf_op jit(solution)/shard_map/ppermute | solution.py:57
  15.9 63.0 %collective-permute-start.5 = (bf16[784,1024]{1,0:T(8,128)(2,1)}, bf16[784,1024]{1,0:T(8,128)(2,1)}, u32[]{:S(2)}, u32[]{:S(2)}) collective-permute-start(bf16[784,1024]{1,0:T(8,128)(2,1)} %get-tuple-element.45), channel_id=1, source_target_pairs={{0,2},{1,3},{2,0},{3,1},{4,6},{5,7},{6,4},{7,5},{8,10},{9,11},{10,... | collective-permute-start | bytes 4816904 | tf_op jit(solution)/shard_map/ppermute | solution.py:57
  23.2 7.9 %copy-start.2 = (s32[1,2]{1,0:T(1,128)S(1)}, s32[1,2]{1,0:T(1,128)}, u32[]{:S(2)}) copy-start(s32[1,2]{1,0:T(1,128)} %param.11) | copy-start | bytes 28
  31.1 9.6 %collective-permute-start = (bf16[784,3584]{1,0:T(8,128)(2,1)}, bf16[784,3584]{1,0:T(8,128)(2,1)}, u32[]{:S(2)}, u32[]{:S(2)}) collective-permute-start(bf16[784,3584]{1,0:T(8,128)(2,1)} %param.1), channel_id=1, source_target_pairs={{0,1},{1,0},{2,3},{3,2},{4,5},{5,4},{6,7},{7,6},{8,9},{9,8},{10,11... | collective-permute-start | bytes 16859144 | tf_op jit(solution)/shard_map/cond/branch_1_fun/ppermute | solution.py:57
  40.8 68.2 %collective-permute-start.8 = (bf16[784,1024]{1,0:T(8,128)(2,1)}, bf16[784,1024]{1,0:T(8,128)(2,1)}, u32[]{:S(2)}, u32[]{:S(2)}) collective-permute-start(bf16[784,1024]{1,0:T(8,128)(2,1)} %get-tuple-element.62), channel_id=1, source_target_pairs={{0,13},{1,12},{2,7},{3,6},{4,1},{5,0},{6,11},{7,10},{8,5},{9,4},{1... | collective-permute-start | bytes 4816904 | tf_op jit(solution)/shard_map/ppermute | solution.py:57
  44.3 3.8 %collective-permute-start.1 = (bf16[768,1024]{1,0:T(8,128)(2,1)}, bf16[768,1024]{1,0:T(8,128)(2,1)}, u32[]{:S(2)}, u32[]{:S(2)}) collective-permute-start(bf16[768,1024]{1,0:T(8,128)(2,1)} %get-tuple-element.13), channel_id=1, source_target_pairs={{0,1},{1,0},{2,3},{3,2},{4,5},{5,4},{6,7},{7,6},{8,9},{9,8},{10,11... | collective-permute-start | bytes 4718600 | tf_op jit(solution)/shard_map/cond/branch_1_fun/ppermute | solution.py:57
  44.7 5.6 %collective-permute-start.2 = (bf16[768,1024]{1,0:T(8,128)(2,1)}, bf16[768,1024]{1,0:T(8,128)(2,1)}, u32[]{:S(2)}, u32[]{:S(2)}) collective-permute-start(bf16[768,1024]{1,0:T(8,128)(2,1)} %get-tuple-element.14), channel_id=1, source_target_pairs={{0,1},{1,0},{2,3},{3,2},{4,5},{5,4},{6,7},{7,6},{8,9},{9,8},{10,11... | collective-permute-start | bytes 4718600 | tf_op jit(solution)/shard_map/cond/branch_1_fun/ppermute | solution.py:57
  50.3 62.4 %collective-permute-start.7 = (bf16[784,1024]{1,0:T(8,128)(2,1)}, bf16[784,1024]{1,0:T(8,128)(2,1)}, u32[]{:S(2)}, u32[]{:S(2)}) collective-permute-start(bf16[784,1024]{1,0:T(8,128)(2,1)} %get-tuple-element.47), channel_id=1, source_target_pairs={{0,3},{1,2},{2,1},{3,0},{4,7},{5,6},{6,5},{7,4},{8,11},{9,10},{10,... | collective-permute-start | bytes 4816904 | tf_op jit(solution)/shard_map/ppermute | solution.py:57
  50.3 73.2 %collective-permute-start.9 = (bf16[768,256]{1,0:T(8,128)(2,1)}, bf16[768,256]{1,0:T(8,128)(2,1)S(1)}, u32[]{:S(2)}, u32[]{:S(2)}) collective-permute-start(bf16[768,256]{1,0:T(8,128)(2,1)} %get-tuple-element.65), channel_id=1, source_target_pairs={{0,2},{1,3},{2,0},{3,1},{4,6},{5,7},{6,4},{7,5},{8,10},{9,11},{10,... | collective-permute-start | bytes 1179656 | tf_op jit(solution)/shard_map/ppermute | solution.py:57
  74.6 49.0 %collective-permute-start.10 = (bf16[768,256]{1,0:T(8,128)(2,1)}, bf16[768,256]{1,0:T(8,128)(2,1)S(1)}, u32[]{:S(2)}, u32[]{:S(2)}) collective-permute-start(bf16[768,256]{1,0:T(8,128)(2,1)} %get-tuple-element.66), channel_id=1, source_target_pairs={{0,12},{1,13},{2,6},{3,7},{4,0},{5,1},{6,10},{7,11},{8,4},{9,5},{1... | collective-permute-start | bytes 1179656 | tf_op jit(solution)/shard_map/ppermute | solution.py:57
  78.9 49.9 %collective-permute-start.11 = (bf16[768,256]{1,0:T(8,128)(2,1)}, bf16[768,256]{1,0:T(8,128)(2,1)}, u32[]{:S(2)}, u32[]{:S(2)}) collective-permute-start(bf16[768,256]{1,0:T(8,128)(2,1)} %get-tuple-element.67), channel_id=1, source_target_pairs={{0,3},{1,2},{2,1},{3,0},{4,7},{5,6},{6,5},{7,4},{8,11},{9,10},{10,... | collective-permute-start | bytes 1179656 | tf_op jit(solution)/shard_map/ppermute | solution.py:57
  109.0 19.8 %collective-permute-start.12 = (bf16[768,256]{1,0:T(8,128)(2,1)}, bf16[768,256]{1,0:T(8,128)(2,1)S(1)}, u32[]{:S(2)}, u32[]{:S(2)}) collective-permute-start(bf16[768,256]{1,0:T(8,128)(2,1)} %get-tuple-element.68), channel_id=1, source_target_pairs={{0,13},{1,12},{2,7},{3,6},{4,1},{5,0},{6,11},{7,10},{8,5},{9,4},{1... | collective-permute-start | bytes 1179656 | tf_op jit(solution)/shard_map/ppermute | solution.py:57
  112.7 10.9 %slice-start = ((s8[7864320]{0:T(1024)(128)(4,1)}), s8[4194304]{0:T(1024)(128)(4,1)S(1)}, s32[]{:S(2)}) async-start(s8[7864320]{0:T(1024)(128)(4,1)} %bitcast.15), calls=%async_computation | async-start | bytes 8388608
  112.7 1.1 copy-start
  113.8 1.0 copy-start.1
  114.8 8.8 %slice-start.1 = ((s8[7864320]{0:T(1024)(128)(4,1)}), s8[3670016]{0:T(1024)(128)(4,1)S(1)}, s32[]{:S(2)}) async-start(s8[7864320]{0:T(1024)(128)(4,1)} %bitcast.15), calls=%async_computation.1 | async-start | bytes 7340032
  134.2 5.9 %collective-permute-start.13 = (f32[48,96]{1,0:T(8,128)S(1)}, f32[48,96]{1,0:T(8,128)S(1)}, u32[]{:S(2)}, u32[]{:S(2)}) collective-permute-start(f32[48,96]{1,0:T(8,128)S(1)} %get-tuple-element.70), channel_id=1, source_target_pairs={{0,4},{1,5},{2,14},{3,15},{4,8},{5,9},{6,2},{7,3},{8,12},{9,13},{1... | collective-permute-start | bytes 55304 | tf_op jit(solution)/shard_map/ppermute | solution.py:57
  134.2 6.3 %collective-permute-start.14 = (f32[48,96]{1,0:T(8,128)S(1)}, f32[48,96]{1,0:T(8,128)S(1)}, u32[]{:S(2)}, u32[]{:S(2)}) collective-permute-start(f32[48,96]{1,0:T(8,128)S(1)} %get-tuple-element.71), channel_id=1, source_target_pairs={{0,5},{1,4},{2,15},{3,14},{4,9},{5,8},{6,3},{7,2},{8,13},{9,12},{1... | collective-permute-start | bytes 55304 | tf_op jit(solution)/shard_map/ppermute | solution.py:57
  135.2 5.3 %collective-permute-start.15 = (f32[48,96]{1,0:T(8,128)S(1)}, f32[48,96]{1,0:T(8,128)S(1)}, u32[]{:S(2)}, u32[]{:S(2)}) collective-permute-start(f32[48,96]{1,0:T(8,128)S(1)} %get-tuple-element.72), channel_id=1, source_target_pairs={{0,2},{1,3},{2,0},{3,1},{4,6},{5,7},{6,4},{7,5},{8,10},{9,11},{10,... | collective-permute-start | bytes 55304 | tf_op jit(solution)/shard_map/ppermute | solution.py:57
  138.2 3.4 %collective-permute-start.16 = (f32[48,96]{1,0:T(8,128)S(1)}, f32[48,96]{1,0:T(8,128)S(1)}, u32[]{:S(2)}, u32[]{:S(2)}) collective-permute-start(f32[48,96]{1,0:T(8,128)S(1)} %get-tuple-element.73), channel_id=1, source_target_pairs={{0,3},{1,2},{2,1},{3,0},{4,7},{5,6},{6,5},{7,4},{8,11},{9,10},{10,... | collective-permute-start | bytes 55304 | tf_op jit(solution)/shard_map/ppermute | solution.py:57
  138.2 3.4 %collective-permute-start.17 = (f32[48,96]{1,0:T(8,128)S(1)}, f32[48,96]{1,0:T(8,128)S(1)}, u32[]{:S(2)}, u32[]{:S(2)}) collective-permute-start(f32[48,96]{1,0:T(8,128)S(1)} %get-tuple-element.74), channel_id=1, source_target_pairs={{0,1},{1,0},{2,3},{3,2},{4,5},{5,4},{6,7},{7,6},{8,9},{9,8},{10,11... | collective-permute-start | bytes 55304 | tf_op jit(solution)/shard_map/ppermute | solution.py:57
where the time goes:
time: 143 us; the launch traced here: 142 us
  Pallas kernels  73.5 us (51%)
  waiting for transfers between devices  36.7 us (26%)
  starting transfers between devices  25.4 us (18%)
  local copies, waits for them, and re-layouts  3.3 us (2%)
  other arithmetic  3.21 us (2%)
    ppermute x18, waiting for transfers between devices, send(): return lax.ppermute(value, 'ex', pairs)  36.7 us
    pallas_call x4, Pallas kernels, call(): pl.pallas_call(kernel, in_specs=[hbm] * len(operands), out_specs=[vmem] *...  34.2 us
    ppermute x18, starting transfers between devices, send(): return lax.ppermute(value, 'ex', pairs)  25.4 us
    pallas_call x1, Pallas kernels, grams(): pl.pallas_call(grams_kernel, in_specs=[pl.BlockSpec(memory_space=pltpu.SM...  18.5 us
    pallas_call x2, Pallas kernels, cut(): pl.pallas_call(cut_kernel, grid_spec=pltpu.PrefetchScalarGridSpec(num_sca...  13 us
    pallas_call x1, Pallas kernels, cut_half(): pl.pallas_call(functools.partial(half_kernel, steps), grid_spec=pltpu.Pre...  7.85 us
  transfers between devices with their start and end apart: 18, of which 8 were waited for; matrix products, arithmetic and copies ran while one was open for 3% of the time, Pallas kernels for 48%

commit v1 on v0

--- a/solution.py
+++ b/solution.py
@@ -13,7 +13,7 @@
 DOMAINS = 48
 LANES = 128
 VMEM_BYTES = 63 * 1024 * 1024
-PAIRS_VMEM_BYTES = 44 * 1024 * 1024
+LAST_VMEM_BYTES = 44 * 1024 * 1024
 
 INFO = 16
 
@@ -76,7 +76,7 @@
 
 
 def chunks(quarter):
-    second = quarter // LANES // 5 * LANES
+    second = quarter // LANES * 3 // 10 * LANES
     return quarter - second, second
 
 
@@ -558,15 +558,15 @@
     zc_two = send(cut_zc_two, along, 1)
     extra = [notes_v, sums_v]
     sums, notes = call(
-        partial(cross_kernel, factor, 0), "cross_one", PAIRS_VMEM_BYTES, one, extra,
+        partial(cross_kernel, factor, 0), "cross_one", LAST_VMEM_BYTES, one, extra,
         (notes, sums, acts, x_half, ys_one, yc_one, zs_one, zc_one, gram), [all_sums, all_notes],
     )
     sums, = call(
-        partial(same_two_kernel, factor, one), "same_two", PAIRS_VMEM_BYTES, two, extra,
+        partial(same_two_kernel, factor, one), "same_two", LAST_VMEM_BYTES, two, extra,
         (notes, sums, acts, x_half, ys_two, zs_two, gram), [all_sums],
     )
     sums = call(
-        partial(cross_kernel, factor, one), "cross_two", PAIRS_VMEM_BYTES, two, extra,
+        partial(cross_kernel, factor, one), "cross_two", LAST_VMEM_BYTES, two, extra,
         (notes, sums, acts, x_half, ys_two, yc_two, zs_two, zc_two, gram),
         [jax.ShapeDtypeStruct((DOMAINS, examples), jnp.float32)] * 6,
     )

time: 143 us -> 139 us (0.972)
  starting transfers between devices: 25.4 us -> 21.3 us
    ppermute x18, starting transfers between devices: 25.4 us -> 21.3 us  [send(): return lax.ppermute(value, 'ex', pairs)]
  transfers between devices with their start and end apart: 18 -> 18, of which waited for: 8 -> 11; matrix products, arithmetic and copies ran while one was open for 3% -> 3% of each run, Pallas kernels for 48% -> 49%
where the time goes in v1:
time: 139 us
  Pallas kernels  74 us (53%)
  waiting for transfers between devices  36.7 us (26%)
  starting transfers between devices  21.3 us (15%)
  local copies, waits for them, and re-layouts  3.3 us (2%)
  other arithmetic  3.26 us (2%)
    ppermute x18, waiting for transfers between devices, send(): return lax.ppermute(value, 'ex', pairs)  36.7 us
    pallas_call x4, Pallas kernels, call(): pl.pallas_call(kernel, in_specs=[hbm] * len(operands), out_specs=[vmem] *...  34.2 us
    ppermute x18, starting transfers between devices, send(): return lax.ppermute(value, 'ex', pairs)  21.3 us
    pallas_call x1, Pallas kernels, grams(): pl.pallas_call(grams_kernel, in_specs=[pl.BlockSpec(memory_space=pltpu.SM...  18.5 us
    pallas_call x2, Pallas kernels, cut(): pl.pallas_call(cut_kernel, grid_spec=pltpu.PrefetchScalarGridSpec(num_sca...  13.6 us
    pallas_call x1, Pallas kernels, cut_half(): pl.pallas_call(functools.partial(half_kernel, steps), grid_spec=pltpu.Pre...  7.85 us
  transfers between devices with their start and end apart: 18, of which 11 were waited for; matrix products, arithmetic and copies ran while one was open for 3% of the time, Pallas kernels for 49%

profile of v1, /device:TPU:0, one launch (start us, length us, event | category | flops | bytes accessed | tf_op | source)
XLA Modules:
  0.0 138.8 jit_solution(16339149943228251561)
XLA Ops:
  0.0 5.0 %collective-permute-start.4 = (bf16[768,1024]{1,0:T(8,128)(2,1)}, bf16[768,1024]{1,0:T(8,128)(2,1)}, u32[]{:S(2)}, u32[]{:S(2)}) collective-permute-start(bf16[768,1024]{1,0:T(8,128)(2,1)} %xs.1), channel_id=1, source_target_pairs={{0,12},{1,13},{2,6},{3,7},{4,0},{5,1},{6,10},{7,11},{8,4},{9,5},{1... | collective-permute-start | bytes 4718600 | tf_op jit(solution)/shard_map/ppermute | solution.py:57
  7.7 6.7 %cut.2 = (bf16[784,896]{1,0:T(8,128)(2,1)}, bf16[784,896]{1,0:T(8,128)(2,1)}, bf16[768,384]{1,0:T(8,128)(2,1)}, bf16[768,384]{1,0:T(8,128)(2,1)}) custom-call(s32[2]{0:T(128)} %pad_add_fusion.places, bf16[16,128]{1,0:T(8,128)(2,1)} %broadcast_in_dim.2.info.own_info, bf16[768,5120]{1,0:T(8,128)(2,1)} %refs_0_.3, bf16[768,5120]{1,0:T(8,128)(2,1)} %refs_0_.3), custom_call_target="tpu_custom_call" | custom-call | flops 1 | bytes 1 | tf_op jit(solution)/shard_map/cut/pallas_call | solution.py:97
  14.4 1.7 %collective-permute-start.6 = (bf16[784,896]{1,0:T(8,128)(2,1)}, bf16[784,896]{1,0:T(8,128)(2,1)}, u32[]{:S(2)}, u32[]{:S(2)}) collective-permute-start(bf16[784,896]{1,0:T(8,128)(2,1)} %get-tuple-element.50), channel_id=1, source_target_pairs={{0,12},{1,13},{2,6},{3,7},{4,0},{5,1},{6,10},{7,11},{8,4},{9,5},{1... | collective-permute-start | bytes 4214792 | tf_op jit(solution)/shard_map/ppermute | solution.py:57
  17.1 6.8 %cut.3 = (bf16[784,896]{1,0:T(8,128)(2,1)}, bf16[784,896]{1,0:T(8,128)(2,1)}, bf16[768,384]{1,0:T(8,128)(2,1)}, bf16[768,384]{1,0:T(8,128)(2,1)}) custom-call(s32[2]{0:T(128)} %pad_add_fusion.1.places, bf16[16,128]{1,0:T(8,128)(2,1)} %broadcast_in_dim.2.info.own_info, bf16[768,5120]{1,0:T(8,128)(2,1)} %refs_0_.3, bf16[768,5120]{1,0:T(8,128)(2,1)} %refs_0_.3), custom_call_target="tpu_custom_call" | custom-call | flops 1 | bytes 1 | tf_op jit(solution)/shard_map/cut/pallas_call | solution.py:97
  23.9 7.8 %half.1 = bf16[784,3584]{1,0:T(8,128)(2,1)} custom-call(s32[1]{0:T(128)} %bitcast.6.place, bf16[16,128]{1,0:T(8,128)(2,1)} %broadcast_in_dim.2.info.own_info, bf16[768,5120]{1,0:T(8,128)(2,1)} %refs_0_.3, bf16[768,1024]{1,0:T(8,128)(2,1)} %xs.1), custom_call_target="tpu_custom_call" | custom-call | flops 1 | bytes 1 | tf_op jit(solution)/shard_map/half/pallas_call | solution.py:132
  31.8 9.6 %conditional.2 = (bf16[784,3584]{1,0:T(8,128)(2,1)}) conditional(s32[]{:T(128)} %bitcast.5, () %tuple.26, bf16[784,3584]{1,0:T(8,128)(2,1)} %half.1), branch_computations={%region_0.1_spmd, %region_1.2_spmd} | conditional | bytes 22478896 | solution.py:506
  31.9 9.5 %collective-permute-done = bf16[784,3584]{1,0:T(8,128)(2,1)} collective-permute-done((bf16[784,3584]{1,0:T(8,128)(2,1)}, bf16[784,3584]{1,0:T(8,128)(2,1)}, u32[]{:S(2)}, u32[]{:S(2)}) %collective-permute-start) | collective-permute-done | bytes 5619744 | tf_op jit(solution)/shard_map/cond/branch_1_fun/ppermute | solution.py:57
  41.4 3.6 %collective-permute-start.8 = (bf16[784,896]{1,0:T(8,128)(2,1)}, bf16[784,896]{1,0:T(8,128)(2,1)}, u32[]{:S(2)}, u32[]{:S(2)}) collective-permute-start(bf16[784,896]{1,0:T(8,128)(2,1)} %get-tuple-element.62), channel_id=1, source_target_pairs={{0,13},{1,12},{2,7},{3,6},{4,1},{5,0},{6,11},{7,10},{8,5},{9,4},{1... | collective-permute-start | bytes 4214792 | tf_op jit(solution)/shard_map/ppermute | solution.py:57
  45.0 6.0 %conditional.3 = (bf16[768,1024]{1,0:T(8,128)(2,1)}, bf16[768,1024]{1,0:T(8,128)(2,1)}) conditional(s32[]{:T(128)} %bitcast.5, () %tuple.28, (bf16[768,1024]{1,0:T(8,128)(2,1)}, bf16[768,1024]{1,0:T(8,128)(2,1)}) %tuple.29), branch_computations={%region_2.3_spmd, %region_3.4_spmd} | conditional | bytes 12583008 | solution.py:506
  45.5 3.2 %collective-permute-done.1 = bf16[768,1024]{1,0:T(8,128)(2,1)} collective-permute-done((bf16[768,1024]{1,0:T(8,128)(2,1)}, bf16[768,1024]{1,0:T(8,128)(2,1)}, u32[]{:S(2)}, u32[]{:S(2)}) %collective-permute-start.1) | collective-permute-done | bytes 1572896 | tf_op jit(solution)/shard_map/cond/branch_1_fun/ppermute | solution.py:57
  48.7 2.2 %collective-permute-done.2 = bf16[768,1024]{1,0:T(8,128)(2,1)} collective-permute-done((bf16[768,1024]{1,0:T(8,128)(2,1)}, bf16[768,1024]{1,0:T(8,128)(2,1)}, u32[]{:S(2)}, u32[]{:S(2)}) %collective-permute-start.2) | collective-permute-done | bytes 1572896 | tf_op jit(solution)/shard_map/cond/branch_1_fun/ppermute | solution.py:57
  51.0 2.0 %collective-permute-start.9 = (bf16[768,384]{1,0:T(8,128)(2,1)}, bf16[768,384]{1,0:T(8,128)(2,1)S(1)}, u32[]{:S(2)}, u32[]{:S(2)}) collective-permute-start(bf16[768,384]{1,0:T(8,128)(2,1)} %get-tuple-element.65), channel_id=1, source_target_pairs={{0,2},{1,3},{2,0},{3,1},{4,6},{5,7},{6,4},{7,5},{8,10},{9,11},{10,... | collective-permute-start | bytes 1769480 | tf_op jit(solution)/shard_map/ppermute | solution.py:57
  53.6 18.5 %grams.1.gram.refs_6_ = f32[7,768,768]{2,1,0:T(8,128)} custom-call(s32[14]{0:T(128)} %stack.47.table, bf16[768,1024]{1,0:T(8,128)(2,1)} %xs.1, bf16[784,3584]{1,0:T(8,128)(2,1)} %get-tuple-element.79.xc.x_half.refs_1_, bf16[768,1024]{1,0:T(8,128)(2,1)} %collective-permute-done.3.ys, bf16[768,1024]{1,0:T(8,128)(2,1)} %get-tuple-element.55.yc, ...), custom_call_target="tpu_custom_call" | custom-call | flops 1 | bytes 1 | tf_op jit(solution)/shard_map/grams/pallas_call | solution.py:182
  72.8 14.7 %same_one.1 = (f32[6,48,128]{2,1,0:T(8,128)}, bf16[6,16,128]{2,1,0:T(8,128)(2,1)}) custom-call(bf16[16,128]{1,0:T(8,128)(2,1)} %broadcast_in_dim.2.info.own_info, bf16[768,5120]{1,0:T(8,128)(2,1)} %refs_0_.3, bf16[784,3584]{1,0:T(8,128)(2,1)} %get-tuple-element.79.xc.x_half.refs_1_, bf16[784,896]{1,0:T(8,128)(2,1)} %collective-permute-done.5.ys.refs_2_, ...), custom_call_target="tpu_custom_call" | custom-call | flops 1 | bytes 1 | tf_op jit(solution)/shard_map/same_one/pallas_call | solution.py:531
  87.5 1.8 %collective-permute-start.10 = (bf16[768,384]{1,0:T(8,128)(2,1)}, bf16[768,384]{1,0:T(8,128)(2,1)S(1)}, u32[]{:S(2)}, u32[]{:S(2)}) collective-permute-start(bf16[768,384]{1,0:T(8,128)(2,1)} %get-tuple-element.66), channel_id=1, source_target_pairs={{0,12},{1,13},{2,6},{3,7},{4,0},{5,1},{6,10},{7,11},{8,4},{9,5},{1... | collective-permute-start | bytes 1769480 | tf_op jit(solution)/shard_map/ppermute | solution.py:57
  89.3 11.1 %collective-permute-done.8.refs_5_ = bf16[784,896]{1,0:T(8,128)(2,1)} collective-permute-done((bf16[784,896]{1,0:T(8,128)(2,1)}, bf16[784,896]{1,0:T(8,128)(2,1)}, u32[]{:S(2)}, u32[]{:S(2)}) %collective-permute-start.8) | collective-permute-done | bytes 1404960 | tf_op jit(solution)/shard_map/ppermute | solution.py:57
  100.4 1.6 %collective-permute-start.11 = (bf16[768,384]{1,0:T(8,128)(2,1)}, bf16[768,384]{1,0:T(8,128)(2,1)S(1)}, u32[]{:S(2)}, u32[]{:S(2)}) collective-permute-start(bf16[768,384]{1,0:T(8,128)(2,1)} %get-tuple-element.67), channel_id=1, source_target_pairs={{0,3},{1,2},{2,1},{3,0},{4,7},{5,6},{6,5},{7,4},{8,11},{9,10},{10,... | collective-permute-start | bytes 1769480 | tf_op jit(solution)/shard_map/ppermute | solution.py:57
  104.1 8.5 %cross_one.1 = (f32[6,48,128]{2,1,0:T(8,128)S(1)}, bf16[6,16,128]{2,1,0:T(8,128)(2,1)S(1)}) custom-call(bf16[6,16,128]{2,1,0:T(8,128)(2,1)S(1)} %copy-done.1, f32[6,48,128]{2,1,0:T(8,128)S(1)} %copy-done, bf16[768,5120]{1,0:T(8,128)(2,1)} %refs_0_.3, bf16[784,3584]{1,0:T(8,128)(2,1)} %get-tuple-element.79.xc.x_half.refs_1_, ...), custom_call_target="tpu_custom_call" | custom-call | flops 1 | bytes 1 | tf_op jit(solution)/shard_map/cross_one/pallas_call | solution.py:531
  112.6 2.9 %collective-permute-done.9.ys.refs_2_ = bf16[768,384]{1,0:T(8,128)(2,1)S(1)} collective-permute-done((bf16[768,384]{1,0:T(8,128)(2,1)}, bf16[768,384]{1,0:T(8,128)(2,1)S(1)}, u32[]{:S(2)}, u32[]{:S(2)}) %collective-permute-start.9) | collective-permute-done | bytes 589856 | tf_op jit(solution)/shard_map/ppermute | solution.py:57
  115.5 5.5 %same_two.1.earlier = f32[6,48,128]{2,1,0:T(8,128)S(1)} custom-call(bf16[6,16,128]{2,1,0:T(8,128)(2,1)S(1)} %get-tuple-element.63.notes, f32[6,48,128]{2,1,0:T(8,128)S(1)} %get-tuple-element.64.earlier, bf16[768,5120]{1,0:T(8,128)(2,1)S(1)} %bitcast.16, bf16[784,3584]{1,0:T(8,128)(2,1)} %get-tuple-element.79.xc.x_half.refs_1_, ...), custom_call_target="tpu_custom_call" | custom-call | flops 1 | bytes 1 | tf_op jit(solution)/shard_map/same_two/pallas_call | solution.py:531
  120.9 3.6 %collective-permute-done.12.refs_5_ = bf16[768,384]{1,0:T(8,128)(2,1)S(1)} collective-permute-done((bf16[768,384]{1,0:T(8,128)(2,1)}, bf16[768,384]{1,0:T(8,128)(2,1)S(1)}, u32[]{:S(2)}, u32[]{:S(2)}) %collective-permute-start.12) | collective-permute-done | bytes 589856 | tf_op jit(solution)/shard_map/ppermute | solution.py:57
  125.1 5.6 %cross_two.1 = (f32[48,96]{1,0:T(8,128)S(1)}, f32[48,96]{1,0:T(8,128)S(1)}, f32[48,96]{1,0:T(8,128)S(1)}, f32[48,96]{1,0:T(8,128)S(1)}, f32[48,96]{1,0:T(8,128)S(1)}, /*index=5*/f32[48,96]{1,0:T(8,128)S(1)}) custom-call(bf16[6,16,128]{2,1,0:T(8,128)(2,1)S(1)} %get-tuple-element.63.notes, f32[6,48,128]{2,1,0:T(8,128)S(1)} %same_two.1.earlier, ...), custom_call_target="tpu_custom_call" | custom-call | flops 1 | bytes 1 | tf_op jit(solution)/shard_map/cross_two/pallas_call | solution.py:531
  130.9 2.3 %collective-permute-start.14 = (f32[48,96]{1,0:T(8,128)S(1)}, f32[48,96]{1,0:T(8,128)S(1)}, u32[]{:S(2)}, u32[]{:S(2)}) collective-permute-start(f32[48,96]{1,0:T(8,128)S(1)} %get-tuple-element.71), channel_id=1, source_target_pairs={{0,5},{1,4},{2,15},{3,14},{4,9},{5,8},{6,3},{7,2},{8,13},{9,12},{1... | collective-permute-start | bytes 55304 | tf_op jit(solution)/shard_map/ppermute | solution.py:57
  133.2 1.7 %collective-permute-start.15 = (f32[48,96]{1,0:T(8,128)S(1)}, f32[48,96]{1,0:T(8,128)S(1)}, u32[]{:S(2)}, u32[]{:S(2)}) collective-permute-start(f32[48,96]{1,0:T(8,128)S(1)} %get-tuple-element.72), channel_id=1, source_target_pairs={{0,2},{1,3},{2,0},{3,1},{4,6},{5,7},{6,4},{7,5},{8,10},{9,11},{10,... | collective-permute-start | bytes 55304 | tf_op jit(solution)/shard_map/ppermute | solution.py:57
  (44 shorter events, 12.2 us)
Async XLA Ops:
  0.0 45.0 %collective-permute-start.4 = (bf16[768,1024]{1,0:T(8,128)(2,1)}, bf16[768,1024]{1,0:T(8,128)(2,1)}, u32[]{:S(2)}, u32[]{:S(2)}) collective-permute-start(bf16[768,1024]{1,0:T(8,128)(2,1)} %xs.1), channel_id=1, source_target_pairs={{0,12},{1,13},{2,6},{3,7},{4,0},{5,1},{6,10},{7,11},{8,4},{9,5},{1... | collective-permute-start | bytes 4718600 | tf_op jit(solution)/shard_map/ppermute | solution.py:57
  5.0 39.9 %collective-permute-start.3 = (bf16[768,1024]{1,0:T(8,128)(2,1)}, bf16[768,1024]{1,0:T(8,128)(2,1)}, u32[]{:S(2)}, u32[]{:S(2)}) collective-permute-start(bf16[768,1024]{1,0:T(8,128)(2,1)} %xs.1), channel_id=1, source_target_pairs={{0,2},{1,3},{2,0},{3,1},{4,6},{5,7},{6,4},{7,5},{8,10},{9,11},{10,... | collective-permute-start | bytes 4718600 | tf_op jit(solution)/shard_map/ppermute | solution.py:57
  14.4 57.6 %collective-permute-start.6 = (bf16[784,896]{1,0:T(8,128)(2,1)}, bf16[784,896]{1,0:T(8,128)(2,1)}, u32[]{:S(2)}, u32[]{:S(2)}) collective-permute-start(bf16[784,896]{1,0:T(8,128)(2,1)} %get-tuple-element.50), channel_id=1, source_target_pairs={{0,12},{1,13},{2,6},{3,7},{4,0},{5,1},{6,10},{7,11},{8,4},{9,5},{1... | collective-permute-start | bytes 4214792 | tf_op jit(solution)/shard_map/ppermute | solution.py:57
  16.2 56.6 %collective-permute-start.5 = (bf16[784,896]{1,0:T(8,128)(2,1)}, bf16[784,896]{1,0:T(8,128)(2,1)}, u32[]{:S(2)}, u32[]{:S(2)}) collective-permute-start(bf16[784,896]{1,0:T(8,128)(2,1)} %get-tuple-element.45), channel_id=1, source_target_pairs={{0,2},{1,3},{2,0},{3,1},{4,6},{5,7},{6,4},{7,5},{8,10},{9,11},{10,... | collective-permute-start | bytes 4214792 | tf_op jit(solution)/shard_map/ppermute | solution.py:57
  23.9 7.9 %copy-start.2 = (s32[1,2]{1,0:T(1,128)S(1)}, s32[1,2]{1,0:T(1,128)}, u32[]{:S(2)}) copy-start(s32[1,2]{1,0:T(1,128)} %param.11) | copy-start | bytes 28
  31.8 9.6 %collective-permute-start = (bf16[784,3584]{1,0:T(8,128)(2,1)}, bf16[784,3584]{1,0:T(8,128)(2,1)}, u32[]{:S(2)}, u32[]{:S(2)}) collective-permute-start(bf16[784,3584]{1,0:T(8,128)(2,1)} %param.1), channel_id=1, source_target_pairs={{0,1},{1,0},{2,3},{3,2},{4,5},{5,4},{6,7},{7,6},{8,9},{9,8},{10,11... | collective-permute-start | bytes 16859144 | tf_op jit(solution)/shard_map/cond/branch_1_fun/ppermute | solution.py:57
  41.4 59.0 %collective-permute-start.8 = (bf16[784,896]{1,0:T(8,128)(2,1)}, bf16[784,896]{1,0:T(8,128)(2,1)}, u32[]{:S(2)}, u32[]{:S(2)}) collective-permute-start(bf16[784,896]{1,0:T(8,128)(2,1)} %get-tuple-element.62), channel_id=1, source_target_pairs={{0,13},{1,12},{2,7},{3,6},{4,1},{5,0},{6,11},{7,10},{8,5},{9,4},{1... | collective-permute-start | bytes 4214792 | tf_op jit(solution)/shard_map/ppermute | solution.py:57
  45.0 3.8 %collective-permute-start.1 = (bf16[768,1024]{1,0:T(8,128)(2,1)}, bf16[768,1024]{1,0:T(8,128)(2,1)}, u32[]{:S(2)}, u32[]{:S(2)}) collective-permute-start(bf16[768,1024]{1,0:T(8,128)(2,1)} %get-tuple-element.13), channel_id=1, source_target_pairs={{0,1},{1,0},{2,3},{3,2},{4,5},{5,4},{6,7},{7,6},{8,9},{9,8},{10,11... | collective-permute-start | bytes 4718600 | tf_op jit(solution)/shard_map/cond/branch_1_fun/ppermute | solution.py:57
  45.3 5.6 %collective-permute-start.2 = (bf16[768,1024]{1,0:T(8,128)(2,1)}, bf16[768,1024]{1,0:T(8,128)(2,1)}, u32[]{:S(2)}, u32[]{:S(2)}) collective-permute-start(bf16[768,1024]{1,0:T(8,128)(2,1)} %get-tuple-element.14), channel_id=1, source_target_pairs={{0,1},{1,0},{2,3},{3,2},{4,5},{5,4},{6,7},{7,6},{8,9},{9,8},{10,11... | collective-permute-start | bytes 4718600 | tf_op jit(solution)/shard_map/cond/branch_1_fun/ppermute | solution.py:57
  51.0 51.0 %collective-permute-start.7 = (bf16[784,896]{1,0:T(8,128)(2,1)}, bf16[784,896]{1,0:T(8,128)(2,1)}, u32[]{:S(2)}, u32[]{:S(2)}) collective-permute-start(bf16[784,896]{1,0:T(8,128)(2,1)} %get-tuple-element.47), channel_id=1, source_target_pairs={{0,3},{1,2},{2,1},{3,0},{4,7},{5,6},{6,5},{7,4},{8,11},{9,10},{10,... | collective-permute-start | bytes 4214792 | tf_op jit(solution)/shard_map/ppermute | solution.py:57
  51.0 64.5 %collective-permute-start.9 = (bf16[768,384]{1,0:T(8,128)(2,1)}, bf16[768,384]{1,0:T(8,128)(2,1)S(1)}, u32[]{:S(2)}, u32[]{:S(2)}) collective-permute-start(bf16[768,384]{1,0:T(8,128)(2,1)} %get-tuple-element.65), channel_id=1, source_target_pairs={{0,2},{1,3},{2,0},{3,1},{4,6},{5,7},{6,4},{7,5},{8,10},{9,11},{10,... | collective-permute-start | bytes 1769480 | tf_op jit(solution)/shard_map/ppermute | solution.py:57
  87.5 28.0 %collective-permute-start.10 = (bf16[768,384]{1,0:T(8,128)(2,1)}, bf16[768,384]{1,0:T(8,128)(2,1)S(1)}, u32[]{:S(2)}, u32[]{:S(2)}) collective-permute-start(bf16[768,384]{1,0:T(8,128)(2,1)} %get-tuple-element.66), channel_id=1, source_target_pairs={{0,12},{1,13},{2,6},{3,7},{4,0},{5,1},{6,10},{7,11},{8,4},{9,5},{1... | collective-permute-start | bytes 1769480 | tf_op jit(solution)/shard_map/ppermute | solution.py:57
  89.3 35.2 %collective-permute-start.12 = (bf16[768,384]{1,0:T(8,128)(2,1)}, bf16[768,384]{1,0:T(8,128)(2,1)S(1)}, u32[]{:S(2)}, u32[]{:S(2)}) collective-permute-start(bf16[768,384]{1,0:T(8,128)(2,1)} %get-tuple-element.68), channel_id=1, source_target_pairs={{0,13},{1,12},{2,7},{3,6},{4,1},{5,0},{6,11},{7,10},{8,5},{9,4},{1... | collective-permute-start | bytes 1769480 | tf_op jit(solution)/shard_map/ppermute | solution.py:57
  100.4 24.8 %collective-permute-start.11 = (bf16[768,384]{1,0:T(8,128)(2,1)}, bf16[768,384]{1,0:T(8,128)(2,1)S(1)}, u32[]{:S(2)}, u32[]{:S(2)}) collective-permute-start(bf16[768,384]{1,0:T(8,128)(2,1)} %get-tuple-element.67), channel_id=1, source_target_pairs={{0,3},{1,2},{2,1},{3,0},{4,7},{5,6},{6,5},{7,4},{8,11},{9,10},{10,... | collective-permute-start | bytes 1769480 | tf_op jit(solution)/shard_map/ppermute | solution.py:57
  102.0 13.4 %slice-start = ((s8[7864320]{0:T(1024)(128)(4,1)}), s8[4194304]{0:T(1024)(128)(4,1)S(1)}, s32[]{:S(2)}) async-start(s8[7864320]{0:T(1024)(128)(4,1)} %bitcast.15), calls=%async_computation | async-start | bytes 8388608
  102.0 1.1 copy-start
  103.1 1.0 copy-start.1
  104.1 11.4 %slice-start.1 = ((s8[7864320]{0:T(1024)(128)(4,1)}), s8[3670016]{0:T(1024)(128)(4,1)S(1)}, s32[]{:S(2)}) async-start(s8[7864320]{0:T(1024)(128)(4,1)} %bitcast.15), calls=%async_computation.1 | async-start | bytes 7340032
  130.7 5.7 %collective-permute-start.13 = (f32[48,96]{1,0:T(8,128)S(1)}, f32[48,96]{1,0:T(8,128)S(1)}, u32[]{:S(2)}, u32[]{:S(2)}) collective-permute-start(f32[48,96]{1,0:T(8,128)S(1)} %get-tuple-element.70), channel_id=1, source_target_pairs={{0,4},{1,5},{2,14},{3,15},{4,8},{5,9},{6,2},{7,3},{8,12},{9,13},{1... | collective-permute-start | bytes 55304 | tf_op jit(solution)/shard_map/ppermute | solution.py:57
  130.9 7.0 %collective-permute-start.14 = (f32[48,96]{1,0:T(8,128)S(1)}, f32[48,96]{1,0:T(8,128)S(1)}, u32[]{:S(2)}, u32[]{:S(2)}) collective-permute-start(f32[48,96]{1,0:T(8,128)S(1)} %get-tuple-element.71), channel_id=1, source_target_pairs={{0,5},{1,4},{2,15},{3,14},{4,9},{5,8},{6,3},{7,2},{8,13},{9,12},{1... | collective-permute-start | bytes 55304 | tf_op jit(solution)/shard_map/ppermute | solution.py:57
  133.2 4.7 %collective-permute-start.15 = (f32[48,96]{1,0:T(8,128)S(1)}, f32[48,96]{1,0:T(8,128)S(1)}, u32[]{:S(2)}, u32[]{:S(2)}) collective-permute-start(f32[48,96]{1,0:T(8,128)S(1)} %get-tuple-element.72), channel_id=1, source_target_pairs={{0,2},{1,3},{2,0},{3,1},{4,6},{5,7},{6,4},{7,5},{8,10},{9,11},{10,... | collective-permute-start | bytes 55304 | tf_op jit(solution)/shard_map/ppermute | solution.py:57
  134.9 3.3 %collective-permute-start.16 = (f32[48,96]{1,0:T(8,128)S(1)}, f32[48,96]{1,0:T(8,128)S(1)}, u32[]{:S(2)}, u32[]{:S(2)}) collective-permute-start(f32[48,96]{1,0:T(8,128)S(1)} %get-tuple-element.73), channel_id=1, source_target_pairs={{0,3},{1,2},{2,1},{3,0},{4,7},{5,6},{6,5},{7,4},{8,11},{9,10},{10,... | collective-permute-start | bytes 55304 | tf_op jit(solution)/shard_map/ppermute | solution.py:57
  135.0 3.2 %collective-permute-start.17 = (f32[48,96]{1,0:T(8,128)S(1)}, f32[48,96]{1,0:T(8,128)S(1)}, u32[]{:S(2)}, u32[]{:S(2)}) collective-permute-start(f32[48,96]{1,0:T(8,128)S(1)} %get-tuple-element.74), channel_id=1, source_target_pairs={{0,1},{1,0},{2,3},{3,2},{4,5},{5,4},{6,7},{7,6},{8,9},{9,8},{10,11... | collective-permute-start | bytes 55304 | tf_op jit(solution)/shard_map/ppermute | solution.py:57

commit v2 on v1

--- a/solution.py
+++ b/solution.py
@@ -13,7 +13,7 @@
 DOMAINS = 48
 LANES = 128
 VMEM_BYTES = 63 * 1024 * 1024
-LAST_VMEM_BYTES = 44 * 1024 * 1024
+LAST_VMEM_BYTES = 30 * 1024 * 1024
 
 INFO = 16
 
@@ -23,8 +23,9 @@
     (YC, XC, 1), (YC, ZC, 1), (YC, ZS, 0), (YS, ZC, 0), (YC, XS, 0),
 )
 ONLY = {2: 0, 6: 0, 7: 1, 8: 1}
-SLOT = (0, 1, 2, 3, 4, 5, 6, 6, 2)
+SLOT = (0, 1, 6, 2, 3, 4, 5, 5, 6)
 SLOTS = 7
+SAME_SLOTS = 3
 FIRST = (0, 1, 2, 3)
 SMALL = pl.CostEstimate(flops=1, bytes_accessed=1, transcendentals=0)
 NT = (((1,), (1,)), ((), ()))
@@ -148,7 +149,7 @@
     )(place, info, acts, grads)
 
 
-def grams_kernel(table, xs, xc, ys, yc, zs, zc, out, held, result, in_sems, out_sems):
+def grams_kernel(table, xs, xc, ys, yc, zs, zc, same, cross, held, result, in_sems, out_sems):
     rows, depth = xs.shape
     order = token_major(rows)
     sources = (xs, xc.at[:rows, xc.shape[1] - depth:], ys, yc, zs, zc)
@@ -163,18 +164,26 @@
     for block in (YS, YC):
         held[block] = reorder(order, held[block])
 
-    def leave(slot):
-        return pltpu.make_async_copy(result.at[slot], out.at[slot], out_sems.at[slot])
+    def leave(slot, array, at):
+        return pltpu.make_async_copy(result.at[slot], array.at[at], out_sems.at[slot])
 
     @pl.loop(0, SLOTS)
     def _(slot):
         result[slot] = lax.dot_general(
             held[table[slot]], held[table[SLOTS + slot]], NT, preferred_element_type=jnp.float32
         )
-        leave(slot).start()
+
+        @pl.when(slot < SAME_SLOTS)
+        def _():
+            leave(slot, same, slot).start()
+
+        @pl.when(slot >= SAME_SLOTS)
+        def _():
+            leave(slot, cross, slot - SAME_SLOTS).start()
 
     for slot in range(SLOTS):
-        leave(slot).wait()
+        array, at = (same, slot) if slot < SAME_SLOTS else (cross, slot - SAME_SLOTS)
+        leave(slot, array, at).wait()
 
 
 def grams(table, grads, *messages):
@@ -182,8 +191,11 @@
     return pl.pallas_call(
         grams_kernel,
         in_specs=[pl.BlockSpec(memory_space=pltpu.SMEM)] + [pl.BlockSpec(memory_space=pl.ANY)] * 6,
-        out_specs=pl.BlockSpec(memory_space=pl.ANY),
-        out_shape=jax.ShapeDtypeStruct((SLOTS, rows, rows), jnp.float32),
+        out_specs=[pl.BlockSpec(memory_space=pl.ANY)] * 2,
+        out_shape=[
+            jax.ShapeDtypeStruct((count, rows, rows), jnp.float32)
+            for count in (SAME_SLOTS, SLOTS - SAME_SLOTS)
+        ],
         scratch_shapes=[
             pltpu.VMEM((6, rows, width), grads.dtype),
             pltpu.VMEM((SLOTS, rows, rows), jnp.float32),
@@ -311,7 +323,7 @@
     return ref.at[:, pl.ds(pl.multiple_of(at, LANES), width)]
 
 
-def same_one_kernel(factor, own_info, acts, x_half, ys, zs, gram, out, notes,
+def same_one_kernel(factor, xs, acts, x_half, ys, zs, gram, cross_gram, out, notes,
                     held, own_v, half_v, gram_v, inner, sums, sems):
     rows, width = inner.shape[1], held.shape[2]
     quarter = acts.shape[1] // 4
@@ -320,20 +332,19 @@
     in_half = (1 - side) * quarter
     half_at = core * 2 * quarter
     copies = copies_of({
-        XS: (columns(acts, half_at + in_half, width), held.at[XS, :rows]),
+        XS: (xs, held.at[XS]),
         XC: (columns(x_half, in_half, width), held.at[XC]),
         YS: (ys, held.at[YS]),
         ZS: (zs, held.at[ZS]),
         "g0": (gram.at[0], gram_v.at[0]),
         "g1": (gram.at[1], gram_v.at[1]),
-        "g2": (gram.at[2], gram_v.at[2]),
+        "g2": (cross_gram.at[3], gram_v.at[2]),
         "own": (columns(acts, half_at, 2 * quarter), own_v),
         "half": (x_half.at[:, :2 * quarter], half_v),
-        "g3": (gram.at[3], gram_v.at[3]),
-        "info": (own_info, held.at[XS, rows:, :LANES]),
+        "g3": (gram.at[2], gram_v.at[3]),
     }, sems)
-    start(copies, YS, XS, "info", ZS, "g0", XC, "g1", "g2", "own", "half", "g3")
-    wait(copies, YS, XS, "info")
+    start(copies, YS, XS, ZS, "g0", XC, "g1", "g2", "own", "half", "g3")
+    wait(copies, YS, XS)
     product(held.at[YS], held.at[XS], inner.at[0])
     wait(copies, "g0", ZS)
     product(held.at[YS], held.at[ZS], inner.at[1])
@@ -356,21 +367,20 @@
         out[block] = value
 
 
-def same_two_kernel(factor, at, notes, earlier, acts, x_half, ys, zs, gram, out,
+def same_two_kernel(factor, quarter, at, notes, earlier, xs, x_half, ys, zs, gram, cross_gram, out,
                     held, notes_v, earlier_v, gram_v, inner, sums, sems):
     rows, width = inner.shape[1], held.shape[2]
-    quarter = acts.shape[1] // 4
     core, side = position()
     mirrored = core ^ side
     in_half = (1 - side) * quarter
     copies = copies_of({
-        XS: (columns(acts, core * 2 * quarter + in_half + at, width), held.at[XS, :rows]),
+        XS: (xs, held.at[XS, :rows]),
         XC: (columns(x_half, in_half + at, width), held.at[XC]),
         YS: (ys, held.at[YS, :rows]),
         ZS: (zs, held.at[ZS, :rows]),
         "g0": (gram.at[0], gram_v.at[0]),
         "g1": (gram.at[1], gram_v.at[1]),
-        "g2": (gram.at[2], gram_v.at[2]),
+        "g2": (cross_gram.at[3], gram_v.at[2]),
         "notes": (notes, notes_v),
         "earlier": (earlier, earlier_v),
     }, sems)
@@ -397,43 +407,58 @@
     return me & 1, lax.shift_right_logical(me, 1) & 1
 
 
-def cross_kernel(factor, at, notes, earlier, *refs):
-    (acts, x_half, ys, yc, zs, zc, gram), refs = refs[:7], refs[7:]
+def cross_kernel(factor, quarter, at, notes, earlier, *refs):
+    (xs, x_half, ys, yc, zs, zc, gram), refs = refs[:7], refs[7:]
     outs, (held, notes_v, earlier_v, gram_v, inner, sums, sems) = refs[:-7], refs[-7:]
     rows, width = inner.shape[1], held.shape[2]
-    quarter = acts.shape[1] // 4
     core, side = position()
     mirrored = core ^ side
     in_half = (1 - side) * quarter
-    work_at = core * 2 * quarter + in_half
     copies = copies_of({
-        XS: (columns(acts, work_at + at, width), held.at[XS, :rows, :]),
+        XS: (xs, held.at[XS, :xs.shape[0]]),
         XC: (columns(x_half, in_half + at, width), held.at[XC]),
         YS: (ys, held.at[YS, :ys.shape[0]]),
         YC: (yc, held.at[YC, :yc.shape[0]]),
         ZS: (zs, held.at[ZS, :zs.shape[0]]),
         ZC: (zc, held.at[ZC, :zc.shape[0]]),
-        "g4": (gram.at[4], gram_v.at[0]),
-        "g5": (gram.at[5], gram_v.at[1]),
-        "g6": (gram.at[6], gram_v.at[2]),
-        "g2": (gram.at[2], gram_v.at[3]),
+        "g4": (gram.at[0], gram_v.at[0]),
+        "g5": (gram.at[1], gram_v.at[1]),
+        "g6": (gram.at[2], gram_v.at[2]),
+        "g2": (gram.at[3], gram_v.at[3]),
         "notes": (notes, notes_v),
         "earlier": (earlier, earlier_v),
     }, sems)
-    start(copies, YC, XC, ZC, "g4", YS, ZS, "g5", XS, "g6", "g2", "notes", "earlier")
+
+    def on_one(act, key):
+        pl.when(mirrored == 1)(lambda: act(copies, key))
+
+    def on_zero(act, key):
+        pl.when(mirrored == 0)(lambda: act(copies, key))
+
+    start(copies, YC, XC, ZC, "g4")
+    on_one(start, YS)
+    on_zero(start, ZS)
+    start(copies, "g5")
+    on_one(start, XS)
+    start(copies, "g6")
+    on_one(start, "g2")
+    start(copies, "notes", "earlier")
     wait(copies, YC, XC)
     product(held.at[YC], held.at[XC], inner.at[0])
     wait(copies, ZC)
     product(held.at[YC], held.at[ZC], inner.at[1])
-    wait(copies, "g4", YS, ZS)
+    wait(copies, "g4")
+    on_one(wait, YS)
+    on_zero(wait, ZS)
     token_sums(inner.at[0], gram_v.at[0], sums.at[0])
     product(held.at[jnp.where(mirrored == 0, YC, YS)], held.at[jnp.where(mirrored == 0, ZS, ZC)], inner.at[0])
-    wait(copies, "g5", XS)
+    wait(copies, "g5")
     token_sums(inner.at[1], gram_v.at[1], sums.at[1])
-    wait(copies, "g6", "g2", "notes", "earlier")
+    wait(copies, "g6", "notes", "earlier")
 
     @pl.when(mirrored == 1)
     def _():
+        wait(copies, XS, "g2")
         product(held.at[YC], held.at[XS], inner.at[1])
         token_sums(inner.at[0], gram_v.at[2], sums.at[2])
         token_sums(inner.at[1], gram_v.at[3], sums.at[3])
@@ -515,7 +540,7 @@
     grads_yc, grads_zc = exchange(grads_ys, grads_zs)
     factor = 1.0 / (TOK * math.sqrt(width * grads.shape[1]))
 
-    gram = grams(table, grads, x_half, grads_ys, grads_yc, grads_zs, grads_zc)
+    gram, cross_gram = grams(table, grads, x_half, grads_ys, grads_yc, grads_zs, grads_zc)
     cut_zs_two, cut_yc_two, gram = lax.optimization_barrier((cut_zs_two, cut_yc_two, gram))
     zs_two = send(cut_zs_two, along, 0)
     yc_two = send(cut_yc_two, across, 1)
@@ -552,22 +577,22 @@
     partial = functools.partial
     sums, notes = call(
         partial(same_one_kernel, factor), "same_one", VMEM_BYTES, one, extra,
-        (own_info, acts, x_half, ys_one, zs_one, gram), [all_sums, all_notes],
+        (cut_zs, acts, x_half, ys_one, zs_one, gram, cross_gram), [all_sums, all_notes],
     )
     cut_zc_two, sums = lax.optimization_barrier((cut_zc_two, sums))
     zc_two = send(cut_zc_two, along, 1)
     extra = [notes_v, sums_v]
     sums, notes = call(
-        partial(cross_kernel, factor, 0), "cross_one", LAST_VMEM_BYTES, one, extra,
-        (notes, sums, acts, x_half, ys_one, yc_one, zs_one, zc_one, gram), [all_sums, all_notes],
+        partial(cross_kernel, factor, quarter, 0), "cross_one", LAST_VMEM_BYTES, one, extra,
+        (notes, sums, cut_zs, x_half, ys_one, yc_one, zs_one, zc_one, cross_gram), [all_sums, all_notes],
     )
     sums, = call(
-        partial(same_two_kernel, factor, one), "same_two", LAST_VMEM_BYTES, two, extra,
-        (notes, sums, acts, x_half, ys_two, zs_two, gram), [all_sums],
+        partial(same_two_kernel, factor, quarter, one), "same_two", LAST_VMEM_BYTES, two, extra,
+        (notes, sums, cut_zs_two, x_half, ys_two, zs_two, gram, cross_gram), [all_sums],
     )
     sums = call(
-        partial(cross_kernel, factor, one), "cross_two", LAST_VMEM_BYTES, two, extra,
-        (notes, sums, acts, x_half, ys_two, yc_two, zs_two, zc_two, gram),
+        partial(cross_kernel, factor, quarter, one), "cross_two", LAST_VMEM_BYTES, two, extra,
+        (notes, sums, cut_zs_two, x_half, ys_two, yc_two, zs_two, zc_two, cross_gram),
         [jax.ShapeDtypeStruct((DOMAINS, examples), jnp.float32)] * 6,
     )
 

time: 139 us -> 139 us (level)
  waiting for transfers between devices: 36.7 us -> 29.9 us
  local copies, waits for them, and re-layouts: 3.3 us -> 7.9 us
  starting transfers between devices: 21.3 us -> 23.3 us
    ppermute x18, waiting for transfers between devices: 36.7 us -> 29.9 us  [send(): return lax.ppermute(value, 'ex', pairs)]
    unnamed x10 -> x16, local copies, waits for them, and re-layouts: 2.07 us -> 6.69 us
    ppermute x18, starting transfers between devices: 21.3 us -> 23.3 us  [send(): return lax.ppermute(value, 'ex', pairs)]
  transfers between devices with their start and end apart: 18 -> 18, of which waited for: 11 -> 9; matrix products, arithmetic and copies ran while one was open for 3% -> 3% of each run, Pallas kernels for 49% -> 49%
where the time goes in v2:
time: 139 us
  Pallas kernels  74.1 us (53%)
  waiting for transfers between devices  29.9 us (22%)
  starting transfers between devices  23.3 us (17%)
  local copies, waits for them, and re-layouts  7.9 us (6%)
  other arithmetic  3.24 us (2%)
    pallas_call x4, Pallas kernels, call(): pl.pallas_call(kernel, in_specs=[hbm] * len(operands), out_specs=[vmem] *...  34 us
    ppermute x18, waiting for transfers between devices, send(): return lax.ppermute(value, 'ex', pairs)  29.9 us
    ppermute x18, starting transfers between devices, send(): return lax.ppermute(value, 'ex', pairs)  23.3 us
    pallas_call x1, Pallas kernels, grams(): pl.pallas_call(grams_kernel, in_specs=[pl.BlockSpec(memory_space=pltpu.SM...  18.6 us
    pallas_call x2, Pallas kernels, cut(): pl.pallas_call(cut_kernel, grid_spec=pltpu.PrefetchScalarGridSpec(num_sca...  13.7 us
    pallas_call x1, Pallas kernels, cut_half(): pl.pallas_call(functools.partial(half_kernel, steps), grid_spec=pltpu.Pre...  7.84 us
    unnamed x16, local copies, waits for them, and re-layouts  6.69 us
  transfers between devices with their start and end apart: 18, of which 9 were waited for; matrix products, arithmetic and copies ran while one was open for 3% of the time, Pallas kernels for 49%

profile of v2, /device:TPU:0, one launch (start us, length us, event | category | flops | bytes accessed | tf_op | source)
XLA Modules:
  0.0 138.6 jit_solution(6753353215758649172)
XLA Ops:
  0.0 3.0 %collective-permute-start.3 = (bf16[768,1024]{1,0:T(8,128)(2,1)}, bf16[768,1024]{1,0:T(8,128)(2,1)}, u32[]{:S(2)}, u32[]{:S(2)}) collective-permute-start(bf16[768,1024]{1,0:T(8,128)(2,1)} %xs.1), channel_id=1, source_target_pairs={{0,2},{1,3},{2,0},{3,1},{4,6},{5,7},{6,4},{7,5},{8,10},{9,11},{10,... | collective-permute-start | bytes 4718600 | tf_op jit(solution)/shard_map/ppermute | solution.py:58
  3.0 3.6 %collective-permute-start.4 = (bf16[768,1024]{1,0:T(8,128)(2,1)}, bf16[768,1024]{1,0:T(8,128)(2,1)}, u32[]{:S(2)}, u32[]{:S(2)}) collective-permute-start(bf16[768,1024]{1,0:T(8,128)(2,1)} %xs.1), channel_id=1, source_target_pairs={{0,12},{1,13},{2,6},{3,7},{4,0},{5,1},{6,10},{7,11},{8,4},{9,5},{1... | collective-permute-start | bytes 4718600 | tf_op jit(solution)/shard_map/ppermute | solution.py:58
  9.2 6.9 %cut.2 = (bf16[784,896]{1,0:T(8,128)(2,1)}, bf16[784,896]{1,0:T(8,128)(2,1)}, bf16[768,384]{1,0:T(8,128)(2,1)}, bf16[768,384]{1,0:T(8,128)(2,1)}) custom-call(s32[2]{0:T(128)} %pad_add_fusion.places, bf16[16,128]{1,0:T(8,128)(2,1)} %broadcast_in_dim.2.info, bf16[768,5120]{1,0:T(8,128)(2,1)} %acts.3, bf16[768,5120]{1,0:T(8,128)(2,1)} %acts.3), custom_call_target="tpu_custom_call" | custom-call | flops 1 | bytes 1 | tf_op jit(solution)/shard_map/cut/pallas_call | solution.py:98
  17.2 6.8 %cut.3 = (bf16[784,896]{1,0:T(8,128)(2,1)}, bf16[784,896]{1,0:T(8,128)(2,1)}, bf16[768,384]{1,0:T(8,128)(2,1)}, bf16[768,384]{1,0:T(8,128)(2,1)}) custom-call(s32[2]{0:T(128)} %pad_add_fusion.1.places, bf16[16,128]{1,0:T(8,128)(2,1)} %broadcast_in_dim.2.info, bf16[768,5120]{1,0:T(8,128)(2,1)} %acts.3, bf16[768,5120]{1,0:T(8,128)(2,1)} %acts.3), custom_call_target="tpu_custom_call" | custom-call | flops 1 | bytes 1 | tf_op jit(solution)/shard_map/cut/pallas_call | solution.py:98
  24.0 7.8 %half.1 = bf16[784,3584]{1,0:T(8,128)(2,1)} custom-call(s32[1]{0:T(128)} %bitcast.4.place, bf16[16,128]{1,0:T(8,128)(2,1)} %broadcast_in_dim.2.info, bf16[768,5120]{1,0:T(8,128)(2,1)} %acts.3, bf16[768,1024]{1,0:T(8,128)(2,1)} %xs.1), custom_call_target="tpu_custom_call" | custom-call | flops 1 | bytes 1 | tf_op jit(solution)/shard_map/half/pallas_call | solution.py:133
  31.9 9.6 %conditional.2 = (bf16[784,3584]{1,0:T(8,128)(2,1)}) conditional(s32[]{:T(128)} %bitcast.3, () %tuple.24, bf16[784,3584]{1,0:T(8,128)(2,1)} %half.1), branch_computations={%region_0.1_spmd, %region_1.2_spmd} | conditional | bytes 22478896 | solution.py:531
  32.0 9.5 %collective-permute-done = bf16[784,3584]{1,0:T(8,128)(2,1)} collective-permute-done((bf16[784,3584]{1,0:T(8,128)(2,1)}, bf16[784,3584]{1,0:T(8,128)(2,1)}, u32[]{:S(2)}, u32[]{:S(2)}) %collective-permute-start) | collective-permute-done | bytes 5619744 | tf_op jit(solution)/shard_map/cond/branch_1_fun/ppermute | solution.py:58
  42.8 6.0 %conditional.3 = (bf16[768,1024]{1,0:T(8,128)(2,1)}, bf16[768,1024]{1,0:T(8,128)(2,1)}) conditional(s32[]{:T(128)} %bitcast.3, () %tuple.28, (bf16[768,1024]{1,0:T(8,128)(2,1)}, bf16[768,1024]{1,0:T(8,128)(2,1)}) %tuple.29), branch_computations={%region_2.3_spmd, %region_3.4_spmd} | conditional | bytes 12583008 | solution.py:531
  43.3 3.2 %collective-permute-done.1 = bf16[768,1024]{1,0:T(8,128)(2,1)} collective-permute-done((bf16[768,1024]{1,0:T(8,128)(2,1)}, bf16[768,1024]{1,0:T(8,128)(2,1)}, u32[]{:S(2)}, u32[]{:S(2)}) %collective-permute-start.1) | collective-permute-done | bytes 1572896 | tf_op jit(solution)/shard_map/cond/branch_1_fun/ppermute | solution.py:58
  46.5 2.2 %collective-permute-done.2 = bf16[768,1024]{1,0:T(8,128)(2,1)} collective-permute-done((bf16[768,1024]{1,0:T(8,128)(2,1)}, bf16[768,1024]{1,0:T(8,128)(2,1)}, u32[]{:S(2)}, u32[]{:S(2)}) %collective-permute-start.2) | collective-permute-done | bytes 1572896 | tf_op jit(solution)/shard_map/cond/branch_1_fun/ppermute | solution.py:58
  48.8 3.8 %collective-permute-start.8 = (bf16[784,896]{1,0:T(8,128)(2,1)}, bf16[784,896]{1,0:T(8,128)(2,1)}, u32[]{:S(2)}, u32[]{:S(2)}) collective-permute-start(bf16[784,896]{1,0:T(8,128)(2,1)} %get-tuple-element.66), channel_id=1, source_target_pairs={{0,13},{1,12},{2,7},{3,6},{4,1},{5,0},{6,11},{7,10},{8,5},{9,4},{1... | collective-permute-start | bytes 4214792 | tf_op jit(solution)/shard_map/ppermute | solution.py:58
  53.2 18.6 %grams.1 = (f32[3,768,768]{2,1,0:T(8,128)}, f32[4,768,768]{2,1,0:T(8,128)}) custom-call(s32[14]{0:T(128)} %stack.47.table, bf16[768,1024]{1,0:T(8,128)(2,1)} %xs.1, bf16[784,3584]{1,0:T(8,128)(2,1)} %get-tuple-element.83.xc.x_half.refs_1_, bf16[768,1024]{1,0:T(8,128)(2,1)} %collective-permute-done.3.ys, bf16[768,1024]{1,0:T(8,128)(2,1)} %get-tuple-element.57.yc, ...), custom_call_target="tpu_custom_call" | custom-call | flops 1 | bytes 1 | tf_op jit(solution)/shard_map/grams/pallas_call | solution.py:191
  71.8 14.7 %same_one.1 = (f32[6,48,128]{2,1,0:T(8,128)}, bf16[6,16,128]{2,1,0:T(8,128)(2,1)}) custom-call(bf16[784,896]{1,0:T(8,128)(2,1)} %get-tuple-element.47.xs.refs_0_, bf16[768,5120]{1,0:T(8,128)(2,1)} %acts.3, bf16[784,3584]{1,0:T(8,128)(2,1)} %get-tuple-element.83.xc.x_half.refs_1_, bf16[784,896]{1,0:T(8,128)(2,1)} %collective-permute-done.5.ys.refs_2_, ...), custom_call_target="tpu_custom_call" | custom-call | flops 1 | bytes 1 | tf_op jit(solution)/shard_map/same_one/pallas_call | solution.py:556
  86.6 4.3 %collective-permute-start.10 = (bf16[768,384]{1,0:T(8,128)(2,1)S(1)}, bf16[768,384]{1,0:T(8,128)(2,1)S(1)}, u32[]{:S(2)}, u32[]{:S(2)}) collective-permute-start(bf16[768,384]{1,0:T(8,128)(2,1)S(1)} %copy-done.4), channel_id=1, source_target_pairs={{0,12},{1,13},{2,6},{3,7},{4,0},{5,1},{6,10},{7,11},{8,4},{9,5},{1... | collective-permute-start | bytes 1769480 | tf_op jit(solution)/shard_map/ppermute | solution.py:58
  90.9 7.4 %collective-permute-done.7.refs_3_ = bf16[784,896]{1,0:T(8,128)(2,1)} collective-permute-done((bf16[784,896]{1,0:T(8,128)(2,1)}, bf16[784,896]{1,0:T(8,128)(2,1)}, u32[]{:S(2)}, u32[]{:S(2)}) %collective-permute-start.7) | collective-permute-done | bytes 1404960 | tf_op jit(solution)/shard_map/ppermute | solution.py:58
  98.3 2.0 %collective-permute-start.11 = (bf16[768,384]{1,0:T(8,128)(2,1)}, bf16[768,384]{1,0:T(8,128)(2,1)}, u32[]{:S(2)}, u32[]{:S(2)}) collective-permute-start(bf16[768,384]{1,0:T(8,128)(2,1)} %get-tuple-element.71), channel_id=1, source_target_pairs={{0,3},{1,2},{2,1},{3,0},{4,7},{5,6},{6,5},{7,4},{8,11},{9,10},{10,... | collective-permute-start | bytes 1769480 | tf_op jit(solution)/shard_map/ppermute | solution.py:58
  100.3 1.6 %collective-permute-done.8.refs_5_ = bf16[784,896]{1,0:T(8,128)(2,1)} collective-permute-done((bf16[784,896]{1,0:T(8,128)(2,1)}, bf16[784,896]{1,0:T(8,128)(2,1)}, u32[]{:S(2)}, u32[]{:S(2)}) %collective-permute-start.8) | collective-permute-done | bytes 1404960 | tf_op jit(solution)/shard_map/ppermute | solution.py:58
  101.9 3.7 %copy-done = f32[4,768,768]{2,1,0:T(8,128)S(1)} copy-done((f32[4,768,768]{2,1,0:T(8,128)S(1)}, f32[4,768,768]{2,1,0:T(8,128)}, u32[]{:S(2)}) %copy-start) | copy-done | bytes 9437208
  108.6 8.5 %cross_one.1 = (f32[6,48,128]{2,1,0:T(8,128)S(1)}, bf16[6,16,128]{2,1,0:T(8,128)(2,1)S(1)}) custom-call(bf16[6,16,128]{2,1,0:T(8,128)(2,1)S(1)} %copy-done.6, f32[6,48,128]{2,1,0:T(8,128)S(1)} %copy-done.5, bf16[784,896]{1,0:T(8,128)(2,1)S(1)} %copy-done.3, bf16[784,3584]{1,0:T(8,128)(2,1)} %get-tuple-element.83.xc.x_half.refs_1_, ...), custom_call_target="tpu_custom_call" | custom-call | flops 1 | bytes 1 | tf_op jit(solution)/shard_map/cross_one/pallas_call | solution.py:556
  117.1 5.2 %same_two.1.earlier = f32[6,48,128]{2,1,0:T(8,128)S(1)} custom-call(bf16[6,16,128]{2,1,0:T(8,128)(2,1)S(1)} %get-tuple-element.67.notes, f32[6,48,128]{2,1,0:T(8,128)S(1)} %get-tuple-element.68.earlier, bf16[768,384]{1,0:T(8,128)(2,1)S(1)} %copy-done.4, bf16[784,3584]{1,0:T(8,128)(2,1)} %get-tuple-element.83.xc.x_half.refs_1_, ...), custom_call_target="tpu_custom_call" | custom-call | flops 1 | bytes 1 | tf_op jit(solution)/shard_map/same_two/pallas_call | solution.py:556
  122.4 3.4 %collective-permute-done.12.refs_5_ = bf16[768,384]{1,0:T(8,128)(2,1)S(1)} collective-permute-done((bf16[768,384]{1,0:T(8,128)(2,1)}, bf16[768,384]{1,0:T(8,128)(2,1)S(1)}, u32[]{:S(2)}, u32[]{:S(2)}) %collective-permute-start.12) | collective-permute-done | bytes 589856 | tf_op jit(solution)/shard_map/ppermute | solution.py:58
  125.8 5.6 %cross_two.1 = (f32[48,96]{1,0:T(8,128)S(1)}, f32[48,96]{1,0:T(8,128)S(1)}, f32[48,96]{1,0:T(8,128)S(1)}, f32[48,96]{1,0:T(8,128)S(1)}, f32[48,96]{1,0:T(8,128)S(1)}, /*index=5*/f32[48,96]{1,0:T(8,128)S(1)}) custom-call(bf16[6,16,128]{2,1,0:T(8,128)(2,1)S(1)} %get-tuple-element.67.notes, f32[6,48,128]{2,1,0:T(8,128)S(1)} %same_two.1.earlier, ...), custom_call_target="tpu_custom_call" | custom-call | flops 1 | bytes 1 | tf_op jit(solution)/shard_map/cross_two/pallas_call | solution.py:556
  131.4 2.0 %collective-permute-start.14 = (f32[48,96]{1,0:T(8,128)S(1)}, f32[48,96]{1,0:T(8,128)S(1)}, u32[]{:S(2)}, u32[]{:S(2)}) collective-permute-start(f32[48,96]{1,0:T(8,128)S(1)} %get-tuple-element.75), channel_id=1, source_target_pairs={{0,5},{1,4},{2,15},{3,14},{4,9},{5,8},{6,3},{7,2},{8,13},{9,12},{1... | collective-permute-start | bytes 55304 | tf_op jit(solution)/shard_map/ppermute | solution.py:58
  135.5 1.5 %collective-permute-done.13 = f32[48,96]{1,0:T(8,128)S(1)} collective-permute-done((f32[48,96]{1,0:T(8,128)S(1)}, f32[48,96]{1,0:T(8,128)S(1)}, u32[]{:S(2)}, u32[]{:S(2)}) %collective-permute-start.13) | collective-permute-done | bytes 18464 | tf_op jit(solution)/shard_map/ppermute | solution.py:58
  (49 shorter events, 13.0 us)
Async XLA Ops:
  0.0 42.8 %collective-permute-start.3 = (bf16[768,1024]{1,0:T(8,128)(2,1)}, bf16[768,1024]{1,0:T(8,128)(2,1)}, u32[]{:S(2)}, u32[]{:S(2)}) collective-permute-start(bf16[768,1024]{1,0:T(8,128)(2,1)} %xs.1), channel_id=1, source_target_pairs={{0,2},{1,3},{2,0},{3,1},{4,6},{5,7},{6,4},{7,5},{8,10},{9,11},{10,... | collective-permute-start | bytes 4718600 | tf_op jit(solution)/shard_map/ppermute | solution.py:58
  3.0 39.8 %collective-permute-start.4 = (bf16[768,1024]{1,0:T(8,128)(2,1)}, bf16[768,1024]{1,0:T(8,128)(2,1)}, u32[]{:S(2)}, u32[]{:S(2)}) collective-permute-start(bf16[768,1024]{1,0:T(8,128)(2,1)} %xs.1), channel_id=1, source_target_pairs={{0,12},{1,13},{2,6},{3,7},{4,0},{5,1},{6,10},{7,11},{8,4},{9,5},{1... | collective-permute-start | bytes 4718600 | tf_op jit(solution)/shard_map/ppermute | solution.py:58
  16.0 55.7 %collective-permute-start.5 = (bf16[784,896]{1,0:T(8,128)(2,1)}, bf16[784,896]{1,0:T(8,128)(2,1)}, u32[]{:S(2)}, u32[]{:S(2)}) collective-permute-start(bf16[784,896]{1,0:T(8,128)(2,1)} %get-tuple-element.48), channel_id=1, source_target_pairs={{0,2},{1,3},{2,0},{3,1},{4,6},{5,7},{6,4},{7,5},{8,10},{9,11},{10,... | collective-permute-start | bytes 4214792 | tf_op jit(solution)/shard_map/ppermute | solution.py:58
  16.0 55.8 %collective-permute-start.6 = (bf16[784,896]{1,0:T(8,128)(2,1)}, bf16[784,896]{1,0:T(8,128)(2,1)}, u32[]{:S(2)}, u32[]{:S(2)}) collective-permute-start(bf16[784,896]{1,0:T(8,128)(2,1)} %get-tuple-element.47.xs.refs_0_), channel_id=1, source_target_pairs={{0,12},{1,13},{2,6},{3,7},{4,0},{5,1},{6,10},{7,11},{8,4},{9,5},{1... | collective-permute-start | bytes 4214792 | tf_op jit(solution)/shard_map/ppermute | solution.py:58
  24.0 7.8 %copy-start.7 = (s32[1,2]{1,0:T(1,128)S(1)}, s32[1,2]{1,0:T(1,128)}, u32[]{:S(2)}) copy-start(s32[1,2]{1,0:T(1,128)} %param.11) | copy-start | bytes 28
  31.9 9.6 %collective-permute-start = (bf16[784,3584]{1,0:T(8,128)(2,1)}, bf16[784,3584]{1,0:T(8,128)(2,1)}, u32[]{:S(2)}, u32[]{:S(2)}) collective-permute-start(bf16[784,3584]{1,0:T(8,128)(2,1)} %param.1), channel_id=1, source_target_pairs={{0,1},{1,0},{2,3},{3,2},{4,5},{5,4},{6,7},{7,6},{8,9},{9,8},{10,11... | collective-permute-start | bytes 16859144 | tf_op jit(solution)/shard_map/cond/branch_1_fun/ppermute | solution.py:58
  41.5 56.8 %collective-permute-start.7 = (bf16[784,896]{1,0:T(8,128)(2,1)}, bf16[784,896]{1,0:T(8,128)(2,1)}, u32[]{:S(2)}, u32[]{:S(2)}) collective-permute-start(bf16[784,896]{1,0:T(8,128)(2,1)} %get-tuple-element.50), channel_id=1, source_target_pairs={{0,3},{1,2},{2,1},{3,0},{4,7},{5,6},{6,5},{7,4},{8,11},{9,10},{10,... | collective-permute-start | bytes 4214792 | tf_op jit(solution)/shard_map/ppermute | solution.py:58
  42.8 3.8 %collective-permute-start.1 = (bf16[768,1024]{1,0:T(8,128)(2,1)}, bf16[768,1024]{1,0:T(8,128)(2,1)}, u32[]{:S(2)}, u32[]{:S(2)}) collective-permute-start(bf16[768,1024]{1,0:T(8,128)(2,1)} %get-tuple-element.13), channel_id=1, source_target_pairs={{0,1},{1,0},{2,3},{3,2},{4,5},{5,4},{6,7},{7,6},{8,9},{9,8},{10,11... | collective-permute-start | bytes 4718600 | tf_op jit(solution)/shard_map/cond/branch_1_fun/ppermute | solution.py:58
  43.1 5.6 %collective-permute-start.2 = (bf16[768,1024]{1,0:T(8,128)(2,1)}, bf16[768,1024]{1,0:T(8,128)(2,1)}, u32[]{:S(2)}, u32[]{:S(2)}) collective-permute-start(bf16[768,1024]{1,0:T(8,128)(2,1)} %get-tuple-element.14), channel_id=1, source_target_pairs={{0,1},{1,0},{2,3},{3,2},{4,5},{5,4},{6,7},{7,6},{8,9},{9,8},{10,11... | collective-permute-start | bytes 4718600 | tf_op jit(solution)/shard_map/cond/branch_1_fun/ppermute | solution.py:58
  48.8 53.2 %collective-permute-start.8 = (bf16[784,896]{1,0:T(8,128)(2,1)}, bf16[784,896]{1,0:T(8,128)(2,1)}, u32[]{:S(2)}, u32[]{:S(2)}) collective-permute-start(bf16[784,896]{1,0:T(8,128)(2,1)} %get-tuple-element.66), channel_id=1, source_target_pairs={{0,13},{1,12},{2,7},{3,6},{4,1},{5,0},{6,11},{7,10},{8,5},{9,4},{1... | collective-permute-start | bytes 4214792 | tf_op jit(solution)/shard_map/ppermute | solution.py:58
  52.6 64.5 %collective-permute-start.9 = (bf16[768,384]{1,0:T(8,128)(2,1)}, bf16[768,384]{1,0:T(8,128)(2,1)}, u32[]{:S(2)}, u32[]{:S(2)}) collective-permute-start(bf16[768,384]{1,0:T(8,128)(2,1)} %get-tuple-element.70), channel_id=1, source_target_pairs={{0,2},{1,3},{2,0},{3,1},{4,6},{5,7},{6,4},{7,5},{8,10},{9,11},{10,... | collective-permute-start | bytes 1769480 | tf_op jit(solution)/shard_map/ppermute | solution.py:58
  71.8 14.7 %copy-start.4 = (bf16[768,384]{1,0:T(8,128)(2,1)S(1)}, bf16[768,384]{1,0:T(8,128)(2,1)}, u32[]{:S(2)}) copy-start(bf16[768,384]{1,0:T(8,128)(2,1)} %get-tuple-element.69.xs.refs_0_) | copy-start | bytes 1769476
  86.6 30.5 %collective-permute-start.10 = (bf16[768,384]{1,0:T(8,128)(2,1)S(1)}, bf16[768,384]{1,0:T(8,128)(2,1)S(1)}, u32[]{:S(2)}, u32[]{:S(2)}) collective-permute-start(bf16[768,384]{1,0:T(8,128)(2,1)S(1)} %copy-done.4), channel_id=1, source_target_pairs={{0,12},{1,13},{2,6},{3,7},{4,0},{5,1},{6,10},{7,11},{8,4},{9,5},{1... | collective-permute-start | bytes 1769480 | tf_op jit(solution)/shard_map/ppermute | solution.py:58
  90.9 34.9 %collective-permute-start.12 = (bf16[768,384]{1,0:T(8,128)(2,1)}, bf16[768,384]{1,0:T(8,128)(2,1)S(1)}, u32[]{:S(2)}, u32[]{:S(2)}) collective-permute-start(bf16[768,384]{1,0:T(8,128)(2,1)} %get-tuple-element.72), channel_id=1, source_target_pairs={{0,13},{1,12},{2,7},{3,6},{4,1},{5,0},{6,11},{7,10},{8,5},{9,4},{1... | collective-permute-start | bytes 1769480 | tf_op jit(solution)/shard_map/ppermute | solution.py:58
  98.3 27.5 %collective-permute-start.11 = (bf16[768,384]{1,0:T(8,128)(2,1)}, bf16[768,384]{1,0:T(8,128)(2,1)}, u32[]{:S(2)}, u32[]{:S(2)}) collective-permute-start(bf16[768,384]{1,0:T(8,128)(2,1)} %get-tuple-element.71), channel_id=1, source_target_pairs={{0,3},{1,2},{2,1},{3,0},{4,7},{5,6},{6,5},{7,4},{8,11},{9,10},{10,... | collective-permute-start | bytes 1769480 | tf_op jit(solution)/shard_map/ppermute | solution.py:58
  101.9 3.7 %copy-start = (f32[4,768,768]{2,1,0:T(8,128)S(1)}, f32[4,768,768]{2,1,0:T(8,128)}, u32[]{:S(2)}) copy-start(f32[4,768,768]{2,1,0:T(8,128)} %get-tuple-element.61.cross_gram.refs_6_) | copy-start | bytes 28311556
  105.6 1.3 copy-start.3
  108.6 8.5 %copy-start.1 = (f32[4,768,768]{2,1,0:T(8,128)S(1)}, f32[4,768,768]{2,1,0:T(8,128)}, u32[]{:S(2)}) copy-start(f32[4,768,768]{2,1,0:T(8,128)} %get-tuple-element.61.cross_gram.refs_6_) | copy-start | bytes 28311556
  108.6 8.5 %copy-start.2 = (f32[3,768,768]{2,1,0:T(8,128)S(1)}, f32[3,768,768]{2,1,0:T(8,128)}, u32[]{:S(2)}) copy-start(f32[3,768,768]{2,1,0:T(8,128)} %get-tuple-element.60.gram) | copy-start | bytes 21233668
  131.3 5.7 %collective-permute-start.13 = (f32[48,96]{1,0:T(8,128)S(1)}, f32[48,96]{1,0:T(8,128)S(1)}, u32[]{:S(2)}, u32[]{:S(2)}) collective-permute-start(f32[48,96]{1,0:T(8,128)S(1)} %get-tuple-element.74), channel_id=1, source_target_pairs={{0,4},{1,5},{2,14},{3,15},{4,8},{5,9},{6,2},{7,3},{8,12},{9,13},{1... | collective-permute-start | bytes 55304 | tf_op jit(solution)/shard_map/ppermute | solution.py:58
  131.4 6.5 %collective-permute-start.14 = (f32[48,96]{1,0:T(8,128)S(1)}, f32[48,96]{1,0:T(8,128)S(1)}, u32[]{:S(2)}, u32[]{:S(2)}) collective-permute-start(f32[48,96]{1,0:T(8,128)S(1)} %get-tuple-element.75), channel_id=1, source_target_pairs={{0,5},{1,4},{2,15},{3,14},{4,9},{5,8},{6,3},{7,2},{8,13},{9,12},{1... | collective-permute-start | bytes 55304 | tf_op jit(solution)/shard_map/ppermute | solution.py:58
  133.4 4.6 %collective-permute-start.15 = (f32[48,96]{1,0:T(8,128)S(1)}, f32[48,96]{1,0:T(8,128)S(1)}, u32[]{:S(2)}, u32[]{:S(2)}) collective-permute-start(f32[48,96]{1,0:T(8,128)S(1)} %get-tuple-element.76), channel_id=1, source_target_pairs={{0,2},{1,3},{2,0},{3,1},{4,6},{5,7},{6,4},{7,5},{8,10},{9,11},{10,... | collective-permute-start | bytes 55304 | tf_op jit(solution)/shard_map/ppermute | solution.py:58
  133.9 4.0 %collective-permute-start.16 = (f32[48,96]{1,0:T(8,128)S(1)}, f32[48,96]{1,0:T(8,128)S(1)}, u32[]{:S(2)}, u32[]{:S(2)}) collective-permute-start(f32[48,96]{1,0:T(8,128)S(1)} %get-tuple-element.77), channel_id=1, source_target_pairs={{0,3},{1,2},{2,1},{3,0},{4,7},{5,6},{6,5},{7,4},{8,11},{9,10},{10,... | collective-permute-start | bytes 55304 | tf_op jit(solution)/shard_map/ppermute | solution.py:58
  134.6 3.4 %collective-permute-start.17 = (f32[48,96]{1,0:T(8,128)S(1)}, f32[48,96]{1,0:T(8,128)S(1)}, u32[]{:S(2)}, u32[]{:S(2)}) collective-permute-start(f32[48,96]{1,0:T(8,128)S(1)} %get-tuple-element.78), channel_id=1, source_target_pairs={{0,1},{1,0},{2,3},{3,2},{4,5},{5,4},{6,7},{7,6},{8,9},{9,8},{10,11... | collective-permute-start | bytes 55304 | tf_op jit(solution)/shard_map/ppermute | solution.py:58
  (2 other events, 1.6 us)

commit v3 on v2

--- a/solution.py
+++ b/solution.py
@@ -13,7 +13,7 @@
 DOMAINS = 48
 LANES = 128
 VMEM_BYTES = 63 * 1024 * 1024
-LAST_VMEM_BYTES = 30 * 1024 * 1024
+LAST_VMEM_BYTES = 44 * 1024 * 1024
 
 INFO = 16
 

time: 139 us -> 139 us (level)
  waiting for transfers between devices: 29.9 us -> 33.3 us
  local copies, waits for them, and re-layouts: 7.9 us -> 4.57 us
    ppermute x18, waiting for transfers between devices: 29.9 us -> 33.3 us  [send(): return lax.ppermute(value, 'ex', pairs)]
    unnamed x16 -> x14, local copies, waits for them, and re-layouts: 6.69 us -> 3.34 us
  transfers between devices with their start and end apart: 18 -> 18, of which waited for: 9 -> 10; matrix products, arithmetic and copies ran while one was open for 3% -> 3% of each run, Pallas kernels for 49% -> 49%
where the time goes in v3:
time: 139 us
  Pallas kernels  74 us (53%)
  waiting for transfers between devices  33.3 us (24%)
  starting transfers between devices  23.3 us (17%)
  local copies, waits for them, and re-layouts  4.57 us (3%)
  other arithmetic  3.2 us (2%)
    pallas_call x4, Pallas kernels, call(): pl.pallas_call(kernel, in_specs=[hbm] * len(operands), out_specs=[vmem] *...  33.9 us
    ppermute x18, waiting for transfers between devices, send(): return lax.ppermute(value, 'ex', pairs)  33.3 us
    ppermute x18, starting transfers between devices, send(): return lax.ppermute(value, 'ex', pairs)  23.3 us
    pallas_call x1, Pallas kernels, grams(): pl.pallas_call(grams_kernel, in_specs=[pl.BlockSpec(memory_space=pltpu.SM...  18.6 us
    pallas_call x2, Pallas kernels, cut(): pl.pallas_call(cut_kernel, grid_spec=pltpu.PrefetchScalarGridSpec(num_sca...  13.7 us
    pallas_call x1, Pallas kernels, cut_half(): pl.pallas_call(functools.partial(half_kernel, steps), grid_spec=pltpu.Pre...  7.84 us
    unnamed x14, local copies, waits for them, and re-layouts  3.34 us
  transfers between devices with their start and end apart: 18, of which 10 were waited for; matrix products, arithmetic and copies ran while one was open for 3% of the time, Pallas kernels for 49%

profile of v3, /device:TPU:0, one launch (start us, length us, event | category | flops | bytes accessed | tf_op | source)
XLA Modules:
  0.0 138.5 jit_solution(15786677611365153577)
XLA Ops:
  0.0 3.0 %collective-permute-start.3 = (bf16[768,1024]{1,0:T(8,128)(2,1)}, bf16[768,1024]{1,0:T(8,128)(2,1)}, u32[]{:S(2)}, u32[]{:S(2)}) collective-permute-start(bf16[768,1024]{1,0:T(8,128)(2,1)} %xs.1), channel_id=1, source_target_pairs={{0,2},{1,3},{2,0},{3,1},{4,6},{5,7},{6,4},{7,5},{8,10},{9,11},{10,... | collective-permute-start | bytes 4718600 | tf_op jit(solution)/shard_map/ppermute | solution.py:58
  3.0 3.6 %collective-permute-start.4 = (bf16[768,1024]{1,0:T(8,128)(2,1)}, bf16[768,1024]{1,0:T(8,128)(2,1)}, u32[]{:S(2)}, u32[]{:S(2)}) collective-permute-start(bf16[768,1024]{1,0:T(8,128)(2,1)} %xs.1), channel_id=1, source_target_pairs={{0,12},{1,13},{2,6},{3,7},{4,0},{5,1},{6,10},{7,11},{8,4},{9,5},{1... | collective-permute-start | bytes 4718600 | tf_op jit(solution)/shard_map/ppermute | solution.py:58
  9.2 6.9 %cut.2 = (bf16[784,896]{1,0:T(8,128)(2,1)}, bf16[784,896]{1,0:T(8,128)(2,1)}, bf16[768,384]{1,0:T(8,128)(2,1)}, bf16[768,384]{1,0:T(8,128)(2,1)}) custom-call(s32[2]{0:T(128)} %pad_add_fusion.places, bf16[16,128]{1,0:T(8,128)(2,1)} %broadcast_in_dim.2.info, bf16[768,5120]{1,0:T(8,128)(2,1)} %acts.3, bf16[768,5120]{1,0:T(8,128)(2,1)} %acts.3), custom_call_target="tpu_custom_call" | custom-call | flops 1 | bytes 1 | tf_op jit(solution)/shard_map/cut/pallas_call | solution.py:98
  17.1 6.8 %cut.3 = (bf16[784,896]{1,0:T(8,128)(2,1)}, bf16[784,896]{1,0:T(8,128)(2,1)}, bf16[768,384]{1,0:T(8,128)(2,1)}, bf16[768,384]{1,0:T(8,128)(2,1)}) custom-call(s32[2]{0:T(128)} %pad_add_fusion.1.places, bf16[16,128]{1,0:T(8,128)(2,1)} %broadcast_in_dim.2.info, bf16[768,5120]{1,0:T(8,128)(2,1)} %acts.3, bf16[768,5120]{1,0:T(8,128)(2,1)} %acts.3), custom_call_target="tpu_custom_call" | custom-call | flops 1 | bytes 1 | tf_op jit(solution)/shard_map/cut/pallas_call | solution.py:98
  23.9 7.8 %half.1 = bf16[784,3584]{1,0:T(8,128)(2,1)} custom-call(s32[1]{0:T(128)} %bitcast.4.place, bf16[16,128]{1,0:T(8,128)(2,1)} %broadcast_in_dim.2.info, bf16[768,5120]{1,0:T(8,128)(2,1)} %acts.3, bf16[768,1024]{1,0:T(8,128)(2,1)} %xs.1), custom_call_target="tpu_custom_call" | custom-call | flops 1 | bytes 1 | tf_op jit(solution)/shard_map/half/pallas_call | solution.py:133
  31.8 9.6 %conditional.2 = (bf16[784,3584]{1,0:T(8,128)(2,1)}) conditional(s32[]{:T(128)} %bitcast.3, () %tuple.24, bf16[784,3584]{1,0:T(8,128)(2,1)} %half.1), branch_computations={%region_0.1_spmd, %region_1.2_spmd} | conditional | bytes 22478896 | solution.py:531
  31.9 9.5 %collective-permute-done = bf16[784,3584]{1,0:T(8,128)(2,1)} collective-permute-done((bf16[784,3584]{1,0:T(8,128)(2,1)}, bf16[784,3584]{1,0:T(8,128)(2,1)}, u32[]{:S(2)}, u32[]{:S(2)}) %collective-permute-start) | collective-permute-done | bytes 5619744 | tf_op jit(solution)/shard_map/cond/branch_1_fun/ppermute | solution.py:58
  42.7 6.0 %conditional.3 = (bf16[768,1024]{1,0:T(8,128)(2,1)}, bf16[768,1024]{1,0:T(8,128)(2,1)}) conditional(s32[]{:T(128)} %bitcast.3, () %tuple.28, (bf16[768,1024]{1,0:T(8,128)(2,1)}, bf16[768,1024]{1,0:T(8,128)(2,1)}) %tuple.29), branch_computations={%region_2.3_spmd, %region_3.4_spmd} | conditional | bytes 12583008 | solution.py:531
  43.2 3.2 %collective-permute-done.1 = bf16[768,1024]{1,0:T(8,128)(2,1)} collective-permute-done((bf16[768,1024]{1,0:T(8,128)(2,1)}, bf16[768,1024]{1,0:T(8,128)(2,1)}, u32[]{:S(2)}, u32[]{:S(2)}) %collective-permute-start.1) | collective-permute-done | bytes 1572896 | tf_op jit(solution)/shard_map/cond/branch_1_fun/ppermute | solution.py:58
  46.5 2.2 %collective-permute-done.2 = bf16[768,1024]{1,0:T(8,128)(2,1)} collective-permute-done((bf16[768,1024]{1,0:T(8,128)(2,1)}, bf16[768,1024]{1,0:T(8,128)(2,1)}, u32[]{:S(2)}, u32[]{:S(2)}) %collective-permute-start.2) | collective-permute-done | bytes 1572896 | tf_op jit(solution)/shard_map/cond/branch_1_fun/ppermute | solution.py:58
  48.7 3.8 %collective-permute-start.8 = (bf16[784,896]{1,0:T(8,128)(2,1)}, bf16[784,896]{1,0:T(8,128)(2,1)}, u32[]{:S(2)}, u32[]{:S(2)}) collective-permute-start(bf16[784,896]{1,0:T(8,128)(2,1)} %get-tuple-element.66), channel_id=1, source_target_pairs={{0,13},{1,12},{2,7},{3,6},{4,1},{5,0},{6,11},{7,10},{8,5},{9,4},{1... | collective-permute-start | bytes 4214792 | tf_op jit(solution)/shard_map/ppermute | solution.py:58
  53.1 18.6 %grams.1 = (f32[3,768,768]{2,1,0:T(8,128)}, f32[4,768,768]{2,1,0:T(8,128)}) custom-call(s32[14]{0:T(128)} %stack.47.table, bf16[768,1024]{1,0:T(8,128)(2,1)} %xs.1, bf16[784,3584]{1,0:T(8,128)(2,1)} %get-tuple-element.83.xc.x_half.refs_1_, bf16[768,1024]{1,0:T(8,128)(2,1)} %collective-permute-done.3.ys, bf16[768,1024]{1,0:T(8,128)(2,1)} %get-tuple-element.57.yc, ...), custom_call_target="tpu_custom_call" | custom-call | flops 1 | bytes 1 | tf_op jit(solution)/shard_map/grams/pallas_call | solution.py:191
  71.8 14.7 %same_one.1 = (f32[6,48,128]{2,1,0:T(8,128)}, bf16[6,16,128]{2,1,0:T(8,128)(2,1)}) custom-call(bf16[784,896]{1,0:T(8,128)(2,1)} %get-tuple-element.47.xs.refs_0_, bf16[768,5120]{1,0:T(8,128)(2,1)} %acts.3, bf16[784,3584]{1,0:T(8,128)(2,1)} %get-tuple-element.83.xc.x_half.refs_1_, bf16[784,896]{1,0:T(8,128)(2,1)} %collective-permute-done.5.ys.refs_2_, ...), custom_call_target="tpu_custom_call" | custom-call | flops 1 | bytes 1 | tf_op jit(solution)/shard_map/same_one/pallas_call | solution.py:556
  86.6 4.3 %collective-permute-start.10 = (bf16[768,384]{1,0:T(8,128)(2,1)S(1)}, bf16[768,384]{1,0:T(8,128)(2,1)S(1)}, u32[]{:S(2)}, u32[]{:S(2)}) collective-permute-start(bf16[768,384]{1,0:T(8,128)(2,1)S(1)} %copy-done.1), channel_id=1, source_target_pairs={{0,12},{1,13},{2,6},{3,7},{4,0},{5,1},{6,10},{7,11},{8,4},{9,5},{1... | collective-permute-start | bytes 1769480 | tf_op jit(solution)/shard_map/ppermute | solution.py:58
  90.9 7.4 %collective-permute-done.7.refs_3_ = bf16[784,896]{1,0:T(8,128)(2,1)} collective-permute-done((bf16[784,896]{1,0:T(8,128)(2,1)}, bf16[784,896]{1,0:T(8,128)(2,1)}, u32[]{:S(2)}, u32[]{:S(2)}) %collective-permute-start.7) | collective-permute-done | bytes 1404960 | tf_op jit(solution)/shard_map/ppermute | solution.py:58
  98.3 2.0 %collective-permute-start.11 = (bf16[768,384]{1,0:T(8,128)(2,1)}, bf16[768,384]{1,0:T(8,128)(2,1)S(1)}, u32[]{:S(2)}, u32[]{:S(2)}) collective-permute-start(bf16[768,384]{1,0:T(8,128)(2,1)} %get-tuple-element.71), channel_id=1, source_target_pairs={{0,3},{1,2},{2,1},{3,0},{4,7},{5,6},{6,5},{7,4},{8,11},{9,10},{10,... | collective-permute-start | bytes 1769480 | tf_op jit(solution)/shard_map/ppermute | solution.py:58
  100.3 1.6 %collective-permute-done.8.refs_5_ = bf16[784,896]{1,0:T(8,128)(2,1)} collective-permute-done((bf16[784,896]{1,0:T(8,128)(2,1)}, bf16[784,896]{1,0:T(8,128)(2,1)}, u32[]{:S(2)}, u32[]{:S(2)}) %collective-permute-start.8) | collective-permute-done | bytes 1404960 | tf_op jit(solution)/shard_map/ppermute | solution.py:58
  101.9 1.5 %copy-done = bf16[784,896]{1,0:T(8,128)(2,1)S(1)} copy-done((bf16[784,896]{1,0:T(8,128)(2,1)S(1)}, bf16[784,896]{1,0:T(8,128)(2,1)}, u32[]{:S(2)}) %copy-start) | copy-done | bytes 1404952
  105.3 8.5 %cross_one.1 = (f32[6,48,128]{2,1,0:T(8,128)S(1)}, bf16[6,16,128]{2,1,0:T(8,128)(2,1)S(1)}) custom-call(bf16[6,16,128]{2,1,0:T(8,128)(2,1)S(1)} %copy-done.3, f32[6,48,128]{2,1,0:T(8,128)S(1)} %copy-done.2, bf16[784,896]{1,0:T(8,128)(2,1)S(1)} %copy-done, bf16[784,3584]{1,0:T(8,128)(2,1)} %get-tuple-element.83.xc.x_half.refs_1_, ...), custom_call_target="tpu_custom_call" | custom-call | flops 1 | bytes 1 | tf_op jit(solution)/shard_map/cross_one/pallas_call | solution.py:556
  114.5 5.2 %same_two.1.earlier = f32[6,48,128]{2,1,0:T(8,128)S(1)} custom-call(bf16[6,16,128]{2,1,0:T(8,128)(2,1)S(1)} %get-tuple-element.67.notes, f32[6,48,128]{2,1,0:T(8,128)S(1)} %get-tuple-element.68.earlier, bf16[768,384]{1,0:T(8,128)(2,1)S(1)} %copy-done.1, bf16[784,3584]{1,0:T(8,128)(2,1)} %get-tuple-element.83.xc.x_half.refs_1_, ...), custom_call_target="tpu_custom_call" | custom-call | flops 1 | bytes 1 | tf_op jit(solution)/shard_map/same_two/pallas_call | solution.py:556
  119.7 6.0 %collective-permute-done.12.refs_5_ = bf16[768,384]{1,0:T(8,128)(2,1)S(1)} collective-permute-done((bf16[768,384]{1,0:T(8,128)(2,1)}, bf16[768,384]{1,0:T(8,128)(2,1)S(1)}, u32[]{:S(2)}, u32[]{:S(2)}) %collective-permute-start.12) | collective-permute-done | bytes 589856 | tf_op jit(solution)/shard_map/ppermute | solution.py:58
  125.8 5.5 %cross_two.1 = (f32[48,96]{1,0:T(8,128)S(1)}, f32[48,96]{1,0:T(8,128)S(1)}, f32[48,96]{1,0:T(8,128)S(1)}, f32[48,96]{1,0:T(8,128)S(1)}, f32[48,96]{1,0:T(8,128)S(1)}, /*index=5*/f32[48,96]{1,0:T(8,128)S(1)}) custom-call(bf16[6,16,128]{2,1,0:T(8,128)(2,1)S(1)} %get-tuple-element.67.notes, f32[6,48,128]{2,1,0:T(8,128)S(1)} %same_two.1.earlier, ...), custom_call_target="tpu_custom_call" | custom-call | flops 1 | bytes 1 | tf_op jit(solution)/shard_map/cross_two/pallas_call | solution.py:556
  131.3 2.0 %collective-permute-start.14 = (f32[48,96]{1,0:T(8,128)S(1)}, f32[48,96]{1,0:T(8,128)S(1)}, u32[]{:S(2)}, u32[]{:S(2)}) collective-permute-start(f32[48,96]{1,0:T(8,128)S(1)} %get-tuple-element.75), channel_id=1, source_target_pairs={{0,5},{1,4},{2,15},{3,14},{4,9},{5,8},{6,3},{7,2},{8,13},{9,12},{1... | collective-permute-start | bytes 55304 | tf_op jit(solution)/shard_map/ppermute | solution.py:58
  135.5 1.5 %collective-permute-done.13 = f32[48,96]{1,0:T(8,128)S(1)} collective-permute-done((f32[48,96]{1,0:T(8,128)S(1)}, f32[48,96]{1,0:T(8,128)S(1)}, u32[]{:S(2)}, u32[]{:S(2)}) %collective-permute-start.13) | collective-permute-done | bytes 18464 | tf_op jit(solution)/shard_map/ppermute | solution.py:58
  (48 shorter events, 12.6 us)
Async XLA Ops:
  0.0 42.7 %collective-permute-start.3 = (bf16[768,1024]{1,0:T(8,128)(2,1)}, bf16[768,1024]{1,0:T(8,128)(2,1)}, u32[]{:S(2)}, u32[]{:S(2)}) collective-permute-start(bf16[768,1024]{1,0:T(8,128)(2,1)} %xs.1), channel_id=1, source_target_pairs={{0,2},{1,3},{2,0},{3,1},{4,6},{5,7},{6,4},{7,5},{8,10},{9,11},{10,... | collective-permute-start | bytes 4718600 | tf_op jit(solution)/shard_map/ppermute | solution.py:58
  3.0 39.7 %collective-permute-start.4 = (bf16[768,1024]{1,0:T(8,128)(2,1)}, bf16[768,1024]{1,0:T(8,128)(2,1)}, u32[]{:S(2)}, u32[]{:S(2)}) collective-permute-start(bf16[768,1024]{1,0:T(8,128)(2,1)} %xs.1), channel_id=1, source_target_pairs={{0,12},{1,13},{2,6},{3,7},{4,0},{5,1},{6,10},{7,11},{8,4},{9,5},{1... | collective-permute-start | bytes 4718600 | tf_op jit(solution)/shard_map/ppermute | solution.py:58
  16.0 55.7 %collective-permute-start.5 = (bf16[784,896]{1,0:T(8,128)(2,1)}, bf16[784,896]{1,0:T(8,128)(2,1)}, u32[]{:S(2)}, u32[]{:S(2)}) collective-permute-start(bf16[784,896]{1,0:T(8,128)(2,1)} %get-tuple-element.48), channel_id=1, source_target_pairs={{0,2},{1,3},{2,0},{3,1},{4,6},{5,7},{6,4},{7,5},{8,10},{9,11},{10,... | collective-permute-start | bytes 4214792 | tf_op jit(solution)/shard_map/ppermute | solution.py:58
  16.0 55.8 %collective-permute-start.6 = (bf16[784,896]{1,0:T(8,128)(2,1)}, bf16[784,896]{1,0:T(8,128)(2,1)}, u32[]{:S(2)}, u32[]{:S(2)}) collective-permute-start(bf16[784,896]{1,0:T(8,128)(2,1)} %get-tuple-element.47.xs.refs_0_), channel_id=1, source_target_pairs={{0,12},{1,13},{2,6},{3,7},{4,0},{5,1},{6,10},{7,11},{8,4},{9,5},{1... | collective-permute-start | bytes 4214792 | tf_op jit(solution)/shard_map/ppermute | solution.py:58
  23.9 7.8 %copy-start.4 = (s32[1,2]{1,0:T(1,128)S(1)}, s32[1,2]{1,0:T(1,128)}, u32[]{:S(2)}) copy-start(s32[1,2]{1,0:T(1,128)} %param.11) | copy-start | bytes 28
  31.8 9.6 %collective-permute-start = (bf16[784,3584]{1,0:T(8,128)(2,1)}, bf16[784,3584]{1,0:T(8,128)(2,1)}, u32[]{:S(2)}, u32[]{:S(2)}) collective-permute-start(bf16[784,3584]{1,0:T(8,128)(2,1)} %param.1), channel_id=1, source_target_pairs={{0,1},{1,0},{2,3},{3,2},{4,5},{5,4},{6,7},{7,6},{8,9},{9,8},{10,11... | collective-permute-start | bytes 16859144 | tf_op jit(solution)/shard_map/cond/branch_1_fun/ppermute | solution.py:58
  41.4 56.9 %collective-permute-start.7 = (bf16[784,896]{1,0:T(8,128)(2,1)}, bf16[784,896]{1,0:T(8,128)(2,1)}, u32[]{:S(2)}, u32[]{:S(2)}) collective-permute-start(bf16[784,896]{1,0:T(8,128)(2,1)} %get-tuple-element.50), channel_id=1, source_target_pairs={{0,3},{1,2},{2,1},{3,0},{4,7},{5,6},{6,5},{7,4},{8,11},{9,10},{10,... | collective-permute-start | bytes 4214792 | tf_op jit(solution)/shard_map/ppermute | solution.py:58
  42.7 3.8 %collective-permute-start.1 = (bf16[768,1024]{1,0:T(8,128)(2,1)}, bf16[768,1024]{1,0:T(8,128)(2,1)}, u32[]{:S(2)}, u32[]{:S(2)}) collective-permute-start(bf16[768,1024]{1,0:T(8,128)(2,1)} %get-tuple-element.13), channel_id=1, source_target_pairs={{0,1},{1,0},{2,3},{3,2},{4,5},{5,4},{6,7},{7,6},{8,9},{9,8},{10,11... | collective-permute-start | bytes 4718600 | tf_op jit(solution)/shard_map/cond/branch_1_fun/ppermute | solution.py:58
  43.1 5.6 %collective-permute-start.2 = (bf16[768,1024]{1,0:T(8,128)(2,1)}, bf16[768,1024]{1,0:T(8,128)(2,1)}, u32[]{:S(2)}, u32[]{:S(2)}) collective-permute-start(bf16[768,1024]{1,0:T(8,128)(2,1)} %get-tuple-element.14), channel_id=1, source_target_pairs={{0,1},{1,0},{2,3},{3,2},{4,5},{5,4},{6,7},{7,6},{8,9},{9,8},{10,11... | collective-permute-start | bytes 4718600 | tf_op jit(solution)/shard_map/cond/branch_1_fun/ppermute | solution.py:58
  48.7 53.2 %collective-permute-start.8 = (bf16[784,896]{1,0:T(8,128)(2,1)}, bf16[784,896]{1,0:T(8,128)(2,1)}, u32[]{:S(2)}, u32[]{:S(2)}) collective-permute-start(bf16[784,896]{1,0:T(8,128)(2,1)} %get-tuple-element.66), channel_id=1, source_target_pairs={{0,13},{1,12},{2,7},{3,6},{4,1},{5,0},{6,11},{7,10},{8,5},{9,4},{1... | collective-permute-start | bytes 4214792 | tf_op jit(solution)/shard_map/ppermute | solution.py:58
  52.5 61.3 %collective-permute-start.9 = (bf16[768,384]{1,0:T(8,128)(2,1)}, bf16[768,384]{1,0:T(8,128)(2,1)}, u32[]{:S(2)}, u32[]{:S(2)}) collective-permute-start(bf16[768,384]{1,0:T(8,128)(2,1)} %get-tuple-element.70), channel_id=1, source_target_pairs={{0,2},{1,3},{2,0},{3,1},{4,6},{5,7},{6,4},{7,5},{8,10},{9,11},{10,... | collective-permute-start | bytes 1769480 | tf_op jit(solution)/shard_map/ppermute | solution.py:58
  71.8 14.7 %copy-start.1 = (bf16[768,384]{1,0:T(8,128)(2,1)S(1)}, bf16[768,384]{1,0:T(8,128)(2,1)}, u32[]{:S(2)}) copy-start(bf16[768,384]{1,0:T(8,128)(2,1)} %get-tuple-element.69.xs.refs_0_) | copy-start | bytes 1769476
  86.6 27.9 %collective-permute-start.10 = (bf16[768,384]{1,0:T(8,128)(2,1)S(1)}, bf16[768,384]{1,0:T(8,128)(2,1)S(1)}, u32[]{:S(2)}, u32[]{:S(2)}) collective-permute-start(bf16[768,384]{1,0:T(8,128)(2,1)S(1)} %copy-done.1), channel_id=1, source_target_pairs={{0,12},{1,13},{2,6},{3,7},{4,0},{5,1},{6,10},{7,11},{8,4},{9,5},{1... | collective-permute-start | bytes 1769480 | tf_op jit(solution)/shard_map/ppermute | solution.py:58
  90.9 34.8 %collective-permute-start.12 = (bf16[768,384]{1,0:T(8,128)(2,1)}, bf16[768,384]{1,0:T(8,128)(2,1)S(1)}, u32[]{:S(2)}, u32[]{:S(2)}) collective-permute-start(bf16[768,384]{1,0:T(8,128)(2,1)} %get-tuple-element.72), channel_id=1, source_target_pairs={{0,13},{1,12},{2,7},{3,6},{4,1},{5,0},{6,11},{7,10},{8,5},{9,4},{1... | collective-permute-start | bytes 1769480 | tf_op jit(solution)/shard_map/ppermute | solution.py:58
  98.3 27.5 %collective-permute-start.11 = (bf16[768,384]{1,0:T(8,128)(2,1)}, bf16[768,384]{1,0:T(8,128)(2,1)S(1)}, u32[]{:S(2)}, u32[]{:S(2)}) collective-permute-start(bf16[768,384]{1,0:T(8,128)(2,1)} %get-tuple-element.71), channel_id=1, source_target_pairs={{0,3},{1,2},{2,1},{3,0},{4,7},{5,6},{6,5},{7,4},{8,11},{9,10},{10,... | collective-permute-start | bytes 1769480 | tf_op jit(solution)/shard_map/ppermute | solution.py:58
  101.9 12.5 %slice-start = ((s8[7077888]{0:T(1024)(128)(4,1)}), s8[4194304]{0:T(1024)(128)(4,1)S(1)}, s32[]{:S(2)}) async-start(s8[7077888]{0:T(1024)(128)(4,1)} %bitcast.15), calls=%async_computation | async-start | bytes 8388608
  101.9 1.5 %copy-start = (bf16[784,896]{1,0:T(8,128)(2,1)S(1)}, bf16[784,896]{1,0:T(8,128)(2,1)}, u32[]{:S(2)}) copy-start(bf16[784,896]{1,0:T(8,128)(2,1)} %get-tuple-element.47.xs.refs_0_) | copy-start | bytes 4214788
  103.4 1.1 copy-start.2
  105.3 9.2 %slice-start.1 = ((s8[7077888]{0:T(1024)(128)(4,1)}), s8[2883584]{0:T(1024)(128)(4,1)S(1)}, s32[]{:S(2)}) async-start(s8[7077888]{0:T(1024)(128)(4,1)} %bitcast.15), calls=%async_computation.1 | async-start | bytes 5767168
  131.3 5.7 %collective-permute-start.13 = (f32[48,96]{1,0:T(8,128)S(1)}, f32[48,96]{1,0:T(8,128)S(1)}, u32[]{:S(2)}, u32[]{:S(2)}) collective-permute-start(f32[48,96]{1,0:T(8,128)S(1)} %get-tuple-element.74), channel_id=1, source_target_pairs={{0,4},{1,5},{2,14},{3,15},{4,8},{5,9},{6,2},{7,3},{8,12},{9,13},{1... | collective-permute-start | bytes 55304 | tf_op jit(solution)/shard_map/ppermute | solution.py:58
  131.3 6.6 %collective-permute-start.14 = (f32[48,96]{1,0:T(8,128)S(1)}, f32[48,96]{1,0:T(8,128)S(1)}, u32[]{:S(2)}, u32[]{:S(2)}) collective-permute-start(f32[48,96]{1,0:T(8,128)S(1)} %get-tuple-element.75), channel_id=1, source_target_pairs={{0,5},{1,4},{2,15},{3,14},{4,9},{5,8},{6,3},{7,2},{8,13},{9,12},{1... | collective-permute-start | bytes 55304 | tf_op jit(solution)/shard_map/ppermute | solution.py:58
  133.3 4.6 %collective-permute-start.15 = (f32[48,96]{1,0:T(8,128)S(1)}, f32[48,96]{1,0:T(8,128)S(1)}, u32[]{:S(2)}, u32[]{:S(2)}) collective-permute-start(f32[48,96]{1,0:T(8,128)S(1)} %get-tuple-element.76), channel_id=1, source_target_pairs={{0,2},{1,3},{2,0},{3,1},{4,6},{5,7},{6,4},{7,5},{8,10},{9,11},{10,... | collective-permute-start | bytes 55304 | tf_op jit(solution)/shard_map/ppermute | solution.py:58
  133.8 4.1 %collective-permute-start.16 = (f32[48,96]{1,0:T(8,128)S(1)}, f32[48,96]{1,0:T(8,128)S(1)}, u32[]{:S(2)}, u32[]{:S(2)}) collective-permute-start(f32[48,96]{1,0:T(8,128)S(1)} %get-tuple-element.77), channel_id=1, source_target_pairs={{0,3},{1,2},{2,1},{3,0},{4,7},{5,6},{6,5},{7,4},{8,11},{9,10},{10,... | collective-permute-start | bytes 55304 | tf_op jit(solution)/shard_map/ppermute | solution.py:58
  134.5 3.4 %collective-permute-start.17 = (f32[48,96]{1,0:T(8,128)S(1)}, f32[48,96]{1,0:T(8,128)S(1)}, u32[]{:S(2)}, u32[]{:S(2)}) collective-permute-start(f32[48,96]{1,0:T(8,128)S(1)} %get-tuple-element.78), channel_id=1, source_target_pairs={{0,1},{1,0},{2,3},{3,2},{4,5},{5,4},{6,7},{7,6},{8,9},{9,8},{10,11... | collective-permute-start | bytes 55304 | tf_op jit(solution)/shard_map/ppermute | solution.py:58
  (1 other events, 0.7 us)

commit v4 on v1

--- a/solution.py
+++ b/solution.py
@@ -231,13 +231,17 @@
     return jnp.concatenate(values, axis=1)
 
 
-def domain_sums(pairs, factor, place, info, sums):
+def tiles_of(sums):
     count, examples, rows = sums.shape
     example = lax.broadcasted_iota(jnp.int32, (LANES, rows), 0)
     column = lax.broadcasted_iota(jnp.int32, (LANES, rows), 1)
     gather = (lax.shift_right_logical(column, TOK_BITS) == example).astype(jnp.bfloat16)
-    tiles = dot_parts(sums[...].reshape(count * examples, rows), gather)
-    tiles = tiles.reshape(count, examples, LANES)
+    tiles = dot_parts(sums.reshape(count * examples, rows), gather)
+    return tiles.reshape(count, examples, LANES)
+
+
+def domain_sums(pairs, factor, place, info, tiles):
+    examples = tiles[0].shape[0]
     mirrored, core, side = place
     lane = lax.broadcasted_iota(jnp.int32, (1, LANES), 1)
     row = lax.broadcasted_iota(jnp.int32, (DOMAINS, LANES), 0)
@@ -350,7 +354,7 @@
     for block in (XS, XC, YS, ZS):
         notes[block] = held[block, rows:, :LANES]
     info = {block: info_row(notes, block) for block in (XS, XC, YS, ZS)}
-    total = domain_sums(tuple(enumerate(FIRST)), factor, (mirrored, core, side), info, sums)
+    total = domain_sums(tuple(enumerate(FIRST)), factor, (mirrored, core, side), info, tiles_of(sums[...]))
     out[...] = jnp.zeros_like(out)
     for block, value in total.items():
         out[block] = value
@@ -386,7 +390,7 @@
     token_sums(inner.at[0], gram_v.at[2], sums.at[2])
     info = {block: info_row(notes_v, block) for block in (XS, XC, YS, ZS)}
     pairs = ((0, 0), (1, 1), (2, 2))
-    total = domain_sums(pairs, factor, (mirrored, core, side), info, sums)
+    total = domain_sums(pairs, factor, (mirrored, core, side), info, tiles_of(sums[...]))
     out[...] = earlier_v[...]
     for block, value in total.items():
         out[block] = earlier_v[block] + value
@@ -431,6 +435,7 @@
     wait(copies, "g5", XS)
     token_sums(inner.at[1], gram_v.at[1], sums.at[1])
     wait(copies, "g6", "g2", "notes", "earlier")
+    early = tiles_of(sums[0:2])
 
     @pl.when(mirrored == 1)
     def _():
@@ -449,8 +454,10 @@
             notes_v[block] = held[block, rows:, :LANES]
         notes_out[...] = notes_v[...]
     info = {block: info_row(notes_v, block) for block in range(6)}
+    late = tiles_of(sums[2:4])
+    tiles = early[0], early[1], late[0], late[1]
     pairs = ((0, 4), (1, 5), (2, 6), (2, 7), (3, 8))
-    total = domain_sums(pairs, factor, (mirrored, core, side), info, sums)
+    total = domain_sums(pairs, factor, (mirrored, core, side), info, tiles)
     examples = sums.shape[1]
     for block, value in total.items():
         value = value + earlier_v[block]

time: 139 us -> 139 us (level)
  transfers between devices with their start and end apart: 18 -> 18, of which waited for: 11 -> 11; matrix products, arithmetic and copies ran while one was open for 3% -> 3% of each run, Pallas kernels for 49% -> 50%
where the time goes in v4:
time: 139 us
  Pallas kernels  74.8 us (54%)
  waiting for transfers between devices  36.2 us (26%)
  starting transfers between devices  21.3 us (15%)
  local copies, waits for them, and re-layouts  3.3 us (2%)
  other arithmetic  3.26 us (2%)
    ppermute x18, waiting for transfers between devices, send(): return lax.ppermute(value, 'ex', pairs)  36.2 us
    pallas_call x4, Pallas kernels, call(): pl.pallas_call(kernel, in_specs=[hbm] * len(operands), out_specs=[vmem] *...  35 us
    ppermute x18, starting transfers between devices, send(): return lax.ppermute(value, 'ex', pairs)  21.3 us
    pallas_call x1, Pallas kernels, grams(): pl.pallas_call(grams_kernel, in_specs=[pl.BlockSpec(memory_space=pltpu.SM...  18.5 us
    pallas_call x2, Pallas kernels, cut(): pl.pallas_call(cut_kernel, grid_spec=pltpu.PrefetchScalarGridSpec(num_sca...  13.6 us
    pallas_call x1, Pallas kernels, cut_half(): pl.pallas_call(functools.partial(half_kernel, steps), grid_spec=pltpu.Pre...  7.85 us
  transfers between devices with their start and end apart: 18, of which 11 were waited for; matrix products, arithmetic and copies ran while one was open for 3% of the time, Pallas kernels for 50%

profile of v4, /device:TPU:0, one launch (start us, length us, event | category | flops | bytes accessed | tf_op | source)
XLA Modules:
  0.0 139.1 jit_solution(5073587178978043326)
XLA Ops:
  0.0 5.0 %collective-permute-start.4 = (bf16[768,1024]{1,0:T(8,128)(2,1)}, bf16[768,1024]{1,0:T(8,128)(2,1)}, u32[]{:S(2)}, u32[]{:S(2)}) collective-permute-start(bf16[768,1024]{1,0:T(8,128)(2,1)} %xs.1), channel_id=1, source_target_pairs={{0,12},{1,13},{2,6},{3,7},{4,0},{5,1},{6,10},{7,11},{8,4},{9,5},{1... | collective-permute-start | bytes 4718600 | tf_op jit(solution)/shard_map/ppermute | solution.py:57
  7.7 6.7 %cut.2 = (bf16[784,896]{1,0:T(8,128)(2,1)}, bf16[784,896]{1,0:T(8,128)(2,1)}, bf16[768,384]{1,0:T(8,128)(2,1)}, bf16[768,384]{1,0:T(8,128)(2,1)}) custom-call(s32[2]{0:T(128)} %pad_add_fusion.places, bf16[16,128]{1,0:T(8,128)(2,1)} %broadcast_in_dim.2.info.own_info, bf16[768,5120]{1,0:T(8,128)(2,1)} %refs_0_.3, bf16[768,5120]{1,0:T(8,128)(2,1)} %refs_0_.3), custom_call_target="tpu_custom_call" | custom-call | flops 1 | bytes 1 | tf_op jit(solution)/shard_map/cut/pallas_call | solution.py:97
  14.4 1.7 %collective-permute-start.6 = (bf16[784,896]{1,0:T(8,128)(2,1)}, bf16[784,896]{1,0:T(8,128)(2,1)}, u32[]{:S(2)}, u32[]{:S(2)}) collective-permute-start(bf16[784,896]{1,0:T(8,128)(2,1)} %get-tuple-element.50), channel_id=1, source_target_pairs={{0,12},{1,13},{2,6},{3,7},{4,0},{5,1},{6,10},{7,11},{8,4},{9,5},{1... | collective-permute-start | bytes 4214792 | tf_op jit(solution)/shard_map/ppermute | solution.py:57
  17.1 6.8 %cut.3 = (bf16[784,896]{1,0:T(8,128)(2,1)}, bf16[784,896]{1,0:T(8,128)(2,1)}, bf16[768,384]{1,0:T(8,128)(2,1)}, bf16[768,384]{1,0:T(8,128)(2,1)}) custom-call(s32[2]{0:T(128)} %pad_add_fusion.1.places, bf16[16,128]{1,0:T(8,128)(2,1)} %broadcast_in_dim.2.info.own_info, bf16[768,5120]{1,0:T(8,128)(2,1)} %refs_0_.3, bf16[768,5120]{1,0:T(8,128)(2,1)} %refs_0_.3), custom_call_target="tpu_custom_call" | custom-call | flops 1 | bytes 1 | tf_op jit(solution)/shard_map/cut/pallas_call | solution.py:97
  23.9 7.8 %half.1 = bf16[784,3584]{1,0:T(8,128)(2,1)} custom-call(s32[1]{0:T(128)} %bitcast.6.place, bf16[16,128]{1,0:T(8,128)(2,1)} %broadcast_in_dim.2.info.own_info, bf16[768,5120]{1,0:T(8,128)(2,1)} %refs_0_.3, bf16[768,1024]{1,0:T(8,128)(2,1)} %xs.1), custom_call_target="tpu_custom_call" | custom-call | flops 1 | bytes 1 | tf_op jit(solution)/shard_map/half/pallas_call | solution.py:132
  31.8 9.6 %conditional.2 = (bf16[784,3584]{1,0:T(8,128)(2,1)}) conditional(s32[]{:T(128)} %bitcast.5, () %tuple.26, bf16[784,3584]{1,0:T(8,128)(2,1)} %half.1), branch_computations={%region_0.1_spmd, %region_1.2_spmd} | conditional | bytes 22478896 | solution.py:513
  31.9 9.5 %collective-permute-done = bf16[784,3584]{1,0:T(8,128)(2,1)} collective-permute-done((bf16[784,3584]{1,0:T(8,128)(2,1)}, bf16[784,3584]{1,0:T(8,128)(2,1)}, u32[]{:S(2)}, u32[]{:S(2)}) %collective-permute-start) | collective-permute-done | bytes 5619744 | tf_op jit(solution)/shard_map/cond/branch_1_fun/ppermute | solution.py:57
  41.4 3.6 %collective-permute-start.8 = (bf16[784,896]{1,0:T(8,128)(2,1)}, bf16[784,896]{1,0:T(8,128)(2,1)}, u32[]{:S(2)}, u32[]{:S(2)}) collective-permute-start(bf16[784,896]{1,0:T(8,128)(2,1)} %get-tuple-element.62), channel_id=1, source_target_pairs={{0,13},{1,12},{2,7},{3,6},{4,1},{5,0},{6,11},{7,10},{8,5},{9,4},{1... | collective-permute-start | bytes 4214792 | tf_op jit(solution)/shard_map/ppermute | solution.py:57
  45.0 6.0 %conditional.3 = (bf16[768,1024]{1,0:T(8,128)(2,1)}, bf16[768,1024]{1,0:T(8,128)(2,1)}) conditional(s32[]{:T(128)} %bitcast.5, () %tuple.28, (bf16[768,1024]{1,0:T(8,128)(2,1)}, bf16[768,1024]{1,0:T(8,128)(2,1)}) %tuple.29), branch_computations={%region_2.3_spmd, %region_3.4_spmd} | conditional | bytes 12583008 | solution.py:513
  45.5 3.2 %collective-permute-done.1 = bf16[768,1024]{1,0:T(8,128)(2,1)} collective-permute-done((bf16[768,1024]{1,0:T(8,128)(2,1)}, bf16[768,1024]{1,0:T(8,128)(2,1)}, u32[]{:S(2)}, u32[]{:S(2)}) %collective-permute-start.1) | collective-permute-done | bytes 1572896 | tf_op jit(solution)/shard_map/cond/branch_1_fun/ppermute | solution.py:57
  48.7 2.2 %collective-permute-done.2 = bf16[768,1024]{1,0:T(8,128)(2,1)} collective-permute-done((bf16[768,1024]{1,0:T(8,128)(2,1)}, bf16[768,1024]{1,0:T(8,128)(2,1)}, u32[]{:S(2)}, u32[]{:S(2)}) %collective-permute-start.2) | collective-permute-done | bytes 1572896 | tf_op jit(solution)/shard_map/cond/branch_1_fun/ppermute | solution.py:57
  51.0 2.0 %collective-permute-start.9 = (bf16[768,384]{1,0:T(8,128)(2,1)}, bf16[768,384]{1,0:T(8,128)(2,1)S(1)}, u32[]{:S(2)}, u32[]{:S(2)}) collective-permute-start(bf16[768,384]{1,0:T(8,128)(2,1)} %get-tuple-element.65), channel_id=1, source_target_pairs={{0,2},{1,3},{2,0},{3,1},{4,6},{5,7},{6,4},{7,5},{8,10},{9,11},{10,... | collective-permute-start | bytes 1769480 | tf_op jit(solution)/shard_map/ppermute | solution.py:57
  53.6 18.5 %grams.1.gram.refs_6_ = f32[7,768,768]{2,1,0:T(8,128)} custom-call(s32[14]{0:T(128)} %stack.47.table, bf16[768,1024]{1,0:T(8,128)(2,1)} %xs.1, bf16[784,3584]{1,0:T(8,128)(2,1)} %get-tuple-element.79.xc.x_half.refs_1_, bf16[768,1024]{1,0:T(8,128)(2,1)} %collective-permute-done.3.ys, bf16[768,1024]{1,0:T(8,128)(2,1)} %get-tuple-element.55.yc, ...), custom_call_target="tpu_custom_call" | custom-call | flops 1 | bytes 1 | tf_op jit(solution)/shard_map/grams/pallas_call | solution.py:182
  72.8 14.7 %same_one.1 = (f32[6,48,128]{2,1,0:T(8,128)}, bf16[6,16,128]{2,1,0:T(8,128)(2,1)}) custom-call(bf16[16,128]{1,0:T(8,128)(2,1)} %broadcast_in_dim.2.info.own_info, bf16[768,5120]{1,0:T(8,128)(2,1)} %refs_0_.3, bf16[784,3584]{1,0:T(8,128)(2,1)} %get-tuple-element.79.xc.x_half.refs_1_, bf16[784,896]{1,0:T(8,128)(2,1)} %collective-permute-done.5.ys.refs_2_, ...), custom_call_target="tpu_custom_call" | custom-call | flops 1 | bytes 1 | tf_op jit(solution)/shard_map/same_one/pallas_call | solution.py:538
  87.5 1.8 %collective-permute-start.10 = (bf16[768,384]{1,0:T(8,128)(2,1)}, bf16[768,384]{1,0:T(8,128)(2,1)S(1)}, u32[]{:S(2)}, u32[]{:S(2)}) collective-permute-start(bf16[768,384]{1,0:T(8,128)(2,1)} %get-tuple-element.66), channel_id=1, source_target_pairs={{0,12},{1,13},{2,6},{3,7},{4,0},{5,1},{6,10},{7,11},{8,4},{9,5},{1... | collective-permute-start | bytes 1769480 | tf_op jit(solution)/shard_map/ppermute | solution.py:57
  89.3 11.1 %collective-permute-done.8.refs_5_ = bf16[784,896]{1,0:T(8,128)(2,1)} collective-permute-done((bf16[784,896]{1,0:T(8,128)(2,1)}, bf16[784,896]{1,0:T(8,128)(2,1)}, u32[]{:S(2)}, u32[]{:S(2)}) %collective-permute-start.8) | collective-permute-done | bytes 1404960 | tf_op jit(solution)/shard_map/ppermute | solution.py:57
  100.4 1.6 %collective-permute-start.11 = (bf16[768,384]{1,0:T(8,128)(2,1)}, bf16[768,384]{1,0:T(8,128)(2,1)S(1)}, u32[]{:S(2)}, u32[]{:S(2)}) collective-permute-start(bf16[768,384]{1,0:T(8,128)(2,1)} %get-tuple-element.67), channel_id=1, source_target_pairs={{0,3},{1,2},{2,1},{3,0},{4,7},{5,6},{6,5},{7,4},{8,11},{9,10},{10,... | collective-permute-start | bytes 1769480 | tf_op jit(solution)/shard_map/ppermute | solution.py:57
  104.1 8.9 %cross_one.1 = (f32[6,48,128]{2,1,0:T(8,128)S(1)}, bf16[6,16,128]{2,1,0:T(8,128)(2,1)S(1)}) custom-call(bf16[6,16,128]{2,1,0:T(8,128)(2,1)S(1)} %copy-done.1, f32[6,48,128]{2,1,0:T(8,128)S(1)} %copy-done, bf16[768,5120]{1,0:T(8,128)(2,1)} %refs_0_.3, bf16[784,3584]{1,0:T(8,128)(2,1)} %get-tuple-element.79.xc.x_half.refs_1_, ...), custom_call_target="tpu_custom_call" | custom-call | flops 1 | bytes 1 | tf_op jit(solution)/shard_map/cross_one/pallas_call | solution.py:538
  113.0 2.4 %collective-permute-done.9.ys.refs_2_ = bf16[768,384]{1,0:T(8,128)(2,1)S(1)} collective-permute-done((bf16[768,384]{1,0:T(8,128)(2,1)}, bf16[768,384]{1,0:T(8,128)(2,1)S(1)}, u32[]{:S(2)}, u32[]{:S(2)}) %collective-permute-start.9) | collective-permute-done | bytes 589856 | tf_op jit(solution)/shard_map/ppermute | solution.py:57
  115.5 5.5 %same_two.1.earlier = f32[6,48,128]{2,1,0:T(8,128)S(1)} custom-call(bf16[6,16,128]{2,1,0:T(8,128)(2,1)S(1)} %get-tuple-element.63.notes, f32[6,48,128]{2,1,0:T(8,128)S(1)} %get-tuple-element.64.earlier, bf16[768,5120]{1,0:T(8,128)(2,1)S(1)} %bitcast.16, bf16[784,3584]{1,0:T(8,128)(2,1)} %get-tuple-element.79.xc.x_half.refs_1_, ...), custom_call_target="tpu_custom_call" | custom-call | flops 1 | bytes 1 | tf_op jit(solution)/shard_map/same_two/pallas_call | solution.py:538
  120.9 3.6 %collective-permute-done.12.refs_5_ = bf16[768,384]{1,0:T(8,128)(2,1)S(1)} collective-permute-done((bf16[768,384]{1,0:T(8,128)(2,1)}, bf16[768,384]{1,0:T(8,128)(2,1)S(1)}, u32[]{:S(2)}, u32[]{:S(2)}) %collective-permute-start.12) | collective-permute-done | bytes 589856 | tf_op jit(solution)/shard_map/ppermute | solution.py:57
  125.1 5.9 %cross_two.1 = (f32[48,96]{1,0:T(8,128)S(1)}, f32[48,96]{1,0:T(8,128)S(1)}, f32[48,96]{1,0:T(8,128)S(1)}, f32[48,96]{1,0:T(8,128)S(1)}, f32[48,96]{1,0:T(8,128)S(1)}, /*index=5*/f32[48,96]{1,0:T(8,128)S(1)}) custom-call(bf16[6,16,128]{2,1,0:T(8,128)(2,1)S(1)} %get-tuple-element.63.notes, f32[6,48,128]{2,1,0:T(8,128)S(1)} %same_two.1.earlier, ...), custom_call_target="tpu_custom_call" | custom-call | flops 1 | bytes 1 | tf_op jit(solution)/shard_map/cross_two/pallas_call | solution.py:538
  131.3 2.3 %collective-permute-start.14 = (f32[48,96]{1,0:T(8,128)S(1)}, f32[48,96]{1,0:T(8,128)S(1)}, u32[]{:S(2)}, u32[]{:S(2)}) collective-permute-start(f32[48,96]{1,0:T(8,128)S(1)} %get-tuple-element.71), channel_id=1, source_target_pairs={{0,5},{1,4},{2,15},{3,14},{4,9},{5,8},{6,3},{7,2},{8,13},{9,12},{1... | collective-permute-start | bytes 55304 | tf_op jit(solution)/shard_map/ppermute | solution.py:57
  133.6 1.7 %collective-permute-start.15 = (f32[48,96]{1,0:T(8,128)S(1)}, f32[48,96]{1,0:T(8,128)S(1)}, u32[]{:S(2)}, u32[]{:S(2)}) collective-permute-start(f32[48,96]{1,0:T(8,128)S(1)} %get-tuple-element.72), channel_id=1, source_target_pairs={{0,2},{1,3},{2,0},{3,1},{4,6},{5,7},{6,4},{7,5},{8,10},{9,11},{10,... | collective-permute-start | bytes 55304 | tf_op jit(solution)/shard_map/ppermute | solution.py:57
  (44 shorter events, 12.2 us)
Async XLA Ops:
  0.0 45.0 %collective-permute-start.4 = (bf16[768,1024]{1,0:T(8,128)(2,1)}, bf16[768,1024]{1,0:T(8,128)(2,1)}, u32[]{:S(2)}, u32[]{:S(2)}) collective-permute-start(bf16[768,1024]{1,0:T(8,128)(2,1)} %xs.1), channel_id=1, source_target_pairs={{0,12},{1,13},{2,6},{3,7},{4,0},{5,1},{6,10},{7,11},{8,4},{9,5},{1... | collective-permute-start | bytes 4718600 | tf_op jit(solution)/shard_map/ppermute | solution.py:57
  5.0 39.9 %collective-permute-start.3 = (bf16[768,1024]{1,0:T(8,128)(2,1)}, bf16[768,1024]{1,0:T(8,128)(2,1)}, u32[]{:S(2)}, u32[]{:S(2)}) collective-permute-start(bf16[768,1024]{1,0:T(8,128)(2,1)} %xs.1), channel_id=1, source_target_pairs={{0,2},{1,3},{2,0},{3,1},{4,6},{5,7},{6,4},{7,5},{8,10},{9,11},{10,... | collective-permute-start | bytes 4718600 | tf_op jit(solution)/shard_map/ppermute | solution.py:57
  14.4 57.6 %collective-permute-start.6 = (bf16[784,896]{1,0:T(8,128)(2,1)}, bf16[784,896]{1,0:T(8,128)(2,1)}, u32[]{:S(2)}, u32[]{:S(2)}) collective-permute-start(bf16[784,896]{1,0:T(8,128)(2,1)} %get-tuple-element.50), channel_id=1, source_target_pairs={{0,12},{1,13},{2,6},{3,7},{4,0},{5,1},{6,10},{7,11},{8,4},{9,5},{1... | collective-permute-start | bytes 4214792 | tf_op jit(solution)/shard_map/ppermute | solution.py:57
  16.2 56.6 %collective-permute-start.5 = (bf16[784,896]{1,0:T(8,128)(2,1)}, bf16[784,896]{1,0:T(8,128)(2,1)}, u32[]{:S(2)}, u32[]{:S(2)}) collective-permute-start(bf16[784,896]{1,0:T(8,128)(2,1)} %get-tuple-element.45), channel_id=1, source_target_pairs={{0,2},{1,3},{2,0},{3,1},{4,6},{5,7},{6,4},{7,5},{8,10},{9,11},{10,... | collective-permute-start | bytes 4214792 | tf_op jit(solution)/shard_map/ppermute | solution.py:57
  23.9 7.9 %copy-start.2 = (s32[1,2]{1,0:T(1,128)S(1)}, s32[1,2]{1,0:T(1,128)}, u32[]{:S(2)}) copy-start(s32[1,2]{1,0:T(1,128)} %param.11) | copy-start | bytes 28
  31.8 9.6 %collective-permute-start = (bf16[784,3584]{1,0:T(8,128)(2,1)}, bf16[784,3584]{1,0:T(8,128)(2,1)}, u32[]{:S(2)}, u32[]{:S(2)}) collective-permute-start(bf16[784,3584]{1,0:T(8,128)(2,1)} %param.1), channel_id=1, source_target_pairs={{0,1},{1,0},{2,3},{3,2},{4,5},{5,4},{6,7},{7,6},{8,9},{9,8},{10,11... | collective-permute-start | bytes 16859144 | tf_op jit(solution)/shard_map/cond/branch_1_fun/ppermute | solution.py:57
  41.4 59.0 %collective-permute-start.8 = (bf16[784,896]{1,0:T(8,128)(2,1)}, bf16[784,896]{1,0:T(8,128)(2,1)}, u32[]{:S(2)}, u32[]{:S(2)}) collective-permute-start(bf16[784,896]{1,0:T(8,128)(2,1)} %get-tuple-element.62), channel_id=1, source_target_pairs={{0,13},{1,12},{2,7},{3,6},{4,1},{5,0},{6,11},{7,10},{8,5},{9,4},{1... | collective-permute-start | bytes 4214792 | tf_op jit(solution)/shard_map/ppermute | solution.py:57
  45.0 3.8 %collective-permute-start.1 = (bf16[768,1024]{1,0:T(8,128)(2,1)}, bf16[768,1024]{1,0:T(8,128)(2,1)}, u32[]{:S(2)}, u32[]{:S(2)}) collective-permute-start(bf16[768,1024]{1,0:T(8,128)(2,1)} %get-tuple-element.13), channel_id=1, source_target_pairs={{0,1},{1,0},{2,3},{3,2},{4,5},{5,4},{6,7},{7,6},{8,9},{9,8},{10,11... | collective-permute-start | bytes 4718600 | tf_op jit(solution)/shard_map/cond/branch_1_fun/ppermute | solution.py:57
  45.3 5.6 %collective-permute-start.2 = (bf16[768,1024]{1,0:T(8,128)(2,1)}, bf16[768,1024]{1,0:T(8,128)(2,1)}, u32[]{:S(2)}, u32[]{:S(2)}) collective-permute-start(bf16[768,1024]{1,0:T(8,128)(2,1)} %get-tuple-element.14), channel_id=1, source_target_pairs={{0,1},{1,0},{2,3},{3,2},{4,5},{5,4},{6,7},{7,6},{8,9},{9,8},{10,11... | collective-permute-start | bytes 4718600 | tf_op jit(solution)/shard_map/cond/branch_1_fun/ppermute | solution.py:57
  51.0 51.0 %collective-permute-start.7 = (bf16[784,896]{1,0:T(8,128)(2,1)}, bf16[784,896]{1,0:T(8,128)(2,1)}, u32[]{:S(2)}, u32[]{:S(2)}) collective-permute-start(bf16[784,896]{1,0:T(8,128)(2,1)} %get-tuple-element.47), channel_id=1, source_target_pairs={{0,3},{1,2},{2,1},{3,0},{4,7},{5,6},{6,5},{7,4},{8,11},{9,10},{10,... | collective-permute-start | bytes 4214792 | tf_op jit(solution)/shard_map/ppermute | solution.py:57
  51.0 64.5 %collective-permute-start.9 = (bf16[768,384]{1,0:T(8,128)(2,1)}, bf16[768,384]{1,0:T(8,128)(2,1)S(1)}, u32[]{:S(2)}, u32[]{:S(2)}) collective-permute-start(bf16[768,384]{1,0:T(8,128)(2,1)} %get-tuple-element.65), channel_id=1, source_target_pairs={{0,2},{1,3},{2,0},{3,1},{4,6},{5,7},{6,4},{7,5},{8,10},{9,11},{10,... | collective-permute-start | bytes 1769480 | tf_op jit(solution)/shard_map/ppermute | solution.py:57
  87.5 28.0 %collective-permute-start.10 = (bf16[768,384]{1,0:T(8,128)(2,1)}, bf16[768,384]{1,0:T(8,128)(2,1)S(1)}, u32[]{:S(2)}, u32[]{:S(2)}) collective-permute-start(bf16[768,384]{1,0:T(8,128)(2,1)} %get-tuple-element.66), channel_id=1, source_target_pairs={{0,12},{1,13},{2,6},{3,7},{4,0},{5,1},{6,10},{7,11},{8,4},{9,5},{1... | collective-permute-start | bytes 1769480 | tf_op jit(solution)/shard_map/ppermute | solution.py:57
  89.3 35.2 %collective-permute-start.12 = (bf16[768,384]{1,0:T(8,128)(2,1)}, bf16[768,384]{1,0:T(8,128)(2,1)S(1)}, u32[]{:S(2)}, u32[]{:S(2)}) collective-permute-start(bf16[768,384]{1,0:T(8,128)(2,1)} %get-tuple-element.68), channel_id=1, source_target_pairs={{0,13},{1,12},{2,7},{3,6},{4,1},{5,0},{6,11},{7,10},{8,5},{9,4},{1... | collective-permute-start | bytes 1769480 | tf_op jit(solution)/shard_map/ppermute | solution.py:57
  100.4 24.8 %collective-permute-start.11 = (bf16[768,384]{1,0:T(8,128)(2,1)}, bf16[768,384]{1,0:T(8,128)(2,1)S(1)}, u32[]{:S(2)}, u32[]{:S(2)}) collective-permute-start(bf16[768,384]{1,0:T(8,128)(2,1)} %get-tuple-element.67), channel_id=1, source_target_pairs={{0,3},{1,2},{2,1},{3,0},{4,7},{5,6},{6,5},{7,4},{8,11},{9,10},{10,... | collective-permute-start | bytes 1769480 | tf_op jit(solution)/shard_map/ppermute | solution.py:57
  102.0 13.4 %slice-start = ((s8[7864320]{0:T(1024)(128)(4,1)}), s8[4194304]{0:T(1024)(128)(4,1)S(1)}, s32[]{:S(2)}) async-start(s8[7864320]{0:T(1024)(128)(4,1)} %bitcast.15), calls=%async_computation | async-start | bytes 8388608
  102.0 1.1 copy-start
  103.1 1.0 copy-start.1
  104.1 11.4 %slice-start.1 = ((s8[7864320]{0:T(1024)(128)(4,1)}), s8[3670016]{0:T(1024)(128)(4,1)S(1)}, s32[]{:S(2)}) async-start(s8[7864320]{0:T(1024)(128)(4,1)} %bitcast.15), calls=%async_computation.1 | async-start | bytes 7340032
  131.0 5.7 %collective-permute-start.13 = (f32[48,96]{1,0:T(8,128)S(1)}, f32[48,96]{1,0:T(8,128)S(1)}, u32[]{:S(2)}, u32[]{:S(2)}) collective-permute-start(f32[48,96]{1,0:T(8,128)S(1)} %get-tuple-element.70), channel_id=1, source_target_pairs={{0,4},{1,5},{2,14},{3,15},{4,8},{5,9},{6,2},{7,3},{8,12},{9,13},{1... | collective-permute-start | bytes 55304 | tf_op jit(solution)/shard_map/ppermute | solution.py:57
  131.3 7.0 %collective-permute-start.14 = (f32[48,96]{1,0:T(8,128)S(1)}, f32[48,96]{1,0:T(8,128)S(1)}, u32[]{:S(2)}, u32[]{:S(2)}) collective-permute-start(f32[48,96]{1,0:T(8,128)S(1)} %get-tuple-element.71), channel_id=1, source_target_pairs={{0,5},{1,4},{2,15},{3,14},{4,9},{5,8},{6,3},{7,2},{8,13},{9,12},{1... | collective-permute-start | bytes 55304 | tf_op jit(solution)/shard_map/ppermute | solution.py:57
  133.6 4.7 %collective-permute-start.15 = (f32[48,96]{1,0:T(8,128)S(1)}, f32[48,96]{1,0:T(8,128)S(1)}, u32[]{:S(2)}, u32[]{:S(2)}) collective-permute-start(f32[48,96]{1,0:T(8,128)S(1)} %get-tuple-element.72), channel_id=1, source_target_pairs={{0,2},{1,3},{2,0},{3,1},{4,6},{5,7},{6,4},{7,5},{8,10},{9,11},{10,... | collective-permute-start | bytes 55304 | tf_op jit(solution)/shard_map/ppermute | solution.py:57
  135.3 3.3 %collective-permute-start.16 = (f32[48,96]{1,0:T(8,128)S(1)}, f32[48,96]{1,0:T(8,128)S(1)}, u32[]{:S(2)}, u32[]{:S(2)}) collective-permute-start(f32[48,96]{1,0:T(8,128)S(1)} %get-tuple-element.73), channel_id=1, source_target_pairs={{0,3},{1,2},{2,1},{3,0},{4,7},{5,6},{6,5},{7,4},{8,11},{9,10},{10,... | collective-permute-start | bytes 55304 | tf_op jit(solution)/shard_map/ppermute | solution.py:57
  135.3 3.2 %collective-permute-start.17 = (f32[48,96]{1,0:T(8,128)S(1)}, f32[48,96]{1,0:T(8,128)S(1)}, u32[]{:S(2)}, u32[]{:S(2)}) collective-permute-start(f32[48,96]{1,0:T(8,128)S(1)} %get-tuple-element.74), channel_id=1, source_target_pairs={{0,1},{1,0},{2,3},{3,2},{4,5},{5,4},{6,7},{7,6},{8,9},{9,8},{10,11... | collective-permute-start | bytes 55304 | tf_op jit(solution)/shard_map/ppermute | solution.py:57

commit v5 on v1

--- a/solution.py
+++ b/solution.py
@@ -573,8 +573,8 @@
 
     total = sums[XS]
     total = total + send(sums[ZS], against, 0)
+    total = total + send(sums[YS], across, 0)
     total = total + send(sums[ZC], against, 1)
-    total = total + send(sums[YS], across, 0)
     total = total + send(sums[YC], across, 1)
     total = total + send(sums[XC], stay, 1)
     return total.T

time: 139 us -> 140 us (level)
  starting transfers between devices: 21.3 us -> 23.9 us
  waiting for transfers between devices: 36.7 us -> 34.8 us
    ppermute x18, starting transfers between devices: 21.3 us -> 23.9 us  [send(): return lax.ppermute(value, 'ex', pairs)]
    ppermute x18, waiting for transfers between devices: 36.7 us -> 34.8 us  [send(): return lax.ppermute(value, 'ex', pairs)]
  transfers between devices with their start and end apart: 18 -> 18, of which waited for: 11 -> 9; matrix products, arithmetic and copies ran while one was open for 3% -> 3% of each run, Pallas kernels for 49% -> 49%
where the time goes in v5:
time: 140 us; the launch traced here: 139 us
  Pallas kernels  74 us (53%)
  waiting for transfers between devices  34.8 us (25%)
  starting transfers between devices  23.9 us (17%)
  local copies, waits for them, and re-layouts  3.3 us (2%)
  other arithmetic  3.26 us (2%)
    ppermute x18, waiting for transfers between devices, send(): return lax.ppermute(value, 'ex', pairs)  34.8 us
    pallas_call x4, Pallas kernels, call(): pl.pallas_call(kernel, in_specs=[hbm] * len(operands), out_specs=[vmem] *...  34.2 us
    ppermute x18, starting transfers between devices, send(): return lax.ppermute(value, 'ex', pairs)  23.9 us
    pallas_call x1, Pallas kernels, grams(): pl.pallas_call(grams_kernel, in_specs=[pl.BlockSpec(memory_space=pltpu.SM...  18.5 us
    pallas_call x2, Pallas kernels, cut(): pl.pallas_call(cut_kernel, grid_spec=pltpu.PrefetchScalarGridSpec(num_sca...  13.6 us
    pallas_call x1, Pallas kernels, cut_half(): pl.pallas_call(functools.partial(half_kernel, steps), grid_spec=pltpu.Pre...  7.85 us
  transfers between devices with their start and end apart: 18, of which 9 were waited for; matrix products, arithmetic and copies ran while one was open for 3% of the time, Pallas kernels for 49%

profile of v5, /device:TPU:0, one launch (start us, length us, event | category | flops | bytes accessed | tf_op | source)
XLA Modules:
  0.0 139.5 jit_solution(4873382767427444474)
XLA Ops:
  0.0 5.0 %collective-permute-start.4 = (bf16[768,1024]{1,0:T(8,128)(2,1)}, bf16[768,1024]{1,0:T(8,128)(2,1)}, u32[]{:S(2)}, u32[]{:S(2)}) collective-permute-start(bf16[768,1024]{1,0:T(8,128)(2,1)} %xs.1), channel_id=1, source_target_pairs={{0,12},{1,13},{2,6},{3,7},{4,0},{5,1},{6,10},{7,11},{8,4},{9,5},{1... | collective-permute-start | bytes 4718600 | tf_op jit(solution)/shard_map/ppermute | solution.py:57
  7.7 6.7 %cut.2 = (bf16[784,896]{1,0:T(8,128)(2,1)}, bf16[784,896]{1,0:T(8,128)(2,1)}, bf16[768,384]{1,0:T(8,128)(2,1)}, bf16[768,384]{1,0:T(8,128)(2,1)}) custom-call(s32[2]{0:T(128)} %pad_add_fusion.places, bf16[16,128]{1,0:T(8,128)(2,1)} %broadcast_in_dim.2.info.own_info, bf16[768,5120]{1,0:T(8,128)(2,1)} %refs_0_.3, bf16[768,5120]{1,0:T(8,128)(2,1)} %refs_0_.3), custom_call_target="tpu_custom_call" | custom-call | flops 1 | bytes 1 | tf_op jit(solution)/shard_map/cut/pallas_call | solution.py:97
  14.4 1.7 %collective-permute-start.6 = (bf16[784,896]{1,0:T(8,128)(2,1)}, bf16[784,896]{1,0:T(8,128)(2,1)}, u32[]{:S(2)}, u32[]{:S(2)}) collective-permute-start(bf16[784,896]{1,0:T(8,128)(2,1)} %get-tuple-element.50), channel_id=1, source_target_pairs={{0,12},{1,13},{2,6},{3,7},{4,0},{5,1},{6,10},{7,11},{8,4},{9,5},{1... | collective-permute-start | bytes 4214792 | tf_op jit(solution)/shard_map/ppermute | solution.py:57
  17.1 6.8 %cut.3 = (bf16[784,896]{1,0:T(8,128)(2,1)}, bf16[784,896]{1,0:T(8,128)(2,1)}, bf16[768,384]{1,0:T(8,128)(2,1)}, bf16[768,384]{1,0:T(8,128)(2,1)}) custom-call(s32[2]{0:T(128)} %pad_add_fusion.1.places, bf16[16,128]{1,0:T(8,128)(2,1)} %broadcast_in_dim.2.info.own_info, bf16[768,5120]{1,0:T(8,128)(2,1)} %refs_0_.3, bf16[768,5120]{1,0:T(8,128)(2,1)} %refs_0_.3), custom_call_target="tpu_custom_call" | custom-call | flops 1 | bytes 1 | tf_op jit(solution)/shard_map/cut/pallas_call | solution.py:97
  23.9 7.8 %half.1 = bf16[784,3584]{1,0:T(8,128)(2,1)} custom-call(s32[1]{0:T(128)} %bitcast.6.place, bf16[16,128]{1,0:T(8,128)(2,1)} %broadcast_in_dim.2.info.own_info, bf16[768,5120]{1,0:T(8,128)(2,1)} %refs_0_.3, bf16[768,1024]{1,0:T(8,128)(2,1)} %xs.1), custom_call_target="tpu_custom_call" | custom-call | flops 1 | bytes 1 | tf_op jit(solution)/shard_map/half/pallas_call | solution.py:132
  31.8 9.6 %conditional.2 = (bf16[784,3584]{1,0:T(8,128)(2,1)}) conditional(s32[]{:T(128)} %bitcast.5, () %tuple.26, bf16[784,3584]{1,0:T(8,128)(2,1)} %half.1), branch_computations={%region_0.1_spmd, %region_1.2_spmd} | conditional | bytes 22478896 | solution.py:506
  31.9 9.5 %collective-permute-done = bf16[784,3584]{1,0:T(8,128)(2,1)} collective-permute-done((bf16[784,3584]{1,0:T(8,128)(2,1)}, bf16[784,3584]{1,0:T(8,128)(2,1)}, u32[]{:S(2)}, u32[]{:S(2)}) %collective-permute-start) | collective-permute-done | bytes 5619744 | tf_op jit(solution)/shard_map/cond/branch_1_fun/ppermute | solution.py:57
  41.4 3.6 %collective-permute-start.8 = (bf16[784,896]{1,0:T(8,128)(2,1)}, bf16[784,896]{1,0:T(8,128)(2,1)}, u32[]{:S(2)}, u32[]{:S(2)}) collective-permute-start(bf16[784,896]{1,0:T(8,128)(2,1)} %get-tuple-element.62), channel_id=1, source_target_pairs={{0,13},{1,12},{2,7},{3,6},{4,1},{5,0},{6,11},{7,10},{8,5},{9,4},{1... | collective-permute-start | bytes 4214792 | tf_op jit(solution)/shard_map/ppermute | solution.py:57
  45.0 6.0 %conditional.3 = (bf16[768,1024]{1,0:T(8,128)(2,1)}, bf16[768,1024]{1,0:T(8,128)(2,1)}) conditional(s32[]{:T(128)} %bitcast.5, () %tuple.28, (bf16[768,1024]{1,0:T(8,128)(2,1)}, bf16[768,1024]{1,0:T(8,128)(2,1)}) %tuple.29), branch_computations={%region_2.3_spmd, %region_3.4_spmd} | conditional | bytes 12583008 | solution.py:506
  45.5 3.2 %collective-permute-done.1 = bf16[768,1024]{1,0:T(8,128)(2,1)} collective-permute-done((bf16[768,1024]{1,0:T(8,128)(2,1)}, bf16[768,1024]{1,0:T(8,128)(2,1)}, u32[]{:S(2)}, u32[]{:S(2)}) %collective-permute-start.1) | collective-permute-done | bytes 1572896 | tf_op jit(solution)/shard_map/cond/branch_1_fun/ppermute | solution.py:57
  48.7 2.2 %collective-permute-done.2 = bf16[768,1024]{1,0:T(8,128)(2,1)} collective-permute-done((bf16[768,1024]{1,0:T(8,128)(2,1)}, bf16[768,1024]{1,0:T(8,128)(2,1)}, u32[]{:S(2)}, u32[]{:S(2)}) %collective-permute-start.2) | collective-permute-done | bytes 1572896 | tf_op jit(solution)/shard_map/cond/branch_1_fun/ppermute | solution.py:57
  51.0 2.0 %collective-permute-start.9 = (bf16[768,384]{1,0:T(8,128)(2,1)}, bf16[768,384]{1,0:T(8,128)(2,1)S(1)}, u32[]{:S(2)}, u32[]{:S(2)}) collective-permute-start(bf16[768,384]{1,0:T(8,128)(2,1)} %get-tuple-element.65), channel_id=1, source_target_pairs={{0,2},{1,3},{2,0},{3,1},{4,6},{5,7},{6,4},{7,5},{8,10},{9,11},{10,... | collective-permute-start | bytes 1769480 | tf_op jit(solution)/shard_map/ppermute | solution.py:57
  53.6 18.5 %grams.1.gram.refs_6_ = f32[7,768,768]{2,1,0:T(8,128)} custom-call(s32[14]{0:T(128)} %stack.47.table, bf16[768,1024]{1,0:T(8,128)(2,1)} %xs.1, bf16[784,3584]{1,0:T(8,128)(2,1)} %get-tuple-element.79.xc.x_half.refs_1_, bf16[768,1024]{1,0:T(8,128)(2,1)} %collective-permute-done.3.ys, bf16[768,1024]{1,0:T(8,128)(2,1)} %get-tuple-element.55.yc, ...), custom_call_target="tpu_custom_call" | custom-call | flops 1 | bytes 1 | tf_op jit(solution)/shard_map/grams/pallas_call | solution.py:182
  72.8 14.7 %same_one.1 = (f32[6,48,128]{2,1,0:T(8,128)}, bf16[6,16,128]{2,1,0:T(8,128)(2,1)}) custom-call(bf16[16,128]{1,0:T(8,128)(2,1)} %broadcast_in_dim.2.info.own_info, bf16[768,5120]{1,0:T(8,128)(2,1)} %refs_0_.3, bf16[784,3584]{1,0:T(8,128)(2,1)} %get-tuple-element.79.xc.x_half.refs_1_, bf16[784,896]{1,0:T(8,128)(2,1)} %collective-permute-done.5.ys.refs_2_, ...), custom_call_target="tpu_custom_call" | custom-call | flops 1 | bytes 1 | tf_op jit(solution)/shard_map/same_one/pallas_call | solution.py:531
  87.5 1.8 %collective-permute-start.10 = (bf16[768,384]{1,0:T(8,128)(2,1)}, bf16[768,384]{1,0:T(8,128)(2,1)S(1)}, u32[]{:S(2)}, u32[]{:S(2)}) collective-permute-start(bf16[768,384]{1,0:T(8,128)(2,1)} %get-tuple-element.66), channel_id=1, source_target_pairs={{0,12},{1,13},{2,6},{3,7},{4,0},{5,1},{6,10},{7,11},{8,4},{9,5},{1... | collective-permute-start | bytes 1769480 | tf_op jit(solution)/shard_map/ppermute | solution.py:57
  89.3 11.1 %collective-permute-done.8.refs_5_ = bf16[784,896]{1,0:T(8,128)(2,1)} collective-permute-done((bf16[784,896]{1,0:T(8,128)(2,1)}, bf16[784,896]{1,0:T(8,128)(2,1)}, u32[]{:S(2)}, u32[]{:S(2)}) %collective-permute-start.8) | collective-permute-done | bytes 1404960 | tf_op jit(solution)/shard_map/ppermute | solution.py:57
  104.1 8.5 %cross_one.1 = (f32[6,48,128]{2,1,0:T(8,128)S(1)}, bf16[6,16,128]{2,1,0:T(8,128)(2,1)S(1)}) custom-call(bf16[6,16,128]{2,1,0:T(8,128)(2,1)S(1)} %copy-done.1, f32[6,48,128]{2,1,0:T(8,128)S(1)} %copy-done, bf16[768,5120]{1,0:T(8,128)(2,1)} %refs_0_.3, bf16[784,3584]{1,0:T(8,128)(2,1)} %get-tuple-element.79.xc.x_half.refs_1_, ...), custom_call_target="tpu_custom_call" | custom-call | flops 1 | bytes 1 | tf_op jit(solution)/shard_map/cross_one/pallas_call | solution.py:531
  112.6 2.9 %collective-permute-done.9.ys.refs_2_ = bf16[768,384]{1,0:T(8,128)(2,1)S(1)} collective-permute-done((bf16[768,384]{1,0:T(8,128)(2,1)}, bf16[768,384]{1,0:T(8,128)(2,1)S(1)}, u32[]{:S(2)}, u32[]{:S(2)}) %collective-permute-start.9) | collective-permute-done | bytes 589856 | tf_op jit(solution)/shard_map/ppermute | solution.py:57
  115.5 5.5 %same_two.1.earlier = f32[6,48,128]{2,1,0:T(8,128)S(1)} custom-call(bf16[6,16,128]{2,1,0:T(8,128)(2,1)S(1)} %get-tuple-element.63.notes, f32[6,48,128]{2,1,0:T(8,128)S(1)} %get-tuple-element.64.earlier, bf16[768,5120]{1,0:T(8,128)(2,1)S(1)} %bitcast.16, bf16[784,3584]{1,0:T(8,128)(2,1)} %get-tuple-element.79.xc.x_half.refs_1_, ...), custom_call_target="tpu_custom_call" | custom-call | flops 1 | bytes 1 | tf_op jit(solution)/shard_map/same_two/pallas_call | solution.py:531
  120.9 3.6 %collective-permute-done.12.refs_5_ = bf16[768,384]{1,0:T(8,128)(2,1)S(1)} collective-permute-done((bf16[768,384]{1,0:T(8,128)(2,1)}, bf16[768,384]{1,0:T(8,128)(2,1)S(1)}, u32[]{:S(2)}, u32[]{:S(2)}) %collective-permute-start.12) | collective-permute-done | bytes 589856 | tf_op jit(solution)/shard_map/ppermute | solution.py:57
  125.1 5.6 %cross_two.1 = (f32[48,96]{1,0:T(8,128)S(1)}, f32[48,96]{1,0:T(8,128)S(1)}, f32[48,96]{1,0:T(8,128)S(1)}, f32[48,96]{1,0:T(8,128)S(1)}, f32[48,96]{1,0:T(8,128)S(1)}, /*index=5*/f32[48,96]{1,0:T(8,128)S(1)}) custom-call(bf16[6,16,128]{2,1,0:T(8,128)(2,1)S(1)} %get-tuple-element.63.notes, f32[6,48,128]{2,1,0:T(8,128)S(1)} %same_two.1.earlier, ...), custom_call_target="tpu_custom_call" | custom-call | flops 1 | bytes 1 | tf_op jit(solution)/shard_map/cross_two/pallas_call | solution.py:531
  130.9 2.9 %collective-permute-start.14 = (f32[48,96]{1,0:T(8,128)S(1)}, f32[48,96]{1,0:T(8,128)S(1)}, u32[]{:S(2)}, u32[]{:S(2)}) collective-permute-start(f32[48,96]{1,0:T(8,128)S(1)} %get-tuple-element.71), channel_id=1, source_target_pairs={{0,2},{1,3},{2,0},{3,1},{4,6},{5,7},{6,4},{7,5},{8,10},{9,11},{10,... | collective-permute-start | bytes 55304 | tf_op jit(solution)/shard_map/ppermute | solution.py:57
  133.8 2.5 %collective-permute-start.16 = (f32[48,96]{1,0:T(8,128)S(1)}, f32[48,96]{1,0:T(8,128)S(1)}, u32[]{:S(2)}, u32[]{:S(2)}) collective-permute-start(f32[48,96]{1,0:T(8,128)S(1)} %get-tuple-element.73), channel_id=1, source_target_pairs={{0,3},{1,2},{2,1},{3,0},{4,7},{5,6},{6,5},{7,4},{8,11},{9,10},{10,... | collective-permute-start | bytes 55304 | tf_op jit(solution)/shard_map/ppermute | solution.py:57
  136.3 1.7 %collective-permute-start.17 = (f32[48,96]{1,0:T(8,128)S(1)}, f32[48,96]{1,0:T(8,128)S(1)}, u32[]{:S(2)}, u32[]{:S(2)}) collective-permute-start(f32[48,96]{1,0:T(8,128)S(1)} %get-tuple-element.74), channel_id=1, source_target_pairs={{0,1},{1,0},{2,3},{3,2},{4,5},{5,4},{6,7},{7,6},{8,9},{9,8},{10,11... | collective-permute-start | bytes 55304 | tf_op jit(solution)/shard_map/ppermute | solution.py:57
  (44 shorter events, 11.5 us)
Async XLA Ops:
  0.0 45.0 %collective-permute-start.4 = (bf16[768,1024]{1,0:T(8,128)(2,1)}, bf16[768,1024]{1,0:T(8,128)(2,1)}, u32[]{:S(2)}, u32[]{:S(2)}) collective-permute-start(bf16[768,1024]{1,0:T(8,128)(2,1)} %xs.1), channel_id=1, source_target_pairs={{0,12},{1,13},{2,6},{3,7},{4,0},{5,1},{6,10},{7,11},{8,4},{9,5},{1... | collective-permute-start | bytes 4718600 | tf_op jit(solution)/shard_map/ppermute | solution.py:57
  5.0 39.9 %collective-permute-start.3 = (bf16[768,1024]{1,0:T(8,128)(2,1)}, bf16[768,1024]{1,0:T(8,128)(2,1)}, u32[]{:S(2)}, u32[]{:S(2)}) collective-permute-start(bf16[768,1024]{1,0:T(8,128)(2,1)} %xs.1), channel_id=1, source_target_pairs={{0,2},{1,3},{2,0},{3,1},{4,6},{5,7},{6,4},{7,5},{8,10},{9,11},{10,... | collective-permute-start | bytes 4718600 | tf_op jit(solution)/shard_map/ppermute | solution.py:57
  14.4 57.6 %collective-permute-start.6 = (bf16[784,896]{1,0:T(8,128)(2,1)}, bf16[784,896]{1,0:T(8,128)(2,1)}, u32[]{:S(2)}, u32[]{:S(2)}) collective-permute-start(bf16[784,896]{1,0:T(8,128)(2,1)} %get-tuple-element.50), channel_id=1, source_target_pairs={{0,12},{1,13},{2,6},{3,7},{4,0},{5,1},{6,10},{7,11},{8,4},{9,5},{1... | collective-permute-start | bytes 4214792 | tf_op jit(solution)/shard_map/ppermute | solution.py:57
  16.2 56.6 %collective-permute-start.5 = (bf16[784,896]{1,0:T(8,128)(2,1)}, bf16[784,896]{1,0:T(8,128)(2,1)}, u32[]{:S(2)}, u32[]{:S(2)}) collective-permute-start(bf16[784,896]{1,0:T(8,128)(2,1)} %get-tuple-element.45), channel_id=1, source_target_pairs={{0,2},{1,3},{2,0},{3,1},{4,6},{5,7},{6,4},{7,5},{8,10},{9,11},{10,... | collective-permute-start | bytes 4214792 | tf_op jit(solution)/shard_map/ppermute | solution.py:57
  23.9 7.9 %copy-start.2 = (s32[1,2]{1,0:T(1,128)S(1)}, s32[1,2]{1,0:T(1,128)}, u32[]{:S(2)}) copy-start(s32[1,2]{1,0:T(1,128)} %param.11) | copy-start | bytes 28
  31.8 9.6 %collective-permute-start = (bf16[784,3584]{1,0:T(8,128)(2,1)}, bf16[784,3584]{1,0:T(8,128)(2,1)}, u32[]{:S(2)}, u32[]{:S(2)}) collective-permute-start(bf16[784,3584]{1,0:T(8,128)(2,1)} %param.1), channel_id=1, source_target_pairs={{0,1},{1,0},{2,3},{3,2},{4,5},{5,4},{6,7},{7,6},{8,9},{9,8},{10,11... | collective-permute-start | bytes 16859144 | tf_op jit(solution)/shard_map/cond/branch_1_fun/ppermute | solution.py:57
  41.4 59.0 %collective-permute-start.8 = (bf16[784,896]{1,0:T(8,128)(2,1)}, bf16[784,896]{1,0:T(8,128)(2,1)}, u32[]{:S(2)}, u32[]{:S(2)}) collective-permute-start(bf16[784,896]{1,0:T(8,128)(2,1)} %get-tuple-element.62), channel_id=1, source_target_pairs={{0,13},{1,12},{2,7},{3,6},{4,1},{5,0},{6,11},{7,10},{8,5},{9,4},{1... | collective-permute-start | bytes 4214792 | tf_op jit(solution)/shard_map/ppermute | solution.py:57
  45.0 3.8 %collective-permute-start.1 = (bf16[768,1024]{1,0:T(8,128)(2,1)}, bf16[768,1024]{1,0:T(8,128)(2,1)}, u32[]{:S(2)}, u32[]{:S(2)}) collective-permute-start(bf16[768,1024]{1,0:T(8,128)(2,1)} %get-tuple-element.13), channel_id=1, source_target_pairs={{0,1},{1,0},{2,3},{3,2},{4,5},{5,4},{6,7},{7,6},{8,9},{9,8},{10,11... | collective-permute-start | bytes 4718600 | tf_op jit(solution)/shard_map/cond/branch_1_fun/ppermute | solution.py:57
  45.3 5.6 %collective-permute-start.2 = (bf16[768,1024]{1,0:T(8,128)(2,1)}, bf16[768,1024]{1,0:T(8,128)(2,1)}, u32[]{:S(2)}, u32[]{:S(2)}) collective-permute-start(bf16[768,1024]{1,0:T(8,128)(2,1)} %get-tuple-element.14), channel_id=1, source_target_pairs={{0,1},{1,0},{2,3},{3,2},{4,5},{5,4},{6,7},{7,6},{8,9},{9,8},{10,11... | collective-permute-start | bytes 4718600 | tf_op jit(solution)/shard_map/cond/branch_1_fun/ppermute | solution.py:57
  51.0 51.0 %collective-permute-start.7 = (bf16[784,896]{1,0:T(8,128)(2,1)}, bf16[784,896]{1,0:T(8,128)(2,1)}, u32[]{:S(2)}, u32[]{:S(2)}) collective-permute-start(bf16[784,896]{1,0:T(8,128)(2,1)} %get-tuple-element.47), channel_id=1, source_target_pairs={{0,3},{1,2},{2,1},{3,0},{4,7},{5,6},{6,5},{7,4},{8,11},{9,10},{10,... | collective-permute-start | bytes 4214792 | tf_op jit(solution)/shard_map/ppermute | solution.py:57
  51.0 64.5 %collective-permute-start.9 = (bf16[768,384]{1,0:T(8,128)(2,1)}, bf16[768,384]{1,0:T(8,128)(2,1)S(1)}, u32[]{:S(2)}, u32[]{:S(2)}) collective-permute-start(bf16[768,384]{1,0:T(8,128)(2,1)} %get-tuple-element.65), channel_id=1, source_target_pairs={{0,2},{1,3},{2,0},{3,1},{4,6},{5,7},{6,4},{7,5},{8,10},{9,11},{10,... | collective-permute-start | bytes 1769480 | tf_op jit(solution)/shard_map/ppermute | solution.py:57
  87.5 28.0 %collective-permute-start.10 = (bf16[768,384]{1,0:T(8,128)(2,1)}, bf16[768,384]{1,0:T(8,128)(2,1)S(1)}, u32[]{:S(2)}, u32[]{:S(2)}) collective-permute-start(bf16[768,384]{1,0:T(8,128)(2,1)} %get-tuple-element.66), channel_id=1, source_target_pairs={{0,12},{1,13},{2,6},{3,7},{4,0},{5,1},{6,10},{7,11},{8,4},{9,5},{1... | collective-permute-start | bytes 1769480 | tf_op jit(solution)/shard_map/ppermute | solution.py:57
  89.3 35.2 %collective-permute-start.12 = (bf16[768,384]{1,0:T(8,128)(2,1)}, bf16[768,384]{1,0:T(8,128)(2,1)S(1)}, u32[]{:S(2)}, u32[]{:S(2)}) collective-permute-start(bf16[768,384]{1,0:T(8,128)(2,1)} %get-tuple-element.68), channel_id=1, source_target_pairs={{0,13},{1,12},{2,7},{3,6},{4,1},{5,0},{6,11},{7,10},{8,5},{9,4},{1... | collective-permute-start | bytes 1769480 | tf_op jit(solution)/shard_map/ppermute | solution.py:57
  100.4 24.8 %collective-permute-start.11 = (bf16[768,384]{1,0:T(8,128)(2,1)}, bf16[768,384]{1,0:T(8,128)(2,1)S(1)}, u32[]{:S(2)}, u32[]{:S(2)}) collective-permute-start(bf16[768,384]{1,0:T(8,128)(2,1)} %get-tuple-element.67), channel_id=1, source_target_pairs={{0,3},{1,2},{2,1},{3,0},{4,7},{5,6},{6,5},{7,4},{8,11},{9,10},{10,... | collective-permute-start | bytes 1769480 | tf_op jit(solution)/shard_map/ppermute | solution.py:57
  102.0 13.4 %slice-start = ((s8[7864320]{0:T(1024)(128)(4,1)}), s8[4194304]{0:T(1024)(128)(4,1)S(1)}, s32[]{:S(2)}) async-start(s8[7864320]{0:T(1024)(128)(4,1)} %bitcast.15), calls=%async_computation | async-start | bytes 8388608
  102.0 1.1 copy-start
  103.1 1.0 copy-start.1
  104.1 11.4 %slice-start.1 = ((s8[7864320]{0:T(1024)(128)(4,1)}), s8[3670016]{0:T(1024)(128)(4,1)S(1)}, s32[]{:S(2)}) async-start(s8[7864320]{0:T(1024)(128)(4,1)} %bitcast.15), calls=%async_computation.1 | async-start | bytes 7340032
  130.7 7.3 %collective-permute-start.13 = (f32[48,96]{1,0:T(8,128)S(1)}, f32[48,96]{1,0:T(8,128)S(1)}, u32[]{:S(2)}, u32[]{:S(2)}) collective-permute-start(f32[48,96]{1,0:T(8,128)S(1)} %get-tuple-element.70), channel_id=1, source_target_pairs={{0,4},{1,5},{2,14},{3,15},{4,8},{5,9},{6,2},{7,3},{8,12},{9,13},{1... | collective-permute-start | bytes 55304 | tf_op jit(solution)/shard_map/ppermute | solution.py:57
  130.9 7.1 %collective-permute-start.14 = (f32[48,96]{1,0:T(8,128)S(1)}, f32[48,96]{1,0:T(8,128)S(1)}, u32[]{:S(2)}, u32[]{:S(2)}) collective-permute-start(f32[48,96]{1,0:T(8,128)S(1)} %get-tuple-element.71), channel_id=1, source_target_pairs={{0,2},{1,3},{2,0},{3,1},{4,6},{5,7},{6,4},{7,5},{8,10},{9,11},{10,... | collective-permute-start | bytes 55304 | tf_op jit(solution)/shard_map/ppermute | solution.py:57
  133.8 5.0 %collective-permute-start.15 = (f32[48,96]{1,0:T(8,128)S(1)}, f32[48,96]{1,0:T(8,128)S(1)}, u32[]{:S(2)}, u32[]{:S(2)}) collective-permute-start(f32[48,96]{1,0:T(8,128)S(1)} %get-tuple-element.72), channel_id=1, source_target_pairs={{0,5},{1,4},{2,15},{3,14},{4,9},{5,8},{6,3},{7,2},{8,13},{9,12},{1... | collective-permute-start | bytes 55304 | tf_op jit(solution)/shard_map/ppermute | solution.py:57
  133.8 5.0 %collective-permute-start.16 = (f32[48,96]{1,0:T(8,128)S(1)}, f32[48,96]{1,0:T(8,128)S(1)}, u32[]{:S(2)}, u32[]{:S(2)}) collective-permute-start(f32[48,96]{1,0:T(8,128)S(1)} %get-tuple-element.73), channel_id=1, source_target_pairs={{0,3},{1,2},{2,1},{3,0},{4,7},{5,6},{6,5},{7,4},{8,11},{9,10},{10,... | collective-permute-start | bytes 55304 | tf_op jit(solution)/shard_map/ppermute | solution.py:57
  136.3 2.5 %collective-permute-start.17 = (f32[48,96]{1,0:T(8,128)S(1)}, f32[48,96]{1,0:T(8,128)S(1)}, u32[]{:S(2)}, u32[]{:S(2)}) collective-permute-start(f32[48,96]{1,0:T(8,128)S(1)} %get-tuple-element.74), channel_id=1, source_target_pairs={{0,1},{1,0},{2,3},{3,2},{4,5},{5,4},{6,7},{7,6},{8,9},{9,8},{10,11... | collective-permute-start | bytes 55304 | tf_op jit(solution)/shard_map/ppermute | solution.py:57
